TPU v7x, 512 devices: a whole 4x8x8 slice. The times are simulated.
512 devices in a mesh: radial: 64 (over z_hi, x, y), axial: 8 (over z_lo, core).
Axes of the slice: x: 4, y: 8, z: 8 (z_hi: 2, z_lo: 4; z = z_hi * 4 + z_lo), core: 2. Of those that a mesh axis runs over, the one named last changes fastest.
Arguments:
- velocity: float32 [3, 32, 512, 512], P(None, 'axial', 'radial'), may hold values from -6 to 6
- previous_rhs: float32 [3, 32, 512, 512], P(None, 'axial', 'radial'), may hold values from -6 to 6
- radial_deriv: float32 [512, 512], replicated, may hold values from -0.25 to 0.25
- inv_radius: float32 [512], P('radial'), may hold values from 0.5 to 2
Outputs:
- velocity_new: float32 [3, 32, 512, 512], P(None, 'axial', 'radial')
- rhs_new: float32 [3, 32, 512, 512], P(None, 'axial', 'radial')
All inputs are finite; a program needn't handle non-finite values.
Results may differ from a plain program's by a relative error of at most 0.00005.
Values sent between devices are 32-bit elements; how exact they have to be, the bound alone decides.
No kernel may reach another device: no remote copies, remote signals or barrier semaphores. Data moves between devices by JAX's collectives and lax.ppermute only.
A program may use at most 64 MiB of HBM per device.

v0:
```python
import math

import jax
import jax.numpy as jnp
from jax import lax
from jax.sharding import PartitionSpec as P

KEEP = 192


first_coefs = (4.0 / 5.0, -1.0 / 5.0, 4.0 / 105.0, -1.0 / 280.0)
second_coefs = (8.0 / 5.0, -1.0 / 5.0, 8.0 / 315.0, -1.0 / 560.0)
second_centre = -205.0 / 72.0
viscosity = 0.05
section_carry = -5.0 / 9.0
section_weight = 15.0 / 16.0
timestep = 0.1


def extended(shard, sides, width):
    for axis, dim in sides:
        size, length = (lax.axis_size(axis), shard.shape[dim])
        up = [(i, (i + 1) % size) for i in range(size)]
        down = [(j, i) for i, j in up]
        last = lax.slice_in_dim(shard, length - width, length, axis=dim)
        first = lax.slice_in_dim(shard, 0, width, axis=dim)
        before = lax.ppermute(last, axis, up)
        after = lax.ppermute(first, axis, down)
        shard = jnp.concatenate([before, shard, after], axis=dim)
    return shard


def tables(kept_modes, points):
    wavenumbers = jnp.arange(kept_modes, dtype=jnp.int32)
    columns = jnp.arange(points, dtype=jnp.int32)
    phases = wavenumbers[:, None] * columns[None, :] % points
    angles = phases.astype(jnp.float32) * (2.0 * math.pi / points)
    cosine_table = jnp.cos(angles)
    sine_table = jnp.sin(angles)
    forward = jnp.concatenate([cosine_table, -sine_table], axis=0).T
    weights = jnp.where(wavenumbers == 0, 1.0, 2.0).astype(jnp.float32)[:, None] / points
    backward = jnp.concatenate([weights * cosine_table, -weights * sine_table], axis=0)
    wavenumber = wavenumbers.astype(jnp.float32) * (2.0 * math.pi / points)
    return (forward, backward, wavenumber)


def rows_first(field):
    components, planes, radial_rows, width = field.shape
    return jnp.transpose(field, (2, 0, 1, 3)).reshape(radial_rows, components * planes * width)


def rows_back(flat, shape):
    components, planes, radial_rows, width = shape
    return jnp.transpose(flat.reshape(radial_rows, components, planes, width), (1, 2, 0, 3))


def radial_apply(matrix, flat):
    return jnp.dot(matrix, flat, precision=lax.Precision.HIGHEST)


def shards(velocity, previous_rhs, radial_deriv, inv_radius):
    components, planes, radial_rows, points = velocity.shape
    forward, backward, wavenumber = tables(KEEP, points)
    spectra = jnp.dot(velocity.reshape(-1, points), forward, precision=lax.Precision.HIGHEST)
    spectra = spectra.reshape(components, planes, radial_rows, 2 * KEEP)
    padded = extended(spectra, (("axial", 1),), 4)
    axial_first = sum(
        (
            first_coefs[offset]
            * (
                padded[:, 5 + offset : 5 + offset + planes]
                - padded[:, 3 - offset : 3 - offset + planes]
            )
            for offset in range(4)
        )
    )
    second = second_centre * spectra + sum(
        (
            second_coefs[offset]
            * (
                padded[:, 5 + offset : 5 + offset + planes]
                + padded[:, 3 - offset : 3 - offset + planes]
            )
            for offset in range(4)
        )
    )
    radius_ratio = inv_radius[None, None, :, None]
    real_part = spectra[..., :KEEP]
    imag_part = spectra[..., KEEP:]
    theta_spec = jnp.concatenate([-wavenumber * imag_part, wavenumber * real_part], axis=-1)
    wave_square = jnp.concatenate([wavenumber * wavenumber, wavenumber * wavenumber])
    spectral_laplace = second - wave_square * spectra * (radius_ratio * radius_ratio)
    stacked = jnp.stack([spectra, theta_spec, axial_first, spectral_laplace])
    flat = jnp.dot(stacked.reshape(-1, 2 * KEEP), backward, precision=lax.Precision.HIGHEST)
    fields = flat.reshape(stacked.shape[:-1] + (points,))
    smooth = fields[0]
    pencil = lax.all_to_all(rows_first(smooth), "radial", split_axis=1, concat_axis=0, tiled=True)
    radial_once = radial_apply(radial_deriv, pencil)
    radial_twice = radial_apply(radial_deriv, radial_once)
    first_flat, second_flat = (
        lax.all_to_all(radial_once, "radial", split_axis=0, concat_axis=1, tiled=True),
        lax.all_to_all(radial_twice, "radial", split_axis=0, concat_axis=1, tiled=True),
    )
    radial_first = rows_back(first_flat, smooth.shape)
    laplace = rows_back(second_flat, smooth.shape) + fields[3]
    theta_deriv = fields[1] * radius_ratio
    axial_deriv = fields[2]
    advection = smooth[0:1] * radial_first + smooth[1:2] * theta_deriv + smooth[2:3] * axial_deriv
    tendency = viscosity * laplace - advection
    rhs_new = section_carry * previous_rhs + tendency
    velocity_new = velocity + section_weight * timestep * rhs_new
    return (velocity_new, rhs_new)


def solution(mesh):
    in_specs = (
        P(None, "axial", "radial", None),
        P(None, "axial", "radial", None),
        P(),
        P("radial"),
    )
    out_specs = (P(None, "axial", "radial", None), P(None, "axial", "radial", None))
    return jax.shard_map(shards, mesh=mesh, in_specs=in_specs, out_specs=out_specs, check_vma=False)
```

profile of v0, /device:TPU:64, one launch (start us, length us, event | category | flops | bytes accessed | tf_op | source)
XLA Modules:
  0.0 100.5 jit_solution(13269798991707380260)
XLA Ops:
  0.6 0.0 copy-start
  0.6 0.0 copy-start.1
  0.7 1.6 %fusion.23 = (f32[192,512]{1,0:T(8,128)S(1)}, f32[192,512]{1,0:T(8,128)S(1)}) fusion(), kind=kLoop, calls=%fused_computation.45 | loop fusion | flops 1474560 | bytes 786432 | tf_op jit(solution)/shard_map/cos | solution.py:38
  2.2 0.0 copy-done.1
  2.2 0.9 fusion
  3.1 1.9 %collective-permute-start.1 = (f32[3,4,8,384]{3,2,1,0:T(8,128)S(1)}, f32[3,4,8,384]{3,2,1,0:T(8,128)S(1)}, u32[]{:S(2)}, u32[]{:S(2)}) collective-permute-start(f32[3,4,8,384]{3,2,1,0:T(8,128)S(1)} %bitcast.61), channel_id=1, source_target_pairs={{0,1},{1,2},{2,3},{3,4},{4,5},{5,6},{6,7},{7,0},{8,9},{9,10},{10,1... | collective-permute-start | bytes 442376 | tf_op jit(solution)/shard_map/ppermute | solution.py:27
  5.0 3.6 %collective-permute-start = (f32[3,4,8,384]{3,2,1,0:T(8,128)S(1)}, f32[3,4,8,384]{3,2,1,0:T(8,128)S(1)}, u32[]{:S(2)}, u32[]{:S(2)}) collective-permute-start(f32[3,4,8,384]{3,2,1,0:T(8,128)S(1)} %bitcast.62), channel_id=1, source_target_pairs={{1,0},{2,1},{3,2},{4,3},{5,4},{6,5},{7,6},{0,7},{9,8},{10,9},{11,1... | collective-permute-start | bytes 442376 | tf_op jit(solution)/shard_map/ppermute | solution.py:28
  8.7 1.6 %broadcast_multiply_fusion = (f32[192,512]{1,0:T(8,128)S(1)}, f32[192,512]{1,0:T(8,128)S(1)}) fusion(f32[192]{0:T(256)S(1)} %fusion.32, f32[192]{0:T(256)S(1)} %fusion.29), kind=kLoop, calls=%fused_computation.42 | loop fusion | flops 1572864 | bytes 787968 | tf_op jit(solution)/shard_map/mul | solution.py:42
  10.3 0.1 slice_multiply_fusion.1
  10.4 0.0 copy-start.3
  10.4 0.1 pad_maximum_fusion.3
  10.5 0.6 copy-done.3
  11.1 0.1 maximum_bitcast_fusion
  11.2 0.0 collective-permute-done.1
  11.2 0.1 collective-permute-done
  11.3 0.1 add_bitcast_fusion
  11.4 0.1 subtract_bitcast_fusion
  11.5 1.4 %fusion.4 = f32[384,512]{1,0:T(8,128)S(1)} fusion(f32[384,384]{1,0:T(8,128)S(1)} %bitcast.67, f32[192,512]{1,0:T(8,128)S(1)} %get-tuple-element.21, f32[192,512]{1,0:T(8,128)S(1)} %get-tuple-element.22), kind=kOutput, calls=%fused_computation.5 | convolution fusion | flops 906166272 | bytes 2162688 | tf_op jit(solution)/shard_map/dot_general | solution.py:94
  12.9 0.1 fusion.36
  13.0 0.1 copy.56
  13.1 0.2 all_to_all.38
  13.3 0.2 copy.24
  13.5 35.7 %all_to_all.51 = f32[8,64,96]{2,0,1:T(8,128)S(1)} all-to-all(f32[8,64,96]{2,0,1:T(8,128)S(1)} %copy.24), channel_id=1, replica_groups=mesh['radial'=64,'axial'=8] {'radial'}, dimensions={1} | all-to-all | bytes 393216 | tf_op jit(solution)/shard_map/all_to_all | solution.py:97
  49.2 0.0 copy-done
  49.2 1.2 %fusion.14 = f32[96,512]{1,0:T(8,128)S(1)} fusion(f32[512,512]{1,0:T(8,128)S(1)} %copy-done, f32[8,64,96]{2,0,1:T(8,128)S(1)} %all_to_all.51), kind=kOutput, calls=%fused_computation.27 | convolution fusion | flops 301989888 | bytes 1441792 | tf_op jit(solution)/shard_map/dot_general | solution.py:58
  50.4 1.1 %convolution_bitcast_fusion = f32[512,96]{0,1:T(8,128)S(1)} fusion(f32[96,512]{1,0:T(8,128)S(1)} %fusion.14, f32[512,512]{1,0:T(8,128)S(1)} %copy-done), kind=kOutput, calls=%fused_computation | convolution fusion | flops 301989888 | bytes 1441792 | tf_op jit(solution)/shard_map/dot_general | solution.py:58
  51.5 0.8 copy.25
  52.4 5.3 %all-to-all-start.1 = ((f32[64,8,96]{2,1,0:T(8,128)}), f32[64,8,96]{2,1,0:T(8,128)S(1)}, u32[]{:S(2)}, u32[]{:S(2)}) async-start(f32[64,8,96]{2,1,0:T(8,128)} %bitcast.14), calls=%async_computation.1 | async-start | bytes 524288 | tf_op jit(solution)/shard_map/all_to_all | solution.py:102
  57.7 0.8 copy.29
  58.5 17.3 %all-to-all-done.1 = f32[64,8,96]{2,1,0:T(8,128)S(1)} async-done(((f32[64,8,96]{2,1,0:T(8,128)}), f32[64,8,96]{2,1,0:T(8,128)S(1)}, u32[]{:S(2)}, u32[]{:S(2)}) %all-to-all-start.1) | async-done | bytes 196640 | tf_op jit(solution)/shard_map/all_to_all | solution.py:102
  75.8 4.6 %all-to-all-start.2 = ((f32[64,8,96]{2,1,0:T(8,128)}), f32[64,8,96]{2,1,0:T(8,128)S(1)}, u32[]{:S(2)}, u32[]{:S(2)}) async-start(f32[64,8,96]{2,1,0:T(8,128)} %bitcast.20), calls=%async_computation.2 | async-start | bytes 524288 | tf_op jit(solution)/shard_map/all_to_all | solution.py:101
  80.6 0.1 copy.26
  80.7 0.2 reshape.73
  80.9 16.4 %all-to-all-done.2 = f32[64,8,96]{2,1,0:T(8,128)S(1)} async-done(((f32[64,8,96]{2,1,0:T(8,128)}), f32[64,8,96]{2,1,0:T(8,128)S(1)}, u32[]{:S(2)}, u32[]{:S(2)}) %all-to-all-start.2) | async-done | bytes 196640 | tf_op jit(solution)/shard_map/all_to_all | solution.py:101
  97.3 0.1 copy.30
  97.4 0.0 copy-start.2
  97.4 0.2 reshape.74
  97.6 0.7 copy-done.2
  98.3 0.7 copy_add_fusion
  99.0 0.7 copy.36
  99.8 0.7 copy.37
  (10 shorter events, 0.2 us)
Async XLA Ops:
  0.6 48.5 %copy-start = (f32[512,512]{1,0:T(8,128)S(1)}, f32[512,512]{1,0:T(8,128)}, u32[]{:S(2)}) copy-start(f32[512,512]{1,0:T(8,128)} %param.6) | copy-start | bytes 3145732
  0.6 1.6 %copy-start.1 = (f32[3,4,8,512]{3,2,1,0:T(8,128)S(1)}, f32[3,4,8,512]{3,2,1,0:T(8,128)}, u32[]{:S(2)}) copy-start(f32[3,4,8,512]{3,2,1,0:T(8,128)} %param.4) | copy-start | bytes 589828
  3.1 8.1 %collective-permute-start.1 = (f32[3,4,8,384]{3,2,1,0:T(8,128)S(1)}, f32[3,4,8,384]{3,2,1,0:T(8,128)S(1)}, u32[]{:S(2)}, u32[]{:S(2)}) collective-permute-start(f32[3,4,8,384]{3,2,1,0:T(8,128)S(1)} %bitcast.61), channel_id=1, source_target_pairs={{0,1},{1,2},{2,3},{3,4},{4,5},{5,6},{6,7},{7,0},{8,9},{9,10},{10,1... | collective-permute-start | bytes 442376 | tf_op jit(solution)/shard_map/ppermute | solution.py:27
  5.0 6.3 %collective-permute-start = (f32[3,4,8,384]{3,2,1,0:T(8,128)S(1)}, f32[3,4,8,384]{3,2,1,0:T(8,128)S(1)}, u32[]{:S(2)}, u32[]{:S(2)}) collective-permute-start(f32[3,4,8,384]{3,2,1,0:T(8,128)S(1)} %bitcast.62), channel_id=1, source_target_pairs={{1,0},{2,1},{3,2},{4,3},{5,4},{6,5},{7,6},{0,7},{9,8},{10,9},{11,1... | collective-permute-start | bytes 442376 | tf_op jit(solution)/shard_map/ppermute | solution.py:28
  10.4 0.7 copy-start.3
  52.4 23.4 %all-to-all-start.1 = ((f32[64,8,96]{2,1,0:T(8,128)}), f32[64,8,96]{2,1,0:T(8,128)S(1)}, u32[]{:S(2)}, u32[]{:S(2)}) async-start(f32[64,8,96]{2,1,0:T(8,128)} %bitcast.14), calls=%async_computation.1 | async-start | bytes 524288 | tf_op jit(solution)/shard_map/all_to_all | solution.py:102
  75.8 21.5 %all-to-all-start.2 = ((f32[64,8,96]{2,1,0:T(8,128)}), f32[64,8,96]{2,1,0:T(8,128)S(1)}, u32[]{:S(2)}, u32[]{:S(2)}) async-start(f32[64,8,96]{2,1,0:T(8,128)} %bitcast.20), calls=%async_computation.2 | async-start | bytes 524288 | tf_op jit(solution)/shard_map/all_to_all | solution.py:101
  97.4 0.9 copy-start.2
where the time goes:
time: 101 us
  blocking collectives  35.7 us (35%)
  waiting for transfers between devices  33.9 us (34%)
  starting transfers between devices  15.5 us (15%)
  local copies, waits for them, and re-layouts  5.65 us (6%)
  matrix products  4.63 us (5%)
  other arithmetic  4.34 us (4%)
    all_to_all x1, blocking collectives, shards(): lax.all_to_all(rows_first(smooth), 'radial', split_axis=1, concat_axis=0,...  35.7 us
    all_to_all x1, waiting for transfers between devices, shards(): lax.all_to_all(radial_twice, 'radial', split_axis=0, concat_axis=1, tiled...  17.3 us
    all_to_all x1, waiting for transfers between devices, shards(): lax.all_to_all(radial_once, 'radial', split_axis=0, concat_axis=1, tiled=...  16.4 us
    all_to_all x1, starting transfers between devices, shards(): lax.all_to_all(radial_twice, 'radial', split_axis=0, concat_axis=1, tiled...  5.27 us
    all_to_all x1, starting transfers between devices, shards(): lax.all_to_all(radial_once, 'radial', split_axis=0, concat_axis=1, tiled=...  4.62 us
    ppermute x1, starting transfers between devices, extended(): after = lax.ppermute(first, axis, down)  3.64 us
    unnamed x10, local copies, waits for them, and re-layouts  2.76 us
    dot_general x2, matrix products, radial_apply(): return jnp.dot(matrix, flat, precision=lax.Precision.HIGHEST)  2.35 us
  transfers between devices with their start and end apart: 4, of which 3 were waited for; matrix products, arithmetic and copies ran while one was open for 3% of the time, Pallas kernels for 0%

commit v1 on v0

v1 whole, which is shorter than its diff:
```python
import functools
import math

import jax
import jax.numpy as jnp
import ml_dtypes
import numpy as np
from jax import lax
from jax.experimental import pallas as pl
from jax.experimental.pallas import tpu as pltpu
from jax.sharding import PartitionSpec as P

KEEP = 192
LANES = 128
GROUP = 32
GROUPS = LANES // GROUP

first_coefs = (4.0 / 5.0, -1.0 / 5.0, 4.0 / 105.0, -1.0 / 280.0)
second_coefs = (8.0 / 5.0, -1.0 / 5.0, 8.0 / 315.0, -1.0 / 560.0)
second_centre = -205.0 / 72.0
viscosity = 0.05
section_carry = -5.0 / 9.0
section_weight = 15.0 / 16.0
timestep = 0.1


def halves(array):
    high = array.astype(jnp.bfloat16)
    low = (array - high.astype(jnp.float32)).astype(jnp.bfloat16)
    return high, low


def host_halves(array):
    high = array.astype(ml_dtypes.bfloat16)
    low = (array - high.astype(np.float64)).astype(ml_dtypes.bfloat16)
    return high, low


def circulants(kept_modes, points):
    modes = np.arange(kept_modes)
    weights = np.where(modes == 0, 1.0, 2.0) / points
    slopes = modes * (2.0 * math.pi / points)
    angles = (modes[:, None] * np.arange(points)[None, :] % points) * (2.0 * math.pi / points)
    shift = (np.arange(points)[None, :] - np.arange(points)[:, None]) % points
    keep = (weights[:, None] * np.cos(angles)).sum(0)
    slope = -(weights[:, None] * slopes[:, None] * np.sin(angles)).sum(0)
    curve = -(weights[:, None] * slopes[:, None] ** 2 * np.cos(angles)).sum(0)
    return keep[shift], slope[shift], curve[shift]


def product(left, right):
    dot = functools.partial(jnp.dot, preferred_element_type=jnp.float32)
    return dot(left[0], right[0]) + (dot(left[0], right[1]) + dot(left[1], right[0]))


def lane_groups(shape):
    return lax.broadcasted_iota(jnp.int32, shape, len(shape) - 1) // GROUP


def filter_kernel(velocity_ref, high_ref, low_ref, smooth_ref, message_ref):
    components, planes, rows, points = velocity_ref.shape
    velocity = velocity_ref[...].reshape(components * planes * rows, points)
    smooth = product(halves(velocity), (high_ref[...], low_ref[...]))
    smooth = smooth.reshape(components, planes, rows, points)
    smooth_ref[...] = smooth
    blocks = points // LANES
    groups = lane_groups((planes, rows, LANES))
    for block in range(blocks):
        tile = smooth[:, :, :, block * LANES : (block + 1) * LANES]
        turned = [tile[0]] + [pltpu.roll(tile[c], c * GROUP, 2) for c in range(1, components)]
        for part in range(GROUPS):
            chosen = jnp.zeros_like(turned[0])
            for c in range(components):
                chosen = jnp.where(groups == (part + c) % GROUPS, turned[c], chosen)
            for plane in range(planes):
                message_ref[(plane * blocks + block) * GROUPS + part] = chosen[plane]


def theta_kernel(velocity_ref, high_ref, low_ref, slope_ref, curve_ref):
    components, planes, rows, points = velocity_ref.shape
    velocity = velocity_ref[...].reshape(components * planes * rows, points)
    both = product(halves(velocity), (high_ref[...], low_ref[...]))
    slope_ref[...] = both[:, :points].reshape(velocity_ref.shape)
    curve_ref[...] = both[:, points:].reshape(velocity_ref.shape)


def radial_kernel(part_ref, pencil_ref, matrix_ref, result_ref):
    part = part_ref[0]
    pencil = pencil_ref[...]
    matrix = halves(matrix_ref[...])
    once = product(matrix, halves(pencil))
    twice = product(matrix, halves(once))
    groups = lane_groups(pencil.shape)
    place = lax.rem(groups - part + GROUPS, GROUPS)
    speed = jnp.where(place == 0, pencil, jnp.zeros_like(pencil))
    speed = jnp.where(place == 1, pltpu.roll(pencil, GROUP, 1), speed)
    speed = jnp.where(place == 2, pltpu.roll(pencil, 2 * GROUP, 1), speed)
    result_ref[...] = viscosity * twice - speed * once


def local_kernel(
    smooth_ref, before_ref, after_ref, slope_ref, curve_ref, previous_ref, ratio_ref, result_ref
):
    components, planes, rows, points = smooth_ref.shape
    ratio = ratio_ref[...]
    square = ratio * ratio
    for plane in range(planes):
        speed_theta = smooth_ref[1, plane] * ratio
        speed_axial = smooth_ref[2, plane]
        for c in range(components):
            def at(index):
                if index < 0:
                    return before_ref[c, index + planes]
                if index >= planes:
                    return after_ref[c, index - planes]
                return smooth_ref[c, index]

            first = jnp.zeros_like(speed_axial)
            second = second_centre * smooth_ref[c, plane]
            for k in range(4):
                up, down = at(plane + k + 1), at(plane - k - 1)
                first = first + first_coefs[k] * (up - down)
                second = second + second_coefs[k] * (up + down)
            second = second + square * curve_ref[c, plane]
            result_ref[c, plane] = (
                section_carry * previous_ref[c, plane]
                + viscosity * second
                - speed_theta * slope_ref[c, plane]
                - speed_axial * first
            )


def final_kernel(radial_ref, local_ref, velocity_ref, velocity_out_ref, rhs_out_ref):
    components, planes, rows, points = velocity_ref.shape
    blocks = points // LANES
    groups = lane_groups((rows, LANES))
    for plane in range(planes):
        for block in range(blocks):
            tiles = [
                radial_ref[(plane * blocks + block) * GROUPS + part] for part in range(GROUPS)
            ]
            for c in range(components):
                chosen = tiles[0]
                for part in range(1, GROUPS):
                    chosen = jnp.where(groups == (part + c) % GROUPS, tiles[part], chosen)
                if c > 0:
                    chosen = pltpu.roll(chosen, LANES - c * GROUP, 1)
                lanes = slice(block * LANES, (block + 1) * LANES)
                rhs = local_ref[c, plane, :, lanes] + chosen
                rhs_out_ref[c, plane, :, lanes] = rhs
                velocity_out_ref[c, plane, :, lanes] = (
                    velocity_ref[c, plane, :, lanes] + (section_weight * timestep) * rhs
                )


VMEM = pl.BlockSpec(memory_space=pltpu.VMEM)
SMEM = pl.BlockSpec(memory_space=pltpu.SMEM)


def call(kernel, in_specs, shapes, name, flops, moved):
    out_shape = [jax.ShapeDtypeStruct(shape, jnp.float32) for shape in shapes]
    single = len(out_shape) == 1
    return pl.pallas_call(
        kernel,
        out_shape=out_shape[0] if single else out_shape,
        in_specs=in_specs,
        out_specs=VMEM if single else [VMEM] * len(out_shape),
        compiler_params=pltpu.CompilerParams(vmem_limit_bytes=24 * 1024 * 1024),
        cost_estimate=pl.CostEstimate(flops=flops, bytes_accessed=moved, transcendentals=0),
        name=name,
    )


def shards(velocity, previous_rhs, radial_deriv, inv_radius):
    components, planes, radial_rows, points = velocity.shape
    peers = lax.axis_size("radial")
    shape = velocity.shape
    size = velocity.size
    keep, slope, curve = circulants(KEEP, points)
    keep_high, keep_low = host_halves(keep)
    theta_high, theta_low = host_halves(np.concatenate([slope, curve], axis=1))

    smooth, message = call(
        filter_kernel,
        [VMEM] * 3,
        [shape, (peers, radial_rows, LANES)],
        "filter",
        6 * size * points,
        20 * size,
    )(velocity, jnp.asarray(keep_high), jnp.asarray(keep_low))
    pencil = lax.all_to_all(message, "radial", split_axis=0, concat_axis=0, tiled=True)

    ring = lax.axis_size("axial")
    up = [(i, (i + 1) % ring) for i in range(ring)]
    down = [(j, i) for i, j in up]
    before = lax.ppermute(smooth, "axial", up)
    after = lax.ppermute(smooth, "axial", down)
    theta_slope, theta_curve = call(
        theta_kernel, [VMEM] * 3, [shape, shape], "theta", 12 * size * points, 24 * size
    )(velocity, jnp.asarray(theta_high), jnp.asarray(theta_low))

    part = (lax.axis_index("radial") % GROUPS).astype(jnp.int32).reshape(1)
    full = peers * radial_rows
    result = call(
        radial_kernel,
        [SMEM, VMEM, VMEM],
        [(full, LANES)],
        "radial",
        12 * full * full * LANES,
        4 * full * (full + 2 * LANES),
    )(part, pencil.reshape(full, LANES), radial_deriv)
    radial = lax.all_to_all(
        result.reshape(peers, radial_rows, LANES), "radial", split_axis=0, concat_axis=0, tiled=True
    )
    ratio = jnp.broadcast_to(inv_radius[:, None], (radial_rows, points))
    local = call(local_kernel, [VMEM] * 7, [shape], "local", 40 * size, 32 * size)(
        smooth, before, after, theta_slope, theta_curve, previous_rhs, ratio
    )
    return call(final_kernel, [VMEM] * 3, [shape, shape], "final", 10 * size, 20 * size)(
        radial, local, velocity
    )


def solution(mesh):
    in_specs = (
        P(None, "axial", "radial", None),
        P(None, "axial", "radial", None),
        P(),
        P("radial"),
    )
    out_specs = (P(None, "axial", "radial", None), P(None, "axial", "radial", None))

    def whole(*args):
        return tuple(shards(*args))

    return jax.shard_map(whole, mesh=mesh, in_specs=in_specs, out_specs=out_specs, check_vma=False)
```

time: 101 us -> 67 us (0.66)
  the two profiles are of different devices: /device:TPU:64 before, /device:TPU:8 now
where the time goes in v1:
time: 67 us; the launch traced here: 66.5 us
  starting transfers between devices  29.9 us (45%)
  waiting for transfers between devices  26.7 us (40%)
  Pallas kernels  4.68 us (7%)
  local copies, waits for them, and re-layouts  4.46 us (7%)
  between operations  0.76 us (1%)
    all_to_all x1, starting transfers between devices, shards(): lax.all_to_all(message, 'radial', split_axis=0, concat_axis=0, tiled=True)  19.1 us
    all_to_all x1, waiting for transfers between devices, shards(): lax.all_to_all(message, 'radial', split_axis=0, concat_axis=0, tiled=True)  16.9 us
    all_to_all x1, starting transfers between devices, shards(): lax.all_to_all(result.reshape(peers, radial_rows, LANES), 'radial', split...  5.22 us
    ppermute x1, waiting for transfers between devices, shards(): after = lax.ppermute(smooth, 'axial', down)  4.8 us
    unnamed x24, local copies, waits for them, and re-layouts  4.39 us
    ppermute x1, waiting for transfers between devices, shards(): before = lax.ppermute(smooth, 'axial', up)  3.81 us
    ppermute x1, starting transfers between devices, shards(): after = lax.ppermute(smooth, 'axial', down)  3.6 us
    ppermute x1, starting transfers between devices, shards(): before = lax.ppermute(smooth, 'axial', up)  1.92 us
  transfers between devices with their start and end apart: 4, of which 4 were waited for; matrix products, arithmetic and copies ran while one was open for 0% of the time, Pallas kernels for 1%

profile of v1, /device:TPU:8, one launch (start us, length us, event | category | flops | bytes accessed | tf_op | source)
XLA Modules:
  0.0 66.5 jit_solution(8271006021071458436)
XLA Ops:
  0.6 0.0 copy-start
  0.6 0.9 %copy-done = f32[3,4,8,512]{3,2,1,0:T(8,128)S(1)} copy-done((f32[3,4,8,512]{3,2,1,0:T(8,128)S(1)}, f32[3,4,8,512]{3,2,1,0:T(8,128)}, u32[]{:S(2)}) %copy-start) | copy-done | bytes 196632
  1.6 0.0 copy-start.6
  1.6 1.0 %copy-done.6 = bf16[512,512]{1,0:T(8,128)(2,1)S(1)} copy-done((bf16[512,512]{1,0:T(8,128)(2,1)S(1)}, bf16[512,512]{1,0:T(8,128)(2,1)}, u32[]{:S(2)}) %copy-start.6) | copy-done | bytes 524312
  2.6 0.0 copy-start.7
  2.6 1.0 %copy-done.7 = bf16[512,512]{1,0:T(8,128)(2,1)S(1)} copy-done((bf16[512,512]{1,0:T(8,128)(2,1)S(1)}, bf16[512,512]{1,0:T(8,128)(2,1)}, u32[]{:S(2)}) %copy-start.7) | copy-done | bytes 524312
  3.6 0.0 copy-start.2
  3.6 1.2 %filter.1 = (f32[3,4,8,512]{3,2,1,0:T(8,128)S(1)}, f32[64,8,128]{2,1,0:T(8,128)}) custom-call(f32[3,4,8,512]{3,2,1,0:T(8,128)S(1)} %copy-done, bf16[512,512]{1,0:T(8,128)(2,1)S(1)} %copy-done.7, bf16[512,512]{1,0:T(8,128)(2,1)S(1)} %copy-done.6), custom_call_target="tpu_custom_call" | custom-call | flops 150994944 | bytes 983040 | tf_op jit(solution)/shard_map/filter/pallas_call | solution.py:183
  4.8 0.0 copy-start.9
  4.8 0.7 %copy-done.9 = f32[3,4,8,512]{3,2,1,0:T(8,128)} copy-done((f32[3,4,8,512]{3,2,1,0:T(8,128)}, f32[3,4,8,512]{3,2,1,0:T(8,128)S(1)}, u32[]{:S(2)}) %copy-start.9) | copy-done | bytes 196632
  5.5 0.0 copy-start.4
  5.5 19.1 %all-to-all-start = ((f32[64,8,128]{2,1,0:T(8,128)}), f32[64,8,128]{2,1,0:T(8,128)S(1)}, u32[]{:S(2)}, u32[]{:S(2)}) async-start(f32[64,8,128]{2,1,0:T(8,128)} %get-tuple-element.6), calls=%async_computation | async-start | bytes 524288 | tf_op jit(solution)/shard_map/all_to_all | solution.py:191
  24.7 16.9 %all-to-all-done = f32[64,8,128]{2,1,0:T(8,128)S(1)} async-done(((f32[64,8,128]{2,1,0:T(8,128)}), f32[64,8,128]{2,1,0:T(8,128)S(1)}, u32[]{:S(2)}, u32[]{:S(2)}) %all-to-all-start) | async-done | bytes 262176 | tf_op jit(solution)/shard_map/all_to_all | solution.py:191
  41.6 0.0 copy-done.2
  41.6 0.0 copy-start.3
  41.6 1.8 %radial.1 = f32[512,128]{1,0:T(8,128)S(1)} custom-call(s32[1]{0:T(128)} %bitcast.part_ref, f32[512,128]{1,0:T(8,128)S(1)} %bitcast.3, f32[512,512]{1,0:T(8,128)S(1)} %copy-done.2), custom_call_target="tpu_custom_call" | custom-call | flops 402653184 | bytes 1572864 | tf_op jit(solution)/shard_map/radial/pallas_call | solution.py:204
  43.4 0.0 copy-start.5
  43.4 0.7 %copy-done.5 = f32[512,128]{1,0:T(8,128)} copy-done((f32[512,128]{1,0:T(8,128)}, f32[512,128]{1,0:T(8,128)S(1)}, u32[]{:S(2)}) %copy-start.5) | copy-done | bytes 262168
  44.1 0.0 copy-start.10
  44.1 0.0 copy-start.1
  44.1 5.2 %all-to-all-start.1 = ((f32[64,8,128]{2,1,0:T(8,128)}), f32[64,8,128]{2,1,0:T(8,128)S(1)}, u32[]{:S(2)}, u32[]{:S(2)}) async-start(f32[64,8,128]{2,1,0:T(8,128)} %bitcast.4), calls=%async_computation.1 | async-start | bytes 524288 | tf_op jit(solution)/shard_map/all_to_all | solution.py:212
  49.3 0.0 copy-done.10
  49.3 0.0 copy-start.11
  49.3 0.0 copy-start.8
  49.4 3.6 %collective-permute-start.1 = (f32[3,4,8,512]{3,2,1,0:T(8,128)S(1)}, f32[3,4,8,512]{3,2,1,0:T(8,128)S(1)}, u32[]{:S(2)}, u32[]{:S(2)}) collective-permute-start(f32[3,4,8,512]{3,2,1,0:T(8,128)S(1)} %copy-done.10), channel_id=1, source_target_pairs={{1,0},{2,1},{3,2},{4,3},{5,4},{6,5},{7,6},{0,7},{9,8},{10,9},{11,1... | collective-permute-start | bytes 589832 | tf_op jit(solution)/shard_map/ppermute | solution.py:197
  53.0 1.9 %collective-permute-start = (f32[3,4,8,512]{3,2,1,0:T(8,128)S(1)}, f32[3,4,8,512]{3,2,1,0:T(8,128)S(1)}, u32[]{:S(2)}, u32[]{:S(2)}) collective-permute-start(f32[3,4,8,512]{3,2,1,0:T(8,128)S(1)} %copy-done.10), channel_id=1, source_target_pairs={{0,1},{1,2},{2,3},{3,4},{4,5},{5,6},{6,7},{7,0},{8,9},{9,10},{10,1... | collective-permute-start | bytes 589832 | tf_op jit(solution)/shard_map/ppermute | solution.py:196
  54.9 0.0 copy-done.4
  54.9 0.0 copy-done.3
  54.9 0.0 copy-done.1
  54.9 0.6 theta.1
  55.6 4.8 %collective-permute-done.1.after_ref = f32[3,4,8,512]{3,2,1,0:T(8,128)S(1)} collective-permute-done((f32[3,4,8,512]{3,2,1,0:T(8,128)S(1)}, f32[3,4,8,512]{3,2,1,0:T(8,128)S(1)}, u32[]{:S(2)}, u32[]{:S(2)}) %collective-permute-start.1) | collective-permute-done | bytes 196640 | tf_op jit(solution)/shard_map/ppermute | solution.py:197
  60.4 3.8 %collective-permute-done.before_ref = f32[3,4,8,512]{3,2,1,0:T(8,128)S(1)} collective-permute-done((f32[3,4,8,512]{3,2,1,0:T(8,128)S(1)}, f32[3,4,8,512]{3,2,1,0:T(8,128)S(1)}, u32[]{:S(2)}, u32[]{:S(2)}) %collective-permute-start) | collective-permute-done | bytes 196640 | tf_op jit(solution)/shard_map/ppermute | solution.py:196
  64.2 0.0 copy-done.11
  64.2 0.1 broadcast_in_dim.2.ratio_ref
  64.2 0.0 copy-done.8
  64.2 0.2 local.1.local_ref
  64.5 1.2 %all-to-all-done.1.radial_ref = f32[64,8,128]{2,1,0:T(8,128)S(1)} async-done(((f32[64,8,128]{2,1,0:T(8,128)}), f32[64,8,128]{2,1,0:T(8,128)S(1)}, u32[]{:S(2)}, u32[]{:S(2)}) %all-to-all-start.1) | async-done | bytes 262176 | tf_op jit(solution)/shard_map/all_to_all | solution.py:212
  65.7 0.9 %final.1 = (f32[3,4,8,512]{3,2,1,0:T(8,128)}, f32[3,4,8,512]{3,2,1,0:T(8,128)}) custom-call(f32[64,8,128]{2,1,0:T(8,128)S(1)} %all-to-all-done.1.radial_ref, f32[3,4,8,512]{3,2,1,0:T(8,128)S(1)} %local.1.local_ref, f32[3,4,8,512]{3,2,1,0:T(8,128)S(1)} %copy-done.1), custom_call_target="tpu_custom_call" | custom-call | flops 491520 | bytes 983040 | tf_op jit(solution)/shard_map/final/pallas_call | solution.py:219
Async XLA Ops:
  0.6 0.9 %copy-start = (f32[3,4,8,512]{3,2,1,0:T(8,128)S(1)}, f32[3,4,8,512]{3,2,1,0:T(8,128)}, u32[]{:S(2)}) copy-start(f32[3,4,8,512]{3,2,1,0:T(8,128)} %velocity_ref.5) | copy-start | bytes 589828
  1.6 1.0 %copy-start.6 = (bf16[512,512]{1,0:T(8,128)(2,1)S(1)}, bf16[512,512]{1,0:T(8,128)(2,1)}, u32[]{:S(2)}) copy-start(bf16[512,512]{1,0:T(8,128)(2,1)} %constant.28.clone.low_ref) | copy-start | bytes 1572868
  2.6 1.0 %copy-start.7 = (bf16[512,512]{1,0:T(8,128)(2,1)S(1)}, bf16[512,512]{1,0:T(8,128)(2,1)}, u32[]{:S(2)}) copy-start(bf16[512,512]{1,0:T(8,128)(2,1)} %constant.27.clone.high_ref) | copy-start | bytes 1572868
  3.6 37.9 %copy-start.2 = (f32[512,512]{1,0:T(8,128)S(1)}, f32[512,512]{1,0:T(8,128)}, u32[]{:S(2)}) copy-start(f32[512,512]{1,0:T(8,128)} %matrix_ref.1) | copy-start | bytes 3145732
  4.8 0.7 %copy-start.9 = (f32[3,4,8,512]{3,2,1,0:T(8,128)}, f32[3,4,8,512]{3,2,1,0:T(8,128)S(1)}, u32[]{:S(2)}) copy-start(f32[3,4,8,512]{3,2,1,0:T(8,128)S(1)} %get-tuple-element.7.smooth_ref) | copy-start | bytes 589828
  5.5 49.4 %copy-start.4 = (bf16[512,1024]{1,0:T(8,128)(2,1)S(1)}, bf16[512,1024]{1,0:T(8,128)(2,1)}, u32[]{:S(2)}) copy-start(bf16[512,1024]{1,0:T(8,128)(2,1)} %constant.29.clone.high_ref) | copy-start | bytes 3145732
  5.5 36.1 %all-to-all-start = ((f32[64,8,128]{2,1,0:T(8,128)}), f32[64,8,128]{2,1,0:T(8,128)S(1)}, u32[]{:S(2)}, u32[]{:S(2)}) async-start(f32[64,8,128]{2,1,0:T(8,128)} %get-tuple-element.6), calls=%async_computation | async-start | bytes 524288 | tf_op jit(solution)/shard_map/all_to_all | solution.py:191
  41.6 13.3 %copy-start.3 = (bf16[512,1024]{1,0:T(8,128)(2,1)S(1)}, bf16[512,1024]{1,0:T(8,128)(2,1)}, u32[]{:S(2)}) copy-start(bf16[512,1024]{1,0:T(8,128)(2,1)} %constant.30.clone.low_ref) | copy-start | bytes 3145732
  43.4 0.7 %copy-start.5 = (f32[512,128]{1,0:T(8,128)}, f32[512,128]{1,0:T(8,128)S(1)}, u32[]{:S(2)}) copy-start(f32[512,128]{1,0:T(8,128)S(1)} %radial.1) | copy-start | bytes 786436
  44.1 5.2 %copy-start.10 = (f32[3,4,8,512]{3,2,1,0:T(8,128)S(1)}, f32[3,4,8,512]{3,2,1,0:T(8,128)}, u32[]{:S(2)}) copy-start(f32[3,4,8,512]{3,2,1,0:T(8,128)} %copy-done.9) | copy-start | bytes 589828
  44.1 10.8 %copy-start.1 = (f32[3,4,8,512]{3,2,1,0:T(8,128)S(1)}, f32[3,4,8,512]{3,2,1,0:T(8,128)}, u32[]{:S(2)}) copy-start(f32[3,4,8,512]{3,2,1,0:T(8,128)} %velocity_ref.5) | copy-start | bytes 589828
  44.1 21.6 %all-to-all-start.1 = ((f32[64,8,128]{2,1,0:T(8,128)}), f32[64,8,128]{2,1,0:T(8,128)S(1)}, u32[]{:S(2)}, u32[]{:S(2)}) async-start(f32[64,8,128]{2,1,0:T(8,128)} %bitcast.4), calls=%async_computation.1 | async-start | bytes 524288 | tf_op jit(solution)/shard_map/all_to_all | solution.py:212
  49.3 14.8 %copy-start.11 = (f32[8]{0:T(128)S(1)}, f32[8]{0:T(128)}, u32[]{:S(2)}) copy-start(f32[8]{0:T(128)} %param.11) | copy-start | bytes 100
  49.3 14.9 %copy-start.8 = (f32[3,4,8,512]{3,2,1,0:T(8,128)S(1)}, f32[3,4,8,512]{3,2,1,0:T(8,128)}, u32[]{:S(2)}) copy-start(f32[3,4,8,512]{3,2,1,0:T(8,128)} %previous_ref.1) | copy-start | bytes 589828
  49.4 11.0 %collective-permute-start.1 = (f32[3,4,8,512]{3,2,1,0:T(8,128)S(1)}, f32[3,4,8,512]{3,2,1,0:T(8,128)S(1)}, u32[]{:S(2)}, u32[]{:S(2)}) collective-permute-start(f32[3,4,8,512]{3,2,1,0:T(8,128)S(1)} %copy-done.10), channel_id=1, source_target_pairs={{1,0},{2,1},{3,2},{4,3},{5,4},{6,5},{7,6},{0,7},{9,8},{10,9},{11,1... | collective-permute-start | bytes 589832 | tf_op jit(solution)/shard_map/ppermute | solution.py:197
  53.0 11.2 %collective-permute-start = (f32[3,4,8,512]{3,2,1,0:T(8,128)S(1)}, f32[3,4,8,512]{3,2,1,0:T(8,128)S(1)}, u32[]{:S(2)}, u32[]{:S(2)}) collective-permute-start(f32[3,4,8,512]{3,2,1,0:T(8,128)S(1)} %copy-done.10), channel_id=1, source_target_pairs={{0,1},{1,2},{2,3},{3,4},{4,5},{5,6},{6,7},{7,0},{8,9},{9,10},{10,1... | collective-permute-start | bytes 589832 | tf_op jit(solution)/shard_map/ppermute | solution.py:196

commit v2 on v1

v2 whole, which is shorter than its diff:
```python
import functools
import math

import jax
import jax.numpy as jnp
import ml_dtypes
import numpy as np
from jax import lax
from jax.experimental import pallas as pl
from jax.experimental.pallas import tpu as pltpu
from jax.sharding import PartitionSpec as P

KEEP = 192
LANES = 128
GROUP = 32
GROUPS = LANES // GROUP

first_coefs = (4.0 / 5.0, -1.0 / 5.0, 4.0 / 105.0, -1.0 / 280.0)
second_coefs = (8.0 / 5.0, -1.0 / 5.0, 8.0 / 315.0, -1.0 / 560.0)
second_centre = -205.0 / 72.0
viscosity = 0.05
section_carry = -5.0 / 9.0
section_weight = 15.0 / 16.0
timestep = 0.1


def halves(array):
    high = array.astype(jnp.bfloat16)
    low = (array - high.astype(jnp.float32)).astype(jnp.bfloat16)
    return high, low


def host_halves(array):
    high = array.astype(ml_dtypes.bfloat16)
    low = (array - high.astype(np.float64)).astype(ml_dtypes.bfloat16)
    return high, low


def circulants(kept_modes, points):
    modes = np.arange(kept_modes)
    weights = np.where(modes == 0, 1.0, 2.0) / points
    slopes = modes * (2.0 * math.pi / points)
    angles = (modes[:, None] * np.arange(points)[None, :] % points) * (2.0 * math.pi / points)
    shift = (np.arange(points)[None, :] - np.arange(points)[:, None]) % points
    keep = (weights[:, None] * np.cos(angles)).sum(0)
    slope = -(weights[:, None] * slopes[:, None] * np.sin(angles)).sum(0)
    curve = -(weights[:, None] * slopes[:, None] ** 2 * np.cos(angles)).sum(0)
    return keep[shift], slope[shift], curve[shift]


def product(left, right):
    dot = functools.partial(jnp.dot, preferred_element_type=jnp.float32)
    return dot(left[0], right[0]) + (dot(left[0], right[1]) + dot(left[1], right[0]))


def lane_groups(shape):
    return lax.broadcasted_iota(jnp.int32, shape, len(shape) - 1) // GROUP


def filter_kernel(
    velocity_hbm,
    high_hbm,
    low_hbm,
    smooth_hbm,
    message_hbm,
    velocity_ref,
    high_ref,
    low_ref,
    smooth_ref,
    message_ref,
    in_sems,
    out_sems,
):
    sections, points, width = high_ref.shape
    components, planes, rows, _ = velocity_ref.shape
    incoming = [pltpu.make_async_copy(velocity_hbm, velocity_ref, in_sems.at[0])]
    for section in range(sections):
        for source, target in ((high_hbm, high_ref), (low_hbm, low_ref)):
            incoming.append(
                pltpu.make_async_copy(
                    source.at[section], target.at[section], in_sems.at[len(incoming)]
                )
            )
    for copy in incoming:
        copy.start()
    incoming[0].wait()
    lines = components * planes * rows
    high, low = halves(velocity_ref[...].reshape(lines, points))
    both = jnp.concatenate([high, low], axis=0)
    groups = lane_groups((planes, rows, LANES))
    outgoing = []
    for section in range(sections):
        incoming[1 + 2 * section].wait()
        large = jnp.dot(both, high_ref[section], preferred_element_type=jnp.float32)
        incoming[2 + 2 * section].wait()
        small = jnp.dot(high, low_ref[section], preferred_element_type=jnp.float32)
        smooth = large[:lines] + (large[lines:] + small)
        smooth = smooth.reshape(components, planes, rows, width)
        for local in range(width // LANES):
            block = section * (width // LANES) + local
            tile = smooth[:, :, :, local * LANES : (local + 1) * LANES]
            smooth_ref[block] = tile
            turned = [tile[0]] + [pltpu.roll(tile[c], c * GROUP, 2) for c in range(1, components)]
            for part in range(GROUPS):
                chosen = jnp.zeros_like(turned[0])
                for c in range(components):
                    chosen = jnp.where(groups == (part + c) % GROUPS, turned[c], chosen)
                message_ref[block, part] = chosen
        here = pl.ds(section * (width // LANES), width // LANES)
        for source, target in ((message_ref, message_hbm), (smooth_ref, smooth_hbm)):
            copy = pltpu.make_async_copy(
                source.at[here], target.at[here], out_sems.at[len(outgoing)]
            )
            copy.start()
            outgoing.append(copy)
    for copy in outgoing:
        copy.wait()


def theta_kernel(velocity_ref, table_hbm, slope_ref, curve_ref, table_ref, sem):
    copy = pltpu.make_async_copy(table_hbm, table_ref, sem)
    copy.start()
    components, planes, rows, points = velocity_ref.shape
    velocity = halves(velocity_ref[...].reshape(components * planes * rows, points))
    copy.wait()
    both = product(velocity, (table_ref[0], table_ref[1]))
    slope_ref[...] = both[:, :points].reshape(velocity_ref.shape)
    curve_ref[...] = both[:, points:].reshape(velocity_ref.shape)


def split_kernel(matrix_ref, split_ref):
    split_ref[0], split_ref[1] = halves(matrix_ref[...])


def wide_product(split_ref, rows, right):
    high, low = halves(right)
    both = jnp.concatenate([high, low], axis=1)
    large = jnp.dot(split_ref[0, rows], both, preferred_element_type=jnp.float32)
    small = jnp.dot(split_ref[1, rows], high, preferred_element_type=jnp.float32)
    return large[:, :LANES] + (large[:, LANES:] + small)


def radial_kernel(planes, pencil_ref, split_ref, result_hbm, result_ref, sems):
    part = lax.rem(lax.div(lax.axis_index("radial"), planes), GROUPS)
    pencil = pencil_ref[...]
    full = pencil.shape[0]
    once = wide_product(split_ref, slice(None), pencil)
    groups = lane_groups(pencil.shape)
    place = lax.rem(groups - part + GROUPS, GROUPS)
    speed = jnp.where(place == 0, pencil, jnp.zeros_like(pencil))
    speed = jnp.where(place == 1, pltpu.roll(pencil, GROUP, 1), speed)
    speed = jnp.where(place == 2, pltpu.roll(pencil, 2 * GROUP, 1), speed)
    pieces = sems.shape[0]
    copies = []
    for piece in range(pieces):
        rows = slice(piece * full // pieces, (piece + 1) * full // pieces)
        twice = wide_product(split_ref, rows, once)
        result_ref[rows] = viscosity * twice - speed[rows] * once[rows]
        here = pl.ds(piece * full // pieces, full // pieces)
        copy = pltpu.make_async_copy(result_ref.at[here], result_hbm.at[here], sems.at[piece])
        copy.start()
        copies.append(copy)
    for copy in copies:
        copy.wait()


def local_kernel(
    smooth_ref, before_ref, after_ref, slope_ref, curve_ref, previous_ref, ratio_ref, result_ref
):
    blocks, components, planes, rows, _ = smooth_ref.shape
    ratio = ratio_ref[...]
    square = ratio * ratio
    for block in range(blocks):
        lanes = slice(block * LANES, (block + 1) * LANES)
        for c in range(components):
            line = [before_ref[block, c, plane] for plane in range(planes)]
            line += [smooth_ref[block, c, plane] for plane in range(planes)]
            line += [after_ref[block, c, plane] for plane in range(planes)]
            for plane in range(planes):
                here = planes + plane
                first = jnp.zeros_like(line[here])
                second = second_centre * line[here]
                for k in range(4):
                    up, down = line[here + k + 1], line[here - k - 1]
                    first = first + first_coefs[k] * (up - down)
                    second = second + second_coefs[k] * (up + down)
                second = second + square * curve_ref[c, plane, :, lanes]
                speed_theta = smooth_ref[block, 1, plane] * ratio
                result_ref[c, plane, :, lanes] = (
                    section_carry * previous_ref[c, plane, :, lanes]
                    + viscosity * second
                    - speed_theta * slope_ref[c, plane, :, lanes]
                    - smooth_ref[block, 2, plane] * first
                )


def final_kernel(radial_ref, local_ref, velocity_ref, velocity_out_ref, rhs_out_ref):
    components, planes, rows, points = velocity_ref.shape
    blocks = points // LANES
    groups = lane_groups((rows, LANES))
    for plane in range(planes):
        for block in range(blocks):
            tiles = [
                radial_ref[(block * GROUPS + part) * planes + plane] for part in range(GROUPS)
            ]
            for c in range(components):
                chosen = tiles[0]
                for part in range(1, GROUPS):
                    chosen = jnp.where(groups == (part + c) % GROUPS, tiles[part], chosen)
                if c > 0:
                    chosen = pltpu.roll(chosen, LANES - c * GROUP, 1)
                lanes = slice(block * LANES, (block + 1) * LANES)
                rhs = local_ref[c, plane, :, lanes] + chosen
                rhs_out_ref[c, plane, :, lanes] = rhs
                velocity_out_ref[c, plane, :, lanes] = (
                    velocity_ref[c, plane, :, lanes] + (section_weight * timestep) * rhs
                )


VMEM = pl.BlockSpec(memory_space=pltpu.VMEM)
HBM = pl.BlockSpec(memory_space=pltpu.HBM)


in_hbm = functools.partial(pltpu.with_memory_space_constraint, memory_space=pltpu.HBM)
in_vmem = functools.partial(pltpu.with_memory_space_constraint, memory_space=pltpu.VMEM)


def call(kernel, name, in_specs, outs, flops, moved, scratch=()):
    return pl.pallas_call(
        kernel,
        out_shape=[
            pltpu.HBM(shape, dtype) if spec is HBM else jax.ShapeDtypeStruct(shape, dtype)
            for shape, dtype, spec in outs
        ],
        in_specs=in_specs,
        out_specs=[spec for _, _, spec in outs],
        scratch_shapes=list(scratch),
        compiler_params=pltpu.CompilerParams(vmem_limit_bytes=24 * 1024 * 1024),
        cost_estimate=pl.CostEstimate(flops=flops, bytes_accessed=moved, transcendentals=0),
        name=name,
    )


def sections_of(matrix, sections):
    points, width = matrix.shape
    return np.ascontiguousarray(
        np.transpose(matrix.reshape(points, sections, width // sections), (1, 0, 2))
    )


def shards(velocity, previous_rhs, radial_deriv, inv_radius):
    components, planes, radial_rows, points = velocity.shape
    peers = lax.axis_size("radial")
    shape = velocity.shape
    size = velocity.size
    blocks = points // LANES
    sections = 2
    f32, bf16, dma = jnp.float32, jnp.bfloat16, pltpu.SemaphoreType.DMA
    keep, slope, curve = circulants(KEEP, points)
    keep_high, keep_low = (sections_of(half, sections) for half in host_halves(keep))
    theta = np.stack(host_halves(np.concatenate([slope, curve], axis=1)))

    smooth_shape = (blocks, components, planes, radial_rows, LANES)
    message_shape = (blocks, GROUPS, planes, radial_rows, LANES)
    smooth, message = call(
        filter_kernel,
        "filter",
        [HBM] * 3,
        [(smooth_shape, f32, HBM), (message_shape, f32, HBM)],
        6 * size * points,
        20 * size,
        [
            pltpu.VMEM(shape, f32),
            pltpu.VMEM(keep_high.shape, bf16),
            pltpu.VMEM(keep_low.shape, bf16),
            pltpu.VMEM(smooth_shape, f32),
            pltpu.VMEM(message_shape, f32),
            dma((1 + 2 * sections,)),
            dma((2 * sections,)),
        ],
    )(*(in_hbm(part) for part in (velocity, jnp.asarray(keep_high), jnp.asarray(keep_low))))
    pencil = lax.all_to_all(
        message.reshape(peers, radial_rows, LANES), "radial", split_axis=0, concat_axis=0, tiled=True
    )

    ring = lax.axis_size("axial")
    up = [(i, (i + 1) % ring) for i in range(ring)]
    down = [(j, i) for i, j in up]
    before = lax.ppermute(smooth, "axial", up)
    after = lax.ppermute(smooth, "axial", down)
    theta_slope, theta_curve = call(
        theta_kernel,
        "theta",
        [VMEM, HBM],
        [(shape, f32, VMEM)] * 2,
        12 * size * points,
        24 * size,
        [pltpu.VMEM(theta.shape, bf16), dma(())],
    )(velocity, in_hbm(jnp.asarray(theta)))

    full = peers * radial_rows
    (split,) = call(
        split_kernel,
        "split",
        [VMEM],
        [((2, full, full), bf16, VMEM)],
        4 * full * full,
        8 * full * full,
    )(radial_deriv)
    pieces = 4
    (result,) = call(
        functools.partial(radial_kernel, planes),
        "radial",
        [VMEM] * 2,
        [((full, LANES), f32, HBM)],
        12 * full * full * LANES,
        4 * full * (full + 2 * LANES),
        [pltpu.VMEM((full, LANES), f32), dma((pieces,))],
    )(in_vmem(pencil.reshape(full, LANES)), split)
    radial = lax.all_to_all(
        result.reshape(peers, radial_rows, LANES), "radial", split_axis=0, concat_axis=0, tiled=True
    )
    ratio = jnp.broadcast_to(inv_radius[:, None], (radial_rows, LANES))
    (local,) = call(
        local_kernel, "local", [VMEM] * 7, [(shape, f32, VMEM)], 40 * size, 32 * size
    )(smooth, before, after, theta_slope, theta_curve, previous_rhs, ratio)
    return call(
        final_kernel, "final", [VMEM] * 3, [(shape, f32, VMEM)] * 2, 10 * size, 20 * size
    )(radial, local, velocity)


def solution(mesh):
    in_specs = (
        P(None, "axial", "radial", None),
        P(None, "axial", "radial", None),
        P(),
        P("radial"),
    )
    out_specs = (P(None, "axial", "radial", None), P(None, "axial", "radial", None))

    def whole(*args):
        return tuple(shards(*args))

    return jax.shard_map(whole, mesh=mesh, in_specs=in_specs, out_specs=out_specs, check_vma=False)
```

time: 67 us -> 63.5 us (0.948)
  local copies, waits for them, and re-layouts: 4.46 us -> 0.09 us
  Pallas kernels: 4.68 us -> 7.68 us
  waiting for transfers between devices: 26.7 us -> 25.1 us
    unnamed x24 -> x10, local copies, waits for them, and re-layouts: 4.39 us -> 0.02 us
    pallas_call x5 -> x6, Pallas kernels: 4.68 us -> 7.68 us  [the longest x1 2.73 us: shards(): call(filter_kernel, 'filter', [HBM] * 3, [(smooth_shape, f32, HBM), (mess...]
    ppermute x1, waiting for transfers between devices: 4.8 us -> 3.33 us  [shards(): after = lax.ppermute(smooth, 'axial', down)]
  transfers between devices with their start and end apart: 4 -> 4, of which waited for: 4 -> 4; matrix products, arithmetic and copies ran while one was open for 0% -> 0% of each run, Pallas kernels for 1% -> 4%
where the time goes in v2:
time: 63.5 us; the launch traced here: 63.2 us
  starting transfers between devices  29.5 us (46%)
  waiting for transfers between devices  25.1 us (40%)
  Pallas kernels  7.68 us (12%)
  between operations  0.75 us (1%)
    all_to_all x1, starting transfers between devices, shards(): lax.all_to_all(message.reshape(peers, radial_rows, LANES), 'radial', spli...  19 us
    all_to_all x1, waiting for transfers between devices, shards(): lax.all_to_all(message.reshape(peers, radial_rows, LANES), 'radial', spli...  16.8 us
    all_to_all x1, starting transfers between devices, shards(): lax.all_to_all(result.reshape(peers, radial_rows, LANES), 'radial', split...  5.11 us
    ppermute x1, waiting for transfers between devices, shards(): before = lax.ppermute(smooth, 'axial', up)  3.84 us
    ppermute x1, starting transfers between devices, shards(): after = lax.ppermute(smooth, 'axial', down)  3.47 us
    ppermute x1, waiting for transfers between devices, shards(): after = lax.ppermute(smooth, 'axial', down)  3.33 us
    pallas_call x1, Pallas kernels, shards(): call(filter_kernel, 'filter', [HBM] * 3, [(smooth_shape, f32, HBM), (mess...  2.73 us
    pallas_call x1, Pallas kernels, shards(): call(theta_kernel, 'theta', [VMEM, HBM], [(shape, f32, VMEM)] * 2, 12 * s...  2.24 us
  transfers between devices with their start and end apart: 4, of which 4 were waited for; matrix products, arithmetic and copies ran while one was open for 0% of the time, Pallas kernels for 4%

profile of v2, /device:TPU:8, one launch (start us, length us, event | category | flops | bytes accessed | tf_op | source)
XLA Modules:
  0.0 63.2 jit_solution(17691065807924606927)
XLA Ops:
  0.6 0.0 copy-start.1
  0.6 2.7 %filter.1 = (f32[4,3,4,8,128]{4,3,2,1,0:T(8,128)}, f32[4,4,4,8,128]{4,3,2,1,0:T(8,128)}) custom-call(f32[3,4,8,512]{3,2,1,0:T(8,128)} %velocity_ref.3, bf16[2,512,256]{2,1,0:T(8,128)(2,1)} %constant.6.clone.high_hbm, bf16[2,512,256]{2,1,0:T(8,128)(2,1)} %constant.7.clone.low_hbm), custom_call_target="tpu_custom_call" | custom-call | flops 150994944 | bytes 983040 | tf_op jit(solution)/shard_map/filter/pallas_call | solution.py:265
  3.4 19.0 %all-to-all-start = ((f32[64,8,128]{2,1,0:T(8,128)}), f32[64,8,128]{2,1,0:T(8,128)S(1)}, u32[]{:S(2)}, u32[]{:S(2)}) async-start(f32[64,8,128]{2,1,0:T(8,128)} %bitcast.5), calls=%async_computation | async-start | bytes 524288 | tf_op jit(solution)/shard_map/all_to_all | solution.py:282
  22.4 0.0 copy-done.1
  22.4 0.0 copy-start.3
  22.4 0.0 copy-start
  22.4 0.1 split.1.split_ref
  22.6 16.8 %all-to-all-done = f32[64,8,128]{2,1,0:T(8,128)S(1)} async-done(((f32[64,8,128]{2,1,0:T(8,128)}), f32[64,8,128]{2,1,0:T(8,128)S(1)}, u32[]{:S(2)}, u32[]{:S(2)}) %all-to-all-start) | async-done | bytes 262176 | tf_op jit(solution)/shard_map/all_to_all | solution.py:282
  39.3 0.0 copy-start.4
  39.3 0.0 copy-start.2
  39.3 1.5 %radial.1 = f32[512,128]{1,0:T(8,128)} custom-call(f32[512,128]{1,0:T(8,128)S(1)} %bitcast.3, bf16[2,512,512]{2,1,0:T(8,128)(2,1)S(1)} %split.1.split_ref), custom_call_target="tpu_custom_call" | custom-call | flops 402653184 | bytes 1572864 | tf_op jit(solution)/shard_map/radial/pallas_call | solution.py:311
  40.9 5.1 %all-to-all-start.1 = ((f32[64,8,128]{2,1,0:T(8,128)}), f32[64,8,128]{2,1,0:T(8,128)S(1)}, u32[]{:S(2)}, u32[]{:S(2)}) async-start(f32[64,8,128]{2,1,0:T(8,128)} %bitcast.4), calls=%async_computation.1 | async-start | bytes 524288 | tf_op jit(solution)/shard_map/all_to_all | solution.py:320
  46.0 0.0 copy-done.3
  46.0 3.5 %collective-permute-start.1 = (f32[4,3,4,8,128]{4,3,2,1,0:T(8,128)S(1)}, f32[4,3,4,8,128]{4,3,2,1,0:T(8,128)S(1)}, u32[]{:S(2)}, u32[]{:S(2)}) collective-permute-start(f32[4,3,4,8,128]{4,3,2,1,0:T(8,128)S(1)} %copy-done.3), channel_id=1, source_target_pairs={{1,0},{2,1},{3,2},{4,3},{5,4},{6,5},{7,6},{0,7},{9,8},{10,9},{11,1... | collective-permute-start | bytes 589832 | tf_op jit(solution)/shard_map/ppermute | solution.py:290
  49.5 1.9 %collective-permute-start = (f32[4,3,4,8,128]{4,3,2,1,0:T(8,128)S(1)}, f32[4,3,4,8,128]{4,3,2,1,0:T(8,128)S(1)}, u32[]{:S(2)}, u32[]{:S(2)}) collective-permute-start(f32[4,3,4,8,128]{4,3,2,1,0:T(8,128)S(1)} %copy-done.3), channel_id=1, source_target_pairs={{0,1},{1,2},{2,3},{3,4},{4,5},{5,6},{6,7},{7,0},{8,9},{9,10},{10,1... | collective-permute-start | bytes 589832 | tf_op jit(solution)/shard_map/ppermute | solution.py:289
  51.4 0.0 copy-done
  51.4 2.2 %theta.1 = (f32[3,4,8,512]{3,2,1,0:T(8,128)S(1)}, f32[3,4,8,512]{3,2,1,0:T(8,128)S(1)}) custom-call(f32[3,4,8,512]{3,2,1,0:T(8,128)S(1)} %copy-done, bf16[2,512,1024]{2,1,0:T(8,128)(2,1)} %constant.8.clone.table_hbm), custom_call_target="tpu_custom_call" | custom-call | flops 301989888 | bytes 1179648 | tf_op jit(solution)/shard_map/theta/pallas_call | solution.py:291
  53.6 3.3 %collective-permute-done.1.after_ref = f32[4,3,4,8,128]{4,3,2,1,0:T(8,128)S(1)} collective-permute-done((f32[4,3,4,8,128]{4,3,2,1,0:T(8,128)S(1)}, f32[4,3,4,8,128]{4,3,2,1,0:T(8,128)S(1)}, u32[]{:S(2)}, u32[]{:S(2)}) %collective-permute-start.1) | collective-permute-done | bytes 196640 | tf_op jit(solution)/shard_map/ppermute | solution.py:290
  57.0 3.8 %collective-permute-done.before_ref = f32[4,3,4,8,128]{4,3,2,1,0:T(8,128)S(1)} collective-permute-done((f32[4,3,4,8,128]{4,3,2,1,0:T(8,128)S(1)}, f32[4,3,4,8,128]{4,3,2,1,0:T(8,128)S(1)}, u32[]{:S(2)}, u32[]{:S(2)}) %collective-permute-start) | collective-permute-done | bytes 196640 | tf_op jit(solution)/shard_map/ppermute | solution.py:289
  60.8 0.0 copy-done.4
  60.8 0.1 broadcast_in_dim.2.ratio_ref
  60.9 0.0 copy-done.2
  60.9 0.2 local.1.local_ref
  61.1 1.2 %all-to-all-done.1.radial_ref = f32[64,8,128]{2,1,0:T(8,128)S(1)} async-done(((f32[64,8,128]{2,1,0:T(8,128)}), f32[64,8,128]{2,1,0:T(8,128)S(1)}, u32[]{:S(2)}, u32[]{:S(2)}) %all-to-all-start.1) | async-done | bytes 262176 | tf_op jit(solution)/shard_map/all_to_all | solution.py:320
  62.3 0.9 %final.1 = (f32[3,4,8,512]{3,2,1,0:T(8,128)}, f32[3,4,8,512]{3,2,1,0:T(8,128)}) custom-call(f32[64,8,128]{2,1,0:T(8,128)S(1)} %all-to-all-done.1.radial_ref, f32[3,4,8,512]{3,2,1,0:T(8,128)S(1)} %local.1.local_ref, f32[3,4,8,512]{3,2,1,0:T(8,128)S(1)} %copy-done), custom_call_target="tpu_custom_call" | custom-call | flops 491520 | bytes 983040 | tf_op jit(solution)/shard_map/final/pallas_call | solution.py:327
Async XLA Ops:
  0.6 21.8 %copy-start.1 = (f32[512,512]{1,0:T(8,128)S(1)}, f32[512,512]{1,0:T(8,128)}, u32[]{:S(2)}) copy-start(f32[512,512]{1,0:T(8,128)} %matrix_ref.1) | copy-start | bytes 3145732
  3.4 36.0 %all-to-all-start = ((f32[64,8,128]{2,1,0:T(8,128)}), f32[64,8,128]{2,1,0:T(8,128)S(1)}, u32[]{:S(2)}, u32[]{:S(2)}) async-start(f32[64,8,128]{2,1,0:T(8,128)} %bitcast.5), calls=%async_computation | async-start | bytes 524288 | tf_op jit(solution)/shard_map/all_to_all | solution.py:282
  22.4 23.6 %copy-start.3 = (f32[4,3,4,8,128]{4,3,2,1,0:T(8,128)S(1)}, f32[4,3,4,8,128]{4,3,2,1,0:T(8,128)}, u32[]{:S(2)}) copy-start(f32[4,3,4,8,128]{4,3,2,1,0:T(8,128)} %get-tuple-element.7.smooth_ref) | copy-start | bytes 589828
  22.4 29.0 %copy-start = (f32[3,4,8,512]{3,2,1,0:T(8,128)S(1)}, f32[3,4,8,512]{3,2,1,0:T(8,128)}, u32[]{:S(2)}) copy-start(f32[3,4,8,512]{3,2,1,0:T(8,128)} %velocity_ref.3) | copy-start | bytes 589828
  39.3 21.5 %copy-start.4 = (f32[8]{0:T(128)S(1)}, f32[8]{0:T(128)}, u32[]{:S(2)}) copy-start(f32[8]{0:T(128)} %param.10) | copy-start | bytes 100
  39.3 21.6 %copy-start.2 = (f32[3,4,8,512]{3,2,1,0:T(8,128)S(1)}, f32[3,4,8,512]{3,2,1,0:T(8,128)}, u32[]{:S(2)}) copy-start(f32[3,4,8,512]{3,2,1,0:T(8,128)} %previous_ref.1) | copy-start | bytes 589828
  40.9 21.5 %all-to-all-start.1 = ((f32[64,8,128]{2,1,0:T(8,128)}), f32[64,8,128]{2,1,0:T(8,128)S(1)}, u32[]{:S(2)}, u32[]{:S(2)}) async-start(f32[64,8,128]{2,1,0:T(8,128)} %bitcast.4), calls=%async_computation.1 | async-start | bytes 524288 | tf_op jit(solution)/shard_map/all_to_all | solution.py:320
  46.0 11.0 %collective-permute-start.1 = (f32[4,3,4,8,128]{4,3,2,1,0:T(8,128)S(1)}, f32[4,3,4,8,128]{4,3,2,1,0:T(8,128)S(1)}, u32[]{:S(2)}, u32[]{:S(2)}) collective-permute-start(f32[4,3,4,8,128]{4,3,2,1,0:T(8,128)S(1)} %copy-done.3), channel_id=1, source_target_pairs={{1,0},{2,1},{3,2},{4,3},{5,4},{6,5},{7,6},{0,7},{9,8},{10,9},{11,1... | collective-permute-start | bytes 589832 | tf_op jit(solution)/shard_map/ppermute | solution.py:290
  49.5 11.4 %collective-permute-start = (f32[4,3,4,8,128]{4,3,2,1,0:T(8,128)S(1)}, f32[4,3,4,8,128]{4,3,2,1,0:T(8,128)S(1)}, u32[]{:S(2)}, u32[]{:S(2)}) collective-permute-start(f32[4,3,4,8,128]{4,3,2,1,0:T(8,128)S(1)} %copy-done.3), channel_id=1, source_target_pairs={{0,1},{1,2},{2,3},{3,4},{4,5},{5,6},{6,7},{7,0},{8,9},{9,10},{10,1... | collective-permute-start | bytes 589832 | tf_op jit(solution)/shard_map/ppermute | solution.py:289

commit v3 on v2

--- a/solution.py
+++ b/solution.py
@@ -48,9 +48,24 @@
     return keep[shift], slope[shift], curve[shift]
 
 
+def even_odd(matrix):
+    half = matrix.shape[0] // 2
+    same, cross = matrix[:half, :half], matrix[:half, half:]
+    return (same + cross) / 2, (same - cross) / 2
+
+
 def product(left, right):
+    rows = left[0].shape[0]
     dot = functools.partial(jnp.dot, preferred_element_type=jnp.float32)
-    return dot(left[0], right[0]) + (dot(left[0], right[1]) + dot(left[1], right[0]))
+    large = dot(jnp.concatenate(left, axis=0), right[0])
+    return large[:rows] + (large[rows:] + dot(left[0], right[1]))
+
+
+def sum_and_difference(velocity):
+    components, planes, rows, points = velocity.shape
+    lines = velocity.reshape(components * planes * rows, points)
+    first, second = lines[:, : points // 2], lines[:, points // 2 :]
+    return halves(first + second), halves(first - second)
 
 
 def lane_groups(shape):
@@ -59,45 +74,37 @@
 
 def filter_kernel(
     velocity_hbm,
-    high_hbm,
-    low_hbm,
+    table_hbm,
     smooth_hbm,
     message_hbm,
     velocity_ref,
-    high_ref,
-    low_ref,
+    table_ref,
     smooth_ref,
     message_ref,
     in_sems,
     out_sems,
 ):
-    sections, points, width = high_ref.shape
-    components, planes, rows, _ = velocity_ref.shape
+    components, planes, rows, points = velocity_ref.shape
     incoming = [pltpu.make_async_copy(velocity_hbm, velocity_ref, in_sems.at[0])]
-    for section in range(sections):
-        for source, target in ((high_hbm, high_ref), (low_hbm, low_ref)):
-            incoming.append(
-                pltpu.make_async_copy(
-                    source.at[section], target.at[section], in_sems.at[len(incoming)]
-                )
-            )
+    for part in range(2):
+        incoming.append(
+            pltpu.make_async_copy(table_hbm.at[part], table_ref.at[part], in_sems.at[1 + part])
+        )
     for copy in incoming:
         copy.start()
     incoming[0].wait()
-    lines = components * planes * rows
-    high, low = halves(velocity_ref[...].reshape(lines, points))
-    both = jnp.concatenate([high, low], axis=0)
+    total, gap = sum_and_difference(velocity_ref[...])
+    incoming[1].wait()
+    even = product(total, (table_ref[0, 0], table_ref[0, 1]))
+    incoming[2].wait()
+    odd = product(gap, (table_ref[1, 0], table_ref[1, 1]))
     groups = lane_groups((planes, rows, LANES))
     outgoing = []
-    for section in range(sections):
-        incoming[1 + 2 * section].wait()
-        large = jnp.dot(both, high_ref[section], preferred_element_type=jnp.float32)
-        incoming[2 + 2 * section].wait()
-        small = jnp.dot(high, low_ref[section], preferred_element_type=jnp.float32)
-        smooth = large[:lines] + (large[lines:] + small)
-        smooth = smooth.reshape(components, planes, rows, width)
-        for local in range(width // LANES):
-            block = section * (width // LANES) + local
+    blocks = points // LANES
+    for section, smooth in enumerate((even + odd, even - odd)):
+        smooth = smooth.reshape(components, planes, rows, points // 2)
+        for local in range(blocks // 2):
+            block = section * (blocks // 2) + local
             tile = smooth[:, :, :, local * LANES : (local + 1) * LANES]
             smooth_ref[block] = tile
             turned = [tile[0]] + [pltpu.roll(tile[c], c * GROUP, 2) for c in range(1, components)]
@@ -106,7 +113,7 @@
                 for c in range(components):
                     chosen = jnp.where(groups == (part + c) % GROUPS, turned[c], chosen)
                 message_ref[block, part] = chosen
-        here = pl.ds(section * (width // LANES), width // LANES)
+        here = pl.ds(section * (blocks // 2), blocks // 2)
         for source, target in ((message_ref, message_hbm), (smooth_ref, smooth_hbm)):
             copy = pltpu.make_async_copy(
                 source.at[here], target.at[here], out_sems.at[len(outgoing)]
@@ -120,43 +127,51 @@
 def theta_kernel(velocity_ref, table_hbm, slope_ref, curve_ref, table_ref, sem):
     copy = pltpu.make_async_copy(table_hbm, table_ref, sem)
     copy.start()
-    components, planes, rows, points = velocity_ref.shape
-    velocity = halves(velocity_ref[...].reshape(components * planes * rows, points))
+    total, gap = sum_and_difference(velocity_ref[...])
     copy.wait()
-    both = product(velocity, (table_ref[0], table_ref[1]))
-    slope_ref[...] = both[:, :points].reshape(velocity_ref.shape)
-    curve_ref[...] = both[:, points:].reshape(velocity_ref.shape)
-
-
-def split_kernel(matrix_ref, split_ref):
-    split_ref[0], split_ref[1] = halves(matrix_ref[...])
-
-
-def wide_product(split_ref, rows, right):
-    high, low = halves(right)
-    both = jnp.concatenate([high, low], axis=1)
-    large = jnp.dot(split_ref[0, rows], both, preferred_element_type=jnp.float32)
-    small = jnp.dot(split_ref[1, rows], high, preferred_element_type=jnp.float32)
-    return large[:, :LANES] + (large[:, LANES:] + small)
+    even = product(total, (table_ref[0, 0], table_ref[0, 1]))
+    odd = product(gap, (table_ref[1, 0], table_ref[1, 1]))
+    half = even.shape[1] // 2
+    shape = velocity_ref.shape[:3] + (half,)
+    for index, result_ref in enumerate((slope_ref, curve_ref)):
+        columns = slice(index * half, (index + 1) * half)
+        result_ref[..., :half] = (even[:, columns] + odd[:, columns]).reshape(shape)
+        result_ref[..., half:] = (even[:, columns] - odd[:, columns]).reshape(shape)
+
+
+def matrix_kernel(matrix_ref, split_ref):
+    matrix = matrix_ref[...]
+    once = halves(matrix)
+    twice = halves(product(once, once))
+    _, pieces, rows, _ = split_ref.shape
+    rows //= 2
+    for piece in range(pieces):
+        here = slice(piece * rows, (piece + 1) * rows)
+        for half in range(2):
+            split_ref[half, piece, :rows] = once[half][here]
+            split_ref[half, piece, rows:] = twice[half][here]
 
 
 def radial_kernel(planes, pencil_ref, split_ref, result_hbm, result_ref, sems):
     part = lax.rem(lax.div(lax.axis_index("radial"), planes), GROUPS)
     pencil = pencil_ref[...]
-    full = pencil.shape[0]
-    once = wide_product(split_ref, slice(None), pencil)
+    high, low = halves(pencil)
+    both = jnp.concatenate([high, low], axis=1)
     groups = lane_groups(pencil.shape)
     place = lax.rem(groups - part + GROUPS, GROUPS)
     speed = jnp.where(place == 0, pencil, jnp.zeros_like(pencil))
     speed = jnp.where(place == 1, pltpu.roll(pencil, GROUP, 1), speed)
     speed = jnp.where(place == 2, pltpu.roll(pencil, 2 * GROUP, 1), speed)
-    pieces = sems.shape[0]
+    _, pieces, rows, _ = split_ref.shape
+    rows //= 2
     copies = []
     for piece in range(pieces):
-        rows = slice(piece * full // pieces, (piece + 1) * full // pieces)
-        twice = wide_product(split_ref, rows, once)
-        result_ref[rows] = viscosity * twice - speed[rows] * once[rows]
-        here = pl.ds(piece * full // pieces, full // pieces)
+        large = jnp.dot(split_ref[0, piece], both, preferred_element_type=jnp.float32)
+        small = jnp.dot(split_ref[1, piece], high, preferred_element_type=jnp.float32)
+        derivs = large[:, :LANES] + (large[:, LANES:] + small)
+        here = slice(piece * rows, (piece + 1) * rows)
+        result_ref[here] = viscosity * derivs[rows:] - speed[here] * derivs[:rows]
+        here = pl.ds(piece * rows, rows)
         copy = pltpu.make_async_copy(result_ref.at[here], result_hbm.at[here], sems.at[piece])
         copy.start()
         copies.append(copy)
@@ -194,10 +209,20 @@
                 )
 
 
-def final_kernel(radial_ref, local_ref, velocity_ref, velocity_out_ref, rhs_out_ref):
+def final_kernel(
+    radial_ref,
+    local_ref,
+    velocity_ref,
+    velocity_hbm,
+    rhs_hbm,
+    velocity_out_ref,
+    rhs_out_ref,
+    sems,
+):
     components, planes, rows, points = velocity_ref.shape
     blocks = points // LANES
     groups = lane_groups((rows, LANES))
+    copies = []
     for plane in range(planes):
         for block in range(blocks):
             tiles = [
@@ -215,6 +240,15 @@
                 velocity_out_ref[c, plane, :, lanes] = (
                     velocity_ref[c, plane, :, lanes] + (section_weight * timestep) * rhs
                 )
+        here = (slice(None), pl.ds(plane, 1))
+        for source, target in ((rhs_out_ref, rhs_hbm), (velocity_out_ref, velocity_hbm)):
+            copy = pltpu.make_async_copy(
+                source.at[here], target.at[here], sems.at[len(copies)]
+            )
+            copy.start()
+            copies.append(copy)
+    for copy in copies:
+        copy.wait()
 
 
 VMEM = pl.BlockSpec(memory_space=pltpu.VMEM)
@@ -241,44 +275,37 @@
     )
 
 
-def sections_of(matrix, sections):
-    points, width = matrix.shape
-    return np.ascontiguousarray(
-        np.transpose(matrix.reshape(points, sections, width // sections), (1, 0, 2))
-    )
-
-
 def shards(velocity, previous_rhs, radial_deriv, inv_radius):
     components, planes, radial_rows, points = velocity.shape
     peers = lax.axis_size("radial")
     shape = velocity.shape
     size = velocity.size
     blocks = points // LANES
-    sections = 2
     f32, bf16, dma = jnp.float32, jnp.bfloat16, pltpu.SemaphoreType.DMA
-    keep, slope, curve = circulants(KEEP, points)
-    keep_high, keep_low = (sections_of(half, sections) for half in host_halves(keep))
-    theta = np.stack(host_halves(np.concatenate([slope, curve], axis=1)))
+    keep, slope, curve = (even_odd(matrix) for matrix in circulants(KEEP, points))
+    keep = np.stack([np.stack(host_halves(part)) for part in keep])
+    theta = np.stack(
+        [np.stack(host_halves(np.concatenate(pair, axis=1))) for pair in zip(slope, curve)]
+    )
 
     smooth_shape = (blocks, components, planes, radial_rows, LANES)
     message_shape = (blocks, GROUPS, planes, radial_rows, LANES)
     smooth, message = call(
         filter_kernel,
         "filter",
-        [HBM] * 3,
+        [HBM] * 2,
         [(smooth_shape, f32, HBM), (message_shape, f32, HBM)],
         6 * size * points,
         20 * size,
         [
             pltpu.VMEM(shape, f32),
-            pltpu.VMEM(keep_high.shape, bf16),
-            pltpu.VMEM(keep_low.shape, bf16),
+            pltpu.VMEM(keep.shape, bf16),
             pltpu.VMEM(smooth_shape, f32),
             pltpu.VMEM(message_shape, f32),
-            dma((1 + 2 * sections,)),
-            dma((2 * sections,)),
+            dma((3,)),
+            dma((4,)),
         ],
-    )(*(in_hbm(part) for part in (velocity, jnp.asarray(keep_high), jnp.asarray(keep_low))))
+    )(in_hbm(velocity), in_hbm(jnp.asarray(keep)))
     pencil = lax.all_to_all(
         message.reshape(peers, radial_rows, LANES), "radial", split_axis=0, concat_axis=0, tiled=True
     )
@@ -299,15 +326,15 @@
     )(velocity, in_hbm(jnp.asarray(theta)))
 
     full = peers * radial_rows
+    pieces = 4
     (split,) = call(
-        split_kernel,
-        "split",
+        matrix_kernel,
+        "matrix",
         [VMEM],
-        [((2, full, full), bf16, VMEM)],
-        4 * full * full,
-        8 * full * full,
+        [((2, pieces, 2 * full // pieces, full), bf16, VMEM)],
+        6 * full * full * full,
+        12 * full * full,
     )(radial_deriv)
-    pieces = 4
     (result,) = call(
         functools.partial(radial_kernel, planes),
         "radial",
@@ -325,7 +352,13 @@
         local_kernel, "local", [VMEM] * 7, [(shape, f32, VMEM)], 40 * size, 32 * size
     )(smooth, before, after, theta_slope, theta_curve, previous_rhs, ratio)
     return call(
-        final_kernel, "final", [VMEM] * 3, [(shape, f32, VMEM)] * 2, 10 * size, 20 * size
+        final_kernel,
+        "final",
+        [VMEM] * 3,
+        [(shape, f32, HBM)] * 2,
+        10 * size,
+        20 * size,
+        [pltpu.VMEM(shape, f32), pltpu.VMEM(shape, f32), dma((2 * planes,))],
     )(radial, local, velocity)
 
 

time: 63.5 us -> 63.1 us (level)
  waiting for transfers between devices: 25.1 us -> 23.7 us
  local copies, waits for them, and re-layouts: 0.09 us -> 1.31 us
    all_to_all x1, waiting for transfers between devices: 16.8 us -> 14.7 us  [shards(): lax.all_to_all(message.reshape(peers, radial_rows, LANES), 'radial', spli...]
    unnamed x10, local copies, waits for them, and re-layouts: 0.02 us -> 1.24 us
    ppermute x1, waiting for transfers between devices: 3.33 us -> 3.99 us  [shards(): after = lax.ppermute(smooth, 'axial', down)]
    pallas_call x1, Pallas kernels: 2.24 us -> 1.58 us  [shards(): call(theta_kernel, 'theta', [VMEM, HBM], [(shape, f32, VMEM)] * 2, 12 * s...]
where the time goes in v3:
time: 63.1 us; the launch traced here: 62.7 us
  starting transfers between devices  29.5 us (47%)
  waiting for transfers between devices  23.7 us (38%)
  Pallas kernels  7.45 us (12%)
  local copies, waits for them, and re-layouts  1.31 us (2%)
  between operations  0.74 us (1%)
    all_to_all x1, starting transfers between devices, shards(): lax.all_to_all(message.reshape(peers, radial_rows, LANES), 'radial', spli...  19 us
    all_to_all x1, waiting for transfers between devices, shards(): lax.all_to_all(message.reshape(peers, radial_rows, LANES), 'radial', spli...  14.7 us
    all_to_all x1, starting transfers between devices, shards(): lax.all_to_all(result.reshape(peers, radial_rows, LANES), 'radial', split...  5.1 us
    ppermute x1, waiting for transfers between devices, shards(): after = lax.ppermute(smooth, 'axial', down)  3.99 us
    ppermute x1, waiting for transfers between devices, shards(): before = lax.ppermute(smooth, 'axial', up)  3.84 us
    ppermute x1, starting transfers between devices, shards(): after = lax.ppermute(smooth, 'axial', down)  3.48 us
    pallas_call x1, Pallas kernels, shards(): call(filter_kernel, 'filter', [HBM] * 2, [(smooth_shape, f32, HBM), (mess...  2.41 us
    ppermute x1, starting transfers between devices, shards(): before = lax.ppermute(smooth, 'axial', up)  1.92 us
  transfers between devices with their start and end apart: 4, of which 4 were waited for; matrix products, arithmetic and copies ran while one was open for 0% of the time, Pallas kernels for 4%

profile of v3, /device:TPU:8, one launch (start us, length us, event | category | flops | bytes accessed | tf_op | source)
XLA Modules:
  0.0 62.7 jit_solution(2915805733147770892)
XLA Ops:
  0.6 2.4 %filter.1 = (f32[4,3,4,8,128]{4,3,2,1,0:T(8,128)}, f32[4,4,4,8,128]{4,3,2,1,0:T(8,128)}) custom-call(f32[3,4,8,512]{3,2,1,0:T(8,128)} %velocity_ref.3, bf16[2,2,256,256]{3,2,1,0:T(8,128)(2,1)} %constant.4.clone.table_hbm), custom_call_target="tpu_custom_call" | custom-call | flops 150994944 | bytes 983040 | tf_op jit(solution)/shard_map/filter/pallas_call | solution.py:293
  3.0 19.0 %all-to-all-start = ((f32[64,8,128]{2,1,0:T(8,128)}), f32[64,8,128]{2,1,0:T(8,128)S(1)}, u32[]{:S(2)}, u32[]{:S(2)}) async-start(f32[64,8,128]{2,1,0:T(8,128)} %bitcast.5), calls=%async_computation | async-start | bytes 524288 | tf_op jit(solution)/shard_map/all_to_all | solution.py:309
  22.1 0.0 copy-start.1
  22.1 1.2 %copy-done.1 = f32[512,512]{1,0:T(8,128)S(1)} copy-done((f32[512,512]{1,0:T(8,128)S(1)}, f32[512,512]{1,0:T(8,128)}, u32[]{:S(2)}) %copy-start.1) | copy-done | bytes 1048600
  23.3 1.0 %matrix.1.split_ref = bf16[2,4,256,512]{3,2,1,0:T(8,128)(2,1)S(1)} custom-call(f32[512,512]{1,0:T(8,128)S(1)} %copy-done.1), custom_call_target="tpu_custom_call" | custom-call | flops 805306368 | bytes 3145728 | tf_op jit(solution)/shard_map/matrix/pallas_call | solution.py:330
  24.3 0.0 copy-start.3
  24.3 0.0 copy-start
  24.3 14.7 %all-to-all-done = f32[64,8,128]{2,1,0:T(8,128)S(1)} async-done(((f32[64,8,128]{2,1,0:T(8,128)}), f32[64,8,128]{2,1,0:T(8,128)S(1)}, u32[]{:S(2)}, u32[]{:S(2)}) %all-to-all-start) | async-done | bytes 262176 | tf_op jit(solution)/shard_map/all_to_all | solution.py:309
  39.0 0.0 copy-start.4
  39.0 0.0 copy-start.2
  39.0 1.4 %radial.1 = f32[512,128]{1,0:T(8,128)} custom-call(f32[512,128]{1,0:T(8,128)S(1)} %bitcast.3, bf16[2,4,256,512]{3,2,1,0:T(8,128)(2,1)S(1)} %matrix.1.split_ref), custom_call_target="tpu_custom_call" | custom-call | flops 402653184 | bytes 1572864 | tf_op jit(solution)/shard_map/radial/pallas_call | solution.py:338
  40.4 5.1 %all-to-all-start.1 = ((f32[64,8,128]{2,1,0:T(8,128)}), f32[64,8,128]{2,1,0:T(8,128)S(1)}, u32[]{:S(2)}, u32[]{:S(2)}) async-start(f32[64,8,128]{2,1,0:T(8,128)} %bitcast.4), calls=%async_computation.1 | async-start | bytes 524288 | tf_op jit(solution)/shard_map/all_to_all | solution.py:347
  45.5 0.0 copy-done.3
  45.5 3.5 %collective-permute-start.1 = (f32[4,3,4,8,128]{4,3,2,1,0:T(8,128)S(1)}, f32[4,3,4,8,128]{4,3,2,1,0:T(8,128)S(1)}, u32[]{:S(2)}, u32[]{:S(2)}) collective-permute-start(f32[4,3,4,8,128]{4,3,2,1,0:T(8,128)S(1)} %copy-done.3), channel_id=1, source_target_pairs={{1,0},{2,1},{3,2},{4,3},{5,4},{6,5},{7,6},{0,7},{9,8},{10,9},{11,1... | collective-permute-start | bytes 589832 | tf_op jit(solution)/shard_map/ppermute | solution.py:317
  49.0 1.9 %collective-permute-start = (f32[4,3,4,8,128]{4,3,2,1,0:T(8,128)S(1)}, f32[4,3,4,8,128]{4,3,2,1,0:T(8,128)S(1)}, u32[]{:S(2)}, u32[]{:S(2)}) collective-permute-start(f32[4,3,4,8,128]{4,3,2,1,0:T(8,128)S(1)} %copy-done.3), channel_id=1, source_target_pairs={{0,1},{1,2},{2,3},{3,4},{4,5},{5,6},{6,7},{7,0},{8,9},{9,10},{10,1... | collective-permute-start | bytes 589832 | tf_op jit(solution)/shard_map/ppermute | solution.py:316
  50.9 0.0 copy-done
  50.9 1.6 %theta.1 = (f32[3,4,8,512]{3,2,1,0:T(8,128)S(1)}, f32[3,4,8,512]{3,2,1,0:T(8,128)S(1)}) custom-call(f32[3,4,8,512]{3,2,1,0:T(8,128)S(1)} %copy-done, bf16[2,2,256,512]{3,2,1,0:T(8,128)(2,1)} %constant.5.clone.table_hbm), custom_call_target="tpu_custom_call" | custom-call | flops 301989888 | bytes 1179648 | tf_op jit(solution)/shard_map/theta/pallas_call | solution.py:318
  52.5 4.0 %collective-permute-done.1.after_ref = f32[4,3,4,8,128]{4,3,2,1,0:T(8,128)S(1)} collective-permute-done((f32[4,3,4,8,128]{4,3,2,1,0:T(8,128)S(1)}, f32[4,3,4,8,128]{4,3,2,1,0:T(8,128)S(1)}, u32[]{:S(2)}, u32[]{:S(2)}) %collective-permute-start.1) | collective-permute-done | bytes 196640 | tf_op jit(solution)/shard_map/ppermute | solution.py:317
  56.5 3.8 %collective-permute-done.before_ref = f32[4,3,4,8,128]{4,3,2,1,0:T(8,128)S(1)} collective-permute-done((f32[4,3,4,8,128]{4,3,2,1,0:T(8,128)S(1)}, f32[4,3,4,8,128]{4,3,2,1,0:T(8,128)S(1)}, u32[]{:S(2)}, u32[]{:S(2)}) %collective-permute-start) | collective-permute-done | bytes 196640 | tf_op jit(solution)/shard_map/ppermute | solution.py:316
  60.3 0.0 copy-done.4
  60.3 0.1 broadcast_in_dim.2.ratio_ref
  60.4 0.0 copy-done.2
  60.4 0.2 local.1.local_ref
  60.6 1.2 %all-to-all-done.1.radial_ref = f32[64,8,128]{2,1,0:T(8,128)S(1)} async-done(((f32[64,8,128]{2,1,0:T(8,128)}), f32[64,8,128]{2,1,0:T(8,128)S(1)}, u32[]{:S(2)}, u32[]{:S(2)}) %all-to-all-start.1) | async-done | bytes 262176 | tf_op jit(solution)/shard_map/all_to_all | solution.py:347
  61.9 0.9 %final.1 = (f32[3,4,8,512]{3,2,1,0:T(8,128)}, f32[3,4,8,512]{3,2,1,0:T(8,128)}) custom-call(f32[64,8,128]{2,1,0:T(8,128)S(1)} %all-to-all-done.1.radial_ref, f32[3,4,8,512]{3,2,1,0:T(8,128)S(1)} %local.1.local_ref, f32[3,4,8,512]{3,2,1,0:T(8,128)S(1)} %copy-done), custom_call_target="tpu_custom_call" | custom-call | flops 491520 | bytes 983040 | tf_op jit(solution)/shard_map/final/pallas_call | solution.py:354
Async XLA Ops:
  3.0 36.0 %all-to-all-start = ((f32[64,8,128]{2,1,0:T(8,128)}), f32[64,8,128]{2,1,0:T(8,128)S(1)}, u32[]{:S(2)}, u32[]{:S(2)}) async-start(f32[64,8,128]{2,1,0:T(8,128)} %bitcast.5), calls=%async_computation | async-start | bytes 524288 | tf_op jit(solution)/shard_map/all_to_all | solution.py:309
  22.1 1.2 %copy-start.1 = (f32[512,512]{1,0:T(8,128)S(1)}, f32[512,512]{1,0:T(8,128)}, u32[]{:S(2)}) copy-start(f32[512,512]{1,0:T(8,128)} %matrix_ref.1) | copy-start | bytes 3145732
  24.3 21.2 %copy-start.3 = (f32[4,3,4,8,128]{4,3,2,1,0:T(8,128)S(1)}, f32[4,3,4,8,128]{4,3,2,1,0:T(8,128)}, u32[]{:S(2)}) copy-start(f32[4,3,4,8,128]{4,3,2,1,0:T(8,128)} %get-tuple-element.7.smooth_ref) | copy-start | bytes 589828
  24.3 26.6 %copy-start = (f32[3,4,8,512]{3,2,1,0:T(8,128)S(1)}, f32[3,4,8,512]{3,2,1,0:T(8,128)}, u32[]{:S(2)}) copy-start(f32[3,4,8,512]{3,2,1,0:T(8,128)} %velocity_ref.3) | copy-start | bytes 589828
  39.0 21.3 %copy-start.4 = (f32[8]{0:T(128)S(1)}, f32[8]{0:T(128)}, u32[]{:S(2)}) copy-start(f32[8]{0:T(128)} %param.9) | copy-start | bytes 100
  39.0 21.4 %copy-start.2 = (f32[3,4,8,512]{3,2,1,0:T(8,128)S(1)}, f32[3,4,8,512]{3,2,1,0:T(8,128)}, u32[]{:S(2)}) copy-start(f32[3,4,8,512]{3,2,1,0:T(8,128)} %previous_ref.1) | copy-start | bytes 589828
  40.4 21.5 %all-to-all-start.1 = ((f32[64,8,128]{2,1,0:T(8,128)}), f32[64,8,128]{2,1,0:T(8,128)S(1)}, u32[]{:S(2)}, u32[]{:S(2)}) async-start(f32[64,8,128]{2,1,0:T(8,128)} %bitcast.4), calls=%async_computation.1 | async-start | bytes 524288 | tf_op jit(solution)/shard_map/all_to_all | solution.py:347
  45.5 11.0 %collective-permute-start.1 = (f32[4,3,4,8,128]{4,3,2,1,0:T(8,128)S(1)}, f32[4,3,4,8,128]{4,3,2,1,0:T(8,128)S(1)}, u32[]{:S(2)}, u32[]{:S(2)}) collective-permute-start(f32[4,3,4,8,128]{4,3,2,1,0:T(8,128)S(1)} %copy-done.3), channel_id=1, source_target_pairs={{1,0},{2,1},{3,2},{4,3},{5,4},{6,5},{7,6},{0,7},{9,8},{10,9},{11,1... | collective-permute-start | bytes 589832 | tf_op jit(solution)/shard_map/ppermute | solution.py:317
  49.0 11.4 %collective-permute-start = (f32[4,3,4,8,128]{4,3,2,1,0:T(8,128)S(1)}, f32[4,3,4,8,128]{4,3,2,1,0:T(8,128)S(1)}, u32[]{:S(2)}, u32[]{:S(2)}) collective-permute-start(f32[4,3,4,8,128]{4,3,2,1,0:T(8,128)S(1)} %copy-done.3), channel_id=1, source_target_pairs={{0,1},{1,2},{2,3},{3,4},{4,5},{5,6},{6,7},{7,0},{8,9},{9,10},{10,1... | collective-permute-start | bytes 589832 | tf_op jit(solution)/shard_map/ppermute | solution.py:316

commit v4 on v3

--- a/solution.py
+++ b/solution.py
@@ -14,6 +14,7 @@
 LANES = 128
 GROUP = 32
 GROUPS = LANES // GROUP
+FIRST = 52
 
 first_coefs = (4.0 / 5.0, -1.0 / 5.0, 4.0 / 105.0, -1.0 / 280.0)
 second_coefs = (8.0 / 5.0, -1.0 / 5.0, 8.0 / 315.0, -1.0 / 560.0)
@@ -139,8 +140,8 @@
         result_ref[..., half:] = (even[:, columns] - odd[:, columns]).reshape(shape)
 
 
-def matrix_kernel(matrix_ref, split_ref):
-    matrix = matrix_ref[...]
+def matrix_kernel(turn, matrix_ref, split_ref):
+    matrix = pltpu.roll(pltpu.roll(matrix_ref[...], turn, 0), turn, 1)
     once = halves(matrix)
     twice = halves(product(once, once))
     _, pieces, rows, _ = split_ref.shape
@@ -152,8 +153,9 @@
             split_ref[half, piece, rows:] = twice[half][here]
 
 
-def radial_kernel(planes, pencil_ref, split_ref, result_hbm, result_ref, sems):
-    part = lax.rem(lax.div(lax.axis_index("radial"), planes), GROUPS)
+def radial_kernel(planes, first, peers, pencil_ref, split_ref, result_hbm, result_ref, sems):
+    position = lax.rem(lax.axis_index("radial") + (peers - first), peers)
+    part = lax.rem(lax.div(position, planes), GROUPS)
     pencil = pencil_ref[...]
     high, low = halves(pencil)
     both = jnp.concatenate([high, low], axis=1)
@@ -306,9 +308,16 @@
             dma((4,)),
         ],
     )(in_hbm(velocity), in_hbm(jnp.asarray(keep)))
-    pencil = lax.all_to_all(
-        message.reshape(peers, radial_rows, LANES), "radial", split_axis=0, concat_axis=0, tiled=True
+    first = FIRST % peers
+    exchange = functools.partial(
+        lax.all_to_all,
+        axis_name="radial",
+        split_axis=0,
+        concat_axis=0,
+        tiled=True,
+        axis_index_groups=[[(first + i) % peers for i in range(peers)]],
     )
+    pencil = exchange(message.reshape(peers, radial_rows, LANES))
 
     ring = lax.axis_size("axial")
     up = [(i, (i + 1) % ring) for i in range(ring)]
@@ -328,7 +337,7 @@
     full = peers * radial_rows
     pieces = 4
     (split,) = call(
-        matrix_kernel,
+        functools.partial(matrix_kernel, (peers - first) * radial_rows % full),
         "matrix",
         [VMEM],
         [((2, pieces, 2 * full // pieces, full), bf16, VMEM)],
@@ -336,7 +345,7 @@
         12 * full * full,
     )(radial_deriv)
     (result,) = call(
-        functools.partial(radial_kernel, planes),
+        functools.partial(radial_kernel, planes, first, peers),
         "radial",
         [VMEM] * 2,
         [((full, LANES), f32, HBM)],
@@ -344,9 +353,7 @@
         4 * full * (full + 2 * LANES),
         [pltpu.VMEM((full, LANES), f32), dma((pieces,))],
     )(in_vmem(pencil.reshape(full, LANES)), split)
-    radial = lax.all_to_all(
-        result.reshape(peers, radial_rows, LANES), "radial", split_axis=0, concat_axis=0, tiled=True
-    )
+    radial = exchange(result.reshape(peers, radial_rows, LANES))
     ratio = jnp.broadcast_to(inv_radius[:, None], (radial_rows, LANES))
     (local,) = call(
         local_kernel, "local", [VMEM] * 7, [(shape, f32, VMEM)], 40 * size, 32 * size

time: 63.1 us -> 60.6 us (0.960)
  waiting for transfers between devices: 23.7 us -> 10.3 us
  starting transfers between devices: 29.5 us -> 40.2 us
    all_to_all x2, waiting for transfers between devices: 15.9 us -> 5.05 us  [the longest x1 5.05 us: shards(): pencil = exchange(message.reshape(peers, radial_rows, LANES))]
    all_to_all x2, starting transfers between devices: 24.1 us -> 34.6 us  [the longest x1 19.8 us: shards(): pencil = exchange(message.reshape(peers, radial_rows, LANES))]
    ppermute x1, waiting for transfers between devices: 3.99 us -> 2.07 us  [shards(): after = lax.ppermute(smooth, 'axial', down)]
    ppermute x1, waiting for transfers between devices: 3.84 us -> 3.19 us  [shards(): before = lax.ppermute(smooth, 'axial', up)]
  transfers between devices with their start and end apart: 4 -> 4, of which waited for: 4 -> 3; matrix products, arithmetic and copies ran while one was open for 0% -> 0% of each run, Pallas kernels for 4% -> 5%
where the time goes in v4:
time: 60.6 us; the launch traced here: 60.2 us
  starting transfers between devices  40.2 us (66%)
  waiting for transfers between devices  10.3 us (17%)
  Pallas kernels  7.62 us (13%)
  local copies, waits for them, and re-layouts  1.31 us (2%)
  between operations  0.75 us (1%)
    all_to_all x1, starting transfers between devices, shards(): pencil = exchange(message.reshape(peers, radial_rows, LANES))  19.8 us
    all_to_all x1, starting transfers between devices, shards(): radial = exchange(result.reshape(peers, radial_rows, LANES))  14.8 us
    all_to_all x1, waiting for transfers between devices, shards(): pencil = exchange(message.reshape(peers, radial_rows, LANES))  5.05 us
    ppermute x1, starting transfers between devices, shards(): after = lax.ppermute(smooth, 'axial', down)  3.66 us
    ppermute x1, waiting for transfers between devices, shards(): before = lax.ppermute(smooth, 'axial', up)  3.19 us
    pallas_call x1, Pallas kernels, shards(): call(filter_kernel, 'filter', [HBM] * 2, [(smooth_shape, f32, HBM), (mess...  2.41 us
    ppermute x1, waiting for transfers between devices, shards(): after = lax.ppermute(smooth, 'axial', down)  2.07 us
    ppermute x1, starting transfers between devices, shards(): before = lax.ppermute(smooth, 'axial', up)  1.92 us
  transfers between devices with their start and end apart: 4, of which 3 were waited for; matrix products, arithmetic and copies ran while one was open for 0% of the time, Pallas kernels for 5%

profile of v4, /device:TPU:8, one launch (start us, length us, event | category | flops | bytes accessed | tf_op | source)
XLA Modules:
  0.0 60.2 jit_solution(10457539064452522135)
XLA Ops:
  0.6 2.4 %filter.1 = (f32[4,3,4,8,128]{4,3,2,1,0:T(8,128)}, f32[4,4,4,8,128]{4,3,2,1,0:T(8,128)}) custom-call(f32[3,4,8,512]{3,2,1,0:T(8,128)} %velocity_ref.3, bf16[2,2,256,256]{3,2,1,0:T(8,128)(2,1)} %constant.4.clone.table_hbm), custom_call_target="tpu_custom_call" | custom-call | flops 150994944 | bytes 983040 | tf_op jit(solution)/shard_map/filter/pallas_call | solution.py:295
  3.0 19.8 %all-to-all-start = ((f32[64,8,128]{2,1,0:T(8,128)}), f32[64,8,128]{2,1,0:T(8,128)S(1)}, u32[]{:S(2)}, u32[]{:S(2)}) async-start(f32[64,8,128]{2,1,0:T(8,128)} %bitcast.5), calls=%async_computation | async-start | bytes 524288 | tf_op jit(solution)/shard_map/all_to_all | solution.py:320
  22.9 0.0 copy-start.1
  22.9 1.2 %copy-done.1 = f32[512,512]{1,0:T(8,128)S(1)} copy-done((f32[512,512]{1,0:T(8,128)S(1)}, f32[512,512]{1,0:T(8,128)}, u32[]{:S(2)}) %copy-start.1) | copy-done | bytes 1048600
  24.1 1.2 %matrix.1.split_ref = bf16[2,4,256,512]{3,2,1,0:T(8,128)(2,1)S(1)} custom-call(f32[512,512]{1,0:T(8,128)S(1)} %copy-done.1), custom_call_target="tpu_custom_call" | custom-call | flops 805306368 | bytes 3145728 | tf_op jit(solution)/shard_map/matrix/pallas_call | solution.py:339
  25.3 0.0 copy-start.3
  25.3 0.0 copy-start
  25.3 5.0 %all-to-all-done = f32[64,8,128]{2,1,0:T(8,128)S(1)} async-done(((f32[64,8,128]{2,1,0:T(8,128)}), f32[64,8,128]{2,1,0:T(8,128)S(1)}, u32[]{:S(2)}, u32[]{:S(2)}) %all-to-all-start) | async-done | bytes 262176 | tf_op jit(solution)/shard_map/all_to_all | solution.py:320
  30.4 0.0 copy-start.4
  30.4 0.0 copy-start.2
  30.4 1.4 %radial.1 = f32[512,128]{1,0:T(8,128)} custom-call(f32[512,128]{1,0:T(8,128)S(1)} %bitcast.3, bf16[2,4,256,512]{3,2,1,0:T(8,128)(2,1)S(1)} %matrix.1.split_ref), custom_call_target="tpu_custom_call" | custom-call | flops 402653184 | bytes 1572864 | tf_op jit(solution)/shard_map/radial/pallas_call | solution.py:347
  31.7 14.8 %all-to-all-start.1 = ((f32[64,8,128]{2,1,0:T(8,128)}), f32[64,8,128]{2,1,0:T(8,128)S(1)}, u32[]{:S(2)}, u32[]{:S(2)}) async-start(f32[64,8,128]{2,1,0:T(8,128)} %bitcast.4), calls=%async_computation.1 | async-start | bytes 524288 | tf_op jit(solution)/shard_map/all_to_all | solution.py:356
  46.5 0.0 copy-done.3
  46.6 3.7 %collective-permute-start.1 = (f32[4,3,4,8,128]{4,3,2,1,0:T(8,128)S(1)}, f32[4,3,4,8,128]{4,3,2,1,0:T(8,128)S(1)}, u32[]{:S(2)}, u32[]{:S(2)}) collective-permute-start(f32[4,3,4,8,128]{4,3,2,1,0:T(8,128)S(1)} %copy-done.3), channel_id=1, source_target_pairs={{1,0},{2,1},{3,2},{4,3},{5,4},{6,5},{7,6},{0,7},{9,8},{10,9},{11,1... | collective-permute-start | bytes 589832 | tf_op jit(solution)/shard_map/ppermute | solution.py:326
  50.2 1.9 %collective-permute-start = (f32[4,3,4,8,128]{4,3,2,1,0:T(8,128)S(1)}, f32[4,3,4,8,128]{4,3,2,1,0:T(8,128)S(1)}, u32[]{:S(2)}, u32[]{:S(2)}) collective-permute-start(f32[4,3,4,8,128]{4,3,2,1,0:T(8,128)S(1)} %copy-done.3), channel_id=1, source_target_pairs={{0,1},{1,2},{2,3},{3,4},{4,5},{5,6},{6,7},{7,0},{8,9},{9,10},{10,1... | collective-permute-start | bytes 589832 | tf_op jit(solution)/shard_map/ppermute | solution.py:325
  52.1 0.0 copy-done
  52.2 1.6 %theta.1 = (f32[3,4,8,512]{3,2,1,0:T(8,128)S(1)}, f32[3,4,8,512]{3,2,1,0:T(8,128)S(1)}) custom-call(f32[3,4,8,512]{3,2,1,0:T(8,128)S(1)} %copy-done, bf16[2,2,256,512]{3,2,1,0:T(8,128)(2,1)} %constant.5.clone.table_hbm), custom_call_target="tpu_custom_call" | custom-call | flops 301989888 | bytes 1179648 | tf_op jit(solution)/shard_map/theta/pallas_call | solution.py:327
  53.7 2.1 %collective-permute-done.1.after_ref = f32[4,3,4,8,128]{4,3,2,1,0:T(8,128)S(1)} collective-permute-done((f32[4,3,4,8,128]{4,3,2,1,0:T(8,128)S(1)}, f32[4,3,4,8,128]{4,3,2,1,0:T(8,128)S(1)}, u32[]{:S(2)}, u32[]{:S(2)}) %collective-permute-start.1) | collective-permute-done | bytes 196640 | tf_op jit(solution)/shard_map/ppermute | solution.py:326
  55.8 3.2 %collective-permute-done.before_ref = f32[4,3,4,8,128]{4,3,2,1,0:T(8,128)S(1)} collective-permute-done((f32[4,3,4,8,128]{4,3,2,1,0:T(8,128)S(1)}, f32[4,3,4,8,128]{4,3,2,1,0:T(8,128)S(1)}, u32[]{:S(2)}, u32[]{:S(2)}) %collective-permute-start) | collective-permute-done | bytes 196640 | tf_op jit(solution)/shard_map/ppermute | solution.py:325
  59.0 0.0 copy-done.4
  59.0 0.1 broadcast_in_dim.2.ratio_ref
  59.1 0.0 copy-done.2
  59.1 0.2 local.1.local_ref
  59.3 0.0 all-to-all-done.1.radial_ref
  59.3 0.9 %final.1 = (f32[3,4,8,512]{3,2,1,0:T(8,128)}, f32[3,4,8,512]{3,2,1,0:T(8,128)}) custom-call(f32[64,8,128]{2,1,0:T(8,128)S(1)} %all-to-all-done.1.radial_ref, f32[3,4,8,512]{3,2,1,0:T(8,128)S(1)} %local.1.local_ref, f32[3,4,8,512]{3,2,1,0:T(8,128)S(1)} %copy-done), custom_call_target="tpu_custom_call" | custom-call | flops 491520 | bytes 983040 | tf_op jit(solution)/shard_map/final/pallas_call | solution.py:361
Async XLA Ops:
  3.0 27.3 %all-to-all-start = ((f32[64,8,128]{2,1,0:T(8,128)}), f32[64,8,128]{2,1,0:T(8,128)S(1)}, u32[]{:S(2)}, u32[]{:S(2)}) async-start(f32[64,8,128]{2,1,0:T(8,128)} %bitcast.5), calls=%async_computation | async-start | bytes 524288 | tf_op jit(solution)/shard_map/all_to_all | solution.py:320
  22.9 1.2 %copy-start.1 = (f32[512,512]{1,0:T(8,128)S(1)}, f32[512,512]{1,0:T(8,128)}, u32[]{:S(2)}) copy-start(f32[512,512]{1,0:T(8,128)} %matrix_ref.1) | copy-start | bytes 3145732
  25.3 21.2 %copy-start.3 = (f32[4,3,4,8,128]{4,3,2,1,0:T(8,128)S(1)}, f32[4,3,4,8,128]{4,3,2,1,0:T(8,128)}, u32[]{:S(2)}) copy-start(f32[4,3,4,8,128]{4,3,2,1,0:T(8,128)} %get-tuple-element.7.smooth_ref) | copy-start | bytes 589828
  25.3 26.8 %copy-start = (f32[3,4,8,512]{3,2,1,0:T(8,128)S(1)}, f32[3,4,8,512]{3,2,1,0:T(8,128)}, u32[]{:S(2)}) copy-start(f32[3,4,8,512]{3,2,1,0:T(8,128)} %velocity_ref.3) | copy-start | bytes 589828
  30.4 28.6 %copy-start.4 = (f32[8]{0:T(128)S(1)}, f32[8]{0:T(128)}, u32[]{:S(2)}) copy-start(f32[8]{0:T(128)} %param.9) | copy-start | bytes 100
  30.4 28.7 %copy-start.2 = (f32[3,4,8,512]{3,2,1,0:T(8,128)S(1)}, f32[3,4,8,512]{3,2,1,0:T(8,128)}, u32[]{:S(2)}) copy-start(f32[3,4,8,512]{3,2,1,0:T(8,128)} %previous_ref.1) | copy-start | bytes 589828
  31.7 27.6 %all-to-all-start.1 = ((f32[64,8,128]{2,1,0:T(8,128)}), f32[64,8,128]{2,1,0:T(8,128)S(1)}, u32[]{:S(2)}, u32[]{:S(2)}) async-start(f32[64,8,128]{2,1,0:T(8,128)} %bitcast.4), calls=%async_computation.1 | async-start | bytes 524288 | tf_op jit(solution)/shard_map/all_to_all | solution.py:356
  46.6 9.3 %collective-permute-start.1 = (f32[4,3,4,8,128]{4,3,2,1,0:T(8,128)S(1)}, f32[4,3,4,8,128]{4,3,2,1,0:T(8,128)S(1)}, u32[]{:S(2)}, u32[]{:S(2)}) collective-permute-start(f32[4,3,4,8,128]{4,3,2,1,0:T(8,128)S(1)} %copy-done.3), channel_id=1, source_target_pairs={{1,0},{2,1},{3,2},{4,3},{5,4},{6,5},{7,6},{0,7},{9,8},{10,9},{11,1... | collective-permute-start | bytes 589832 | tf_op jit(solution)/shard_map/ppermute | solution.py:326
  50.2 8.8 %collective-permute-start = (f32[4,3,4,8,128]{4,3,2,1,0:T(8,128)S(1)}, f32[4,3,4,8,128]{4,3,2,1,0:T(8,128)S(1)}, u32[]{:S(2)}, u32[]{:S(2)}) collective-permute-start(f32[4,3,4,8,128]{4,3,2,1,0:T(8,128)S(1)} %copy-done.3), channel_id=1, source_target_pairs={{0,1},{1,2},{2,3},{3,4},{4,5},{5,6},{6,7},{7,0},{8,9},{9,10},{10,1... | collective-permute-start | bytes 589832 | tf_op jit(solution)/shard_map/ppermute | solution.py:325

commit v5 on v4

--- a/solution.py
+++ b/solution.py
@@ -182,17 +182,21 @@
 
 
 def local_kernel(
-    smooth_ref, before_ref, after_ref, slope_ref, curve_ref, previous_ref, ratio_ref, result_ref
+    smooth_ref, near_ref, far_ref, slope_ref, curve_ref, previous_ref, ratio_ref, result_ref
 ):
     blocks, components, planes, rows, _ = smooth_ref.shape
     ratio = ratio_ref[...]
     square = ratio * ratio
+    odd = jnp.full(ratio.shape, lax.rem(lax.axis_index("axial"), 2)) == 1
     for block in range(blocks):
         lanes = slice(block * LANES, (block + 1) * LANES)
         for c in range(components):
-            line = [before_ref[block, c, plane] for plane in range(planes)]
-            line += [smooth_ref[block, c, plane] for plane in range(planes)]
-            line += [after_ref[block, c, plane] for plane in range(planes)]
+            line = [None] * (3 * planes)
+            for plane in range(planes):
+                near, far = near_ref[block, c, plane], far_ref[block, c, plane]
+                line[plane] = jnp.where(odd, near, far)
+                line[planes + plane] = smooth_ref[block, c, plane]
+                line[2 * planes + plane] = jnp.where(odd, far, near)
             for plane in range(planes):
                 here = planes + plane
                 first = jnp.zeros_like(line[here])
@@ -320,10 +324,11 @@
     pencil = exchange(message.reshape(peers, radial_rows, LANES))
 
     ring = lax.axis_size("axial")
-    up = [(i, (i + 1) % ring) for i in range(ring)]
-    down = [(j, i) for i, j in up]
-    before = lax.ppermute(smooth, "axial", up)
-    after = lax.ppermute(smooth, "axial", down)
+    near = lax.ppermute(smooth, "axial", [(i, i ^ 1) for i in range(ring)])
+    far = lax.ppermute(
+        smooth, "axial", [(i, (i + (1 if i % 2 else ring - 1)) % ring) for i in range(ring)]
+    )
+    pencil, far = lax.optimization_barrier((pencil, far))
     theta_slope, theta_curve = call(
         theta_kernel,
         "theta",
@@ -357,7 +362,7 @@
     ratio = jnp.broadcast_to(inv_radius[:, None], (radial_rows, LANES))
     (local,) = call(
         local_kernel, "local", [VMEM] * 7, [(shape, f32, VMEM)], 40 * size, 32 * size
-    )(smooth, before, after, theta_slope, theta_curve, previous_rhs, ratio)
+    )(smooth, near, far, theta_slope, theta_curve, previous_rhs, ratio)
     return call(
         final_kernel,
         "final",

time: 60.6 us -> 60.3 us (level)
  the two profiles are of different devices: /device:TPU:8 before, /device:TPU:1 now
where the time goes in v5:
time: 60.3 us; the launch traced here: 59.8 us
  starting transfers between devices  42.8 us (71%)
  Pallas kernels  7.64 us (13%)
  waiting for transfers between devices  7.25 us (12%)
  local copies, waits for them, and re-layouts  1.31 us (2%)
  between operations  0.75 us (1%)
    all_to_all x1, starting transfers between devices, shards(): pencil = exchange(message.reshape(peers, radial_rows, LANES))  21.4 us
    all_to_all x1, starting transfers between devices, shards(): radial = exchange(result.reshape(peers, radial_rows, LANES))  14.4 us
    ppermute x1, waiting for transfers between devices, shards(): lax.ppermute(smooth, 'axial', [(i, (i + (1 if i % 2 else ring - 1)) % rin...  6.47 us
    ppermute x1, starting transfers between devices, shards(): lax.ppermute(smooth, 'axial', [(i, (i + (1 if i % 2 else ring - 1)) % rin...  3.94 us
    ppermute x1, starting transfers between devices, shards(): near = lax.ppermute(smooth, 'axial', [(i, i ^ 1) for i in range(ring)])  3.04 us
    pallas_call x1, Pallas kernels, shards(): call(filter_kernel, 'filter', [HBM] * 2, [(smooth_shape, f32, HBM), (mess...  2.41 us
    pallas_call x1, Pallas kernels, shards(): call(theta_kernel, 'theta', [VMEM, HBM], [(shape, f32, VMEM)] * 2, 12 * s...  1.58 us
    pallas_call x1, Pallas kernels, shards(): call(functools.partial(radial_kernel, planes, first, peers), 'radial', [V...  1.37 us
  transfers between devices with their start and end apart: 4, of which 2 were waited for; matrix products, arithmetic and copies ran while one was open for 0% of the time, Pallas kernels for 5%

profile of v5, /device:TPU:1, one launch (start us, length us, event | category | flops | bytes accessed | tf_op | source)
XLA Modules:
  0.0 59.8 jit_solution(2706153833280602159)
XLA Ops:
  0.6 2.4 %filter.1 = (f32[4,3,4,8,128]{4,3,2,1,0:T(8,128)}, f32[4,4,4,8,128]{4,3,2,1,0:T(8,128)}) custom-call(f32[3,4,8,512]{3,2,1,0:T(8,128)} %velocity_ref.3, bf16[2,2,256,256]{3,2,1,0:T(8,128)(2,1)} %constant.4.clone.table_hbm), custom_call_target="tpu_custom_call" | custom-call | flops 150994944 | bytes 983040 | tf_op jit(solution)/shard_map/filter/pallas_call | solution.py:299
  3.0 21.4 %all-to-all-start = ((f32[64,8,128]{2,1,0:T(8,128)}), f32[64,8,128]{2,1,0:T(8,128)S(1)}, u32[]{:S(2)}, u32[]{:S(2)}) async-start(f32[64,8,128]{2,1,0:T(8,128)} %bitcast.5), calls=%async_computation | async-start | bytes 524288 | tf_op jit(solution)/shard_map/all_to_all | solution.py:324
  24.5 3.9 %collective-permute-start = (f32[4,3,4,8,128]{4,3,2,1,0:T(8,128)}, f32[4,3,4,8,128]{4,3,2,1,0:T(8,128)S(1)}, u32[]{:S(2)}, u32[]{:S(2)}) collective-permute-start(f32[4,3,4,8,128]{4,3,2,1,0:T(8,128)} %get-tuple-element.9.smooth_ref), channel_id=1, source_target_pairs={{0,7},{1,2},{2,1},{3,4},{4,3},{5,6},{6,5},{7,0},{8,15},{9,10},{10,... | collective-permute-start | bytes 589832 | tf_op jit(solution)/shard_map/ppermute | solution.py:328
  28.4 0.0 copy-start.1
  28.4 1.2 %copy-done.1 = f32[512,512]{1,0:T(8,128)S(1)} copy-done((f32[512,512]{1,0:T(8,128)S(1)}, f32[512,512]{1,0:T(8,128)}, u32[]{:S(2)}) %copy-start.1) | copy-done | bytes 1048600
  29.6 1.2 %matrix.1.split_ref = bf16[2,4,256,512]{3,2,1,0:T(8,128)(2,1)S(1)} custom-call(f32[512,512]{1,0:T(8,128)S(1)} %copy-done.1), custom_call_target="tpu_custom_call" | custom-call | flops 805306368 | bytes 3145728 | tf_op jit(solution)/shard_map/matrix/pallas_call | solution.py:344
  30.8 0.0 copy-start.3
  30.8 0.0 copy-start
  30.8 6.5 %collective-permute-done.far_ref = f32[4,3,4,8,128]{4,3,2,1,0:T(8,128)S(1)} collective-permute-done((f32[4,3,4,8,128]{4,3,2,1,0:T(8,128)}, f32[4,3,4,8,128]{4,3,2,1,0:T(8,128)S(1)}, u32[]{:S(2)}, u32[]{:S(2)}) %collective-permute-start) | collective-permute-done | bytes 196640 | tf_op jit(solution)/shard_map/ppermute | solution.py:328
  37.3 0.0 all-to-all-done
  37.3 0.0 copy-start.4
  37.3 0.0 copy-start.2
  37.3 1.4 %radial.1 = f32[512,128]{1,0:T(8,128)} custom-call(f32[512,128]{1,0:T(8,128)S(1)} %bitcast.3, bf16[2,4,256,512]{3,2,1,0:T(8,128)(2,1)S(1)} %matrix.1.split_ref), custom_call_target="tpu_custom_call" | custom-call | flops 402653184 | bytes 1572864 | tf_op jit(solution)/shard_map/radial/pallas_call | solution.py:352
  38.7 14.4 %all-to-all-start.1 = ((f32[64,8,128]{2,1,0:T(8,128)}), f32[64,8,128]{2,1,0:T(8,128)S(1)}, u32[]{:S(2)}, u32[]{:S(2)}) async-start(f32[64,8,128]{2,1,0:T(8,128)} %bitcast.4), calls=%async_computation.1 | async-start | bytes 524288 | tf_op jit(solution)/shard_map/all_to_all | solution.py:361
  53.1 0.0 copy-done.3
  53.1 3.0 %collective-permute-start.1 = (f32[4,3,4,8,128]{4,3,2,1,0:T(8,128)S(1)}, f32[4,3,4,8,128]{4,3,2,1,0:T(8,128)S(1)}, u32[]{:S(2)}, u32[]{:S(2)}) collective-permute-start(f32[4,3,4,8,128]{4,3,2,1,0:T(8,128)S(1)} %copy-done.3), channel_id=1, source_target_pairs={{0,1},{1,0},{2,3},{3,2},{4,5},{5,4},{6,7},{7,6},{8,9},{9,8},{10,11... | collective-permute-start | bytes 589832 | tf_op jit(solution)/shard_map/ppermute | solution.py:327
  56.2 0.0 copy-done
  56.2 1.6 %theta.1 = (f32[3,4,8,512]{3,2,1,0:T(8,128)S(1)}, f32[3,4,8,512]{3,2,1,0:T(8,128)S(1)}) custom-call(f32[3,4,8,512]{3,2,1,0:T(8,128)S(1)} %copy-done, bf16[2,2,256,512]{3,2,1,0:T(8,128)(2,1)} %constant.5.clone.table_hbm), custom_call_target="tpu_custom_call" | custom-call | flops 301989888 | bytes 1179648 | tf_op jit(solution)/shard_map/theta/pallas_call | solution.py:332
  57.8 0.0 collective-permute-done.1.near_ref
  57.8 0.0 copy-done.4
  57.8 0.1 broadcast_in_dim.2.ratio_ref
  57.9 0.0 copy-done.2
  57.9 0.2 local.1.local_ref
  58.1 0.8 %all-to-all-done.1.radial_ref = f32[64,8,128]{2,1,0:T(8,128)S(1)} async-done(((f32[64,8,128]{2,1,0:T(8,128)}), f32[64,8,128]{2,1,0:T(8,128)S(1)}, u32[]{:S(2)}, u32[]{:S(2)}) %all-to-all-start.1) | async-done | bytes 262176 | tf_op jit(solution)/shard_map/all_to_all | solution.py:361
  58.9 0.9 %final.1 = (f32[3,4,8,512]{3,2,1,0:T(8,128)}, f32[3,4,8,512]{3,2,1,0:T(8,128)}) custom-call(f32[64,8,128]{2,1,0:T(8,128)S(1)} %all-to-all-done.1.radial_ref, f32[3,4,8,512]{3,2,1,0:T(8,128)S(1)} %local.1.local_ref, f32[3,4,8,512]{3,2,1,0:T(8,128)S(1)} %copy-done), custom_call_target="tpu_custom_call" | custom-call | flops 491520 | bytes 983040 | tf_op jit(solution)/shard_map/final/pallas_call | solution.py:366
Async XLA Ops:
  3.0 34.3 %all-to-all-start = ((f32[64,8,128]{2,1,0:T(8,128)}), f32[64,8,128]{2,1,0:T(8,128)S(1)}, u32[]{:S(2)}, u32[]{:S(2)}) async-start(f32[64,8,128]{2,1,0:T(8,128)} %bitcast.5), calls=%async_computation | async-start | bytes 524288 | tf_op jit(solution)/shard_map/all_to_all | solution.py:324
  24.5 12.8 %collective-permute-start = (f32[4,3,4,8,128]{4,3,2,1,0:T(8,128)}, f32[4,3,4,8,128]{4,3,2,1,0:T(8,128)S(1)}, u32[]{:S(2)}, u32[]{:S(2)}) collective-permute-start(f32[4,3,4,8,128]{4,3,2,1,0:T(8,128)} %get-tuple-element.9.smooth_ref), channel_id=1, source_target_pairs={{0,7},{1,2},{2,1},{3,4},{4,3},{5,6},{6,5},{7,0},{8,15},{9,10},{10,... | collective-permute-start | bytes 589832 | tf_op jit(solution)/shard_map/ppermute | solution.py:328
  28.4 1.2 %copy-start.1 = (f32[512,512]{1,0:T(8,128)S(1)}, f32[512,512]{1,0:T(8,128)}, u32[]{:S(2)}) copy-start(f32[512,512]{1,0:T(8,128)} %matrix_ref.1) | copy-start | bytes 3145732
  30.8 22.3 %copy-start.3 = (f32[4,3,4,8,128]{4,3,2,1,0:T(8,128)S(1)}, f32[4,3,4,8,128]{4,3,2,1,0:T(8,128)}, u32[]{:S(2)}) copy-start(f32[4,3,4,8,128]{4,3,2,1,0:T(8,128)} %get-tuple-element.9.smooth_ref) | copy-start | bytes 589828
  30.8 25.4 %copy-start = (f32[3,4,8,512]{3,2,1,0:T(8,128)S(1)}, f32[3,4,8,512]{3,2,1,0:T(8,128)}, u32[]{:S(2)}) copy-start(f32[3,4,8,512]{3,2,1,0:T(8,128)} %velocity_ref.3) | copy-start | bytes 589828
  37.3 20.5 %copy-start.4 = (f32[8]{0:T(128)S(1)}, f32[8]{0:T(128)}, u32[]{:S(2)}) copy-start(f32[8]{0:T(128)} %param.9) | copy-start | bytes 100
  37.3 20.6 %copy-start.2 = (f32[3,4,8,512]{3,2,1,0:T(8,128)S(1)}, f32[3,4,8,512]{3,2,1,0:T(8,128)}, u32[]{:S(2)}) copy-start(f32[3,4,8,512]{3,2,1,0:T(8,128)} %previous_ref.1) | copy-start | bytes 589828
  38.7 20.2 %all-to-all-start.1 = ((f32[64,8,128]{2,1,0:T(8,128)}), f32[64,8,128]{2,1,0:T(8,128)S(1)}, u32[]{:S(2)}, u32[]{:S(2)}) async-start(f32[64,8,128]{2,1,0:T(8,128)} %bitcast.4), calls=%async_computation.1 | async-start | bytes 524288 | tf_op jit(solution)/shard_map/all_to_all | solution.py:361
  53.1 4.7 %collective-permute-start.1 = (f32[4,3,4,8,128]{4,3,2,1,0:T(8,128)S(1)}, f32[4,3,4,8,128]{4,3,2,1,0:T(8,128)S(1)}, u32[]{:S(2)}, u32[]{:S(2)}) collective-permute-start(f32[4,3,4,8,128]{4,3,2,1,0:T(8,128)S(1)} %copy-done.3), channel_id=1, source_target_pairs={{0,1},{1,0},{2,3},{3,2},{4,5},{5,4},{6,7},{7,6},{8,9},{9,8},{10,11... | collective-permute-start | bytes 589832 | tf_op jit(solution)/shard_map/ppermute | solution.py:327

commit v6 on v5

--- a/solution.py
+++ b/solution.py
@@ -328,7 +328,7 @@
     far = lax.ppermute(
         smooth, "axial", [(i, (i + (1 if i % 2 else ring - 1)) % ring) for i in range(ring)]
     )
-    pencil, far = lax.optimization_barrier((pencil, far))
+    pencil, near = lax.optimization_barrier((pencil, near))
     theta_slope, theta_curve = call(
         theta_kernel,
         "theta",

time: 60.3 us -> 61.8 us (1.025)
  starting transfers between devices: 42.8 us -> 44.5 us
    all_to_all x1, starting transfers between devices: 14.4 us -> 15.6 us  [shards(): radial = exchange(result.reshape(peers, radial_rows, LANES))]
    all_to_all x1, waiting for transfers between devices: 0.78 us -> 0.01 us  [shards(): radial = exchange(result.reshape(peers, radial_rows, LANES))]
    ppermute x1, starting transfers between devices: 3.94 us -> 4.62 us  [shards(): lax.ppermute(smooth, 'axial', [(i, (i + (1 if i % 2 else ring - 1)) % rin...]
    all_to_all x1, waiting for transfers between devices: 0.01 us -> 0.63 us  [shards(): pencil = exchange(message.reshape(peers, radial_rows, LANES))]
where the time goes in v6:
time: 61.8 us; the launch traced here: 61.5 us
  starting transfers between devices  44.5 us (72%)
  Pallas kernels  7.64 us (12%)
  waiting for transfers between devices  7.25 us (12%)
  local copies, waits for them, and re-layouts  1.31 us (2%)
  between operations  0.75 us (1%)
    all_to_all x1, starting transfers between devices, shards(): pencil = exchange(message.reshape(peers, radial_rows, LANES))  21.4 us
    all_to_all x1, starting transfers between devices, shards(): radial = exchange(result.reshape(peers, radial_rows, LANES))  15.6 us
    ppermute x1, waiting for transfers between devices, shards(): lax.ppermute(smooth, 'axial', [(i, (i + (1 if i % 2 else ring - 1)) % rin...  6.61 us
    ppermute x1, starting transfers between devices, shards(): lax.ppermute(smooth, 'axial', [(i, (i + (1 if i % 2 else ring - 1)) % rin...  4.62 us
    ppermute x1, starting transfers between devices, shards(): near = lax.ppermute(smooth, 'axial', [(i, i ^ 1) for i in range(ring)])  2.86 us
    pallas_call x1, Pallas kernels, shards(): call(filter_kernel, 'filter', [HBM] * 2, [(smooth_shape, f32, HBM), (mess...  2.41 us
    pallas_call x1, Pallas kernels, shards(): call(theta_kernel, 'theta', [VMEM, HBM], [(shape, f32, VMEM)] * 2, 12 * s...  1.58 us
    pallas_call x1, Pallas kernels, shards(): call(functools.partial(radial_kernel, planes, first, peers), 'radial', [V...  1.37 us
  transfers between devices with their start and end apart: 4, of which 2 were waited for; matrix products, arithmetic and copies ran while one was open for 0% of the time, Pallas kernels for 5%

profile of v6, /device:TPU:1, one launch (start us, length us, event | category | flops | bytes accessed | tf_op | source)
XLA Modules:
  0.0 61.5 jit_solution(12098180743731892000)
XLA Ops:
  0.6 2.4 %filter.1 = (f32[4,3,4,8,128]{4,3,2,1,0:T(8,128)}, f32[4,4,4,8,128]{4,3,2,1,0:T(8,128)}) custom-call(f32[3,4,8,512]{3,2,1,0:T(8,128)} %velocity_ref.3, bf16[2,2,256,256]{3,2,1,0:T(8,128)(2,1)} %constant.4.clone.table_hbm), custom_call_target="tpu_custom_call" | custom-call | flops 150994944 | bytes 983040 | tf_op jit(solution)/shard_map/filter/pallas_call | solution.py:299
  3.0 21.4 %all-to-all-start = ((f32[64,8,128]{2,1,0:T(8,128)}), f32[64,8,128]{2,1,0:T(8,128)S(1)}, u32[]{:S(2)}, u32[]{:S(2)}) async-start(f32[64,8,128]{2,1,0:T(8,128)} %bitcast.5), calls=%async_computation | async-start | bytes 524288 | tf_op jit(solution)/shard_map/all_to_all | solution.py:324
  24.5 2.9 %collective-permute-start = (f32[4,3,4,8,128]{4,3,2,1,0:T(8,128)}, f32[4,3,4,8,128]{4,3,2,1,0:T(8,128)S(1)}, u32[]{:S(2)}, u32[]{:S(2)}) collective-permute-start(f32[4,3,4,8,128]{4,3,2,1,0:T(8,128)} %get-tuple-element.9.smooth_ref), channel_id=1, source_target_pairs={{0,1},{1,0},{2,3},{3,2},{4,5},{5,4},{6,7},{7,6},{8,9},{9,8},{10,11... | collective-permute-start | bytes 589832 | tf_op jit(solution)/shard_map/ppermute | solution.py:327
  27.3 0.0 copy-start.1
  27.3 1.2 %copy-done.1 = f32[512,512]{1,0:T(8,128)S(1)} copy-done((f32[512,512]{1,0:T(8,128)S(1)}, f32[512,512]{1,0:T(8,128)}, u32[]{:S(2)}) %copy-start.1) | copy-done | bytes 1048600
  28.6 1.2 %matrix.1.split_ref = bf16[2,4,256,512]{3,2,1,0:T(8,128)(2,1)S(1)} custom-call(f32[512,512]{1,0:T(8,128)S(1)} %copy-done.1), custom_call_target="tpu_custom_call" | custom-call | flops 805306368 | bytes 3145728 | tf_op jit(solution)/shard_map/matrix/pallas_call | solution.py:344
  29.7 0.0 copy-start.3
  29.7 0.0 copy-start
  29.7 0.0 collective-permute-done.near_ref
  29.8 0.6 %all-to-all-done = f32[64,8,128]{2,1,0:T(8,128)S(1)} async-done(((f32[64,8,128]{2,1,0:T(8,128)}), f32[64,8,128]{2,1,0:T(8,128)S(1)}, u32[]{:S(2)}, u32[]{:S(2)}) %all-to-all-start) | async-done | bytes 262176 | tf_op jit(solution)/shard_map/all_to_all | solution.py:324
  30.4 0.0 copy-start.4
  30.4 0.0 copy-start.2
  30.4 1.4 %radial.1 = f32[512,128]{1,0:T(8,128)} custom-call(f32[512,128]{1,0:T(8,128)S(1)} %bitcast.3, bf16[2,4,256,512]{3,2,1,0:T(8,128)(2,1)S(1)} %matrix.1.split_ref), custom_call_target="tpu_custom_call" | custom-call | flops 402653184 | bytes 1572864 | tf_op jit(solution)/shard_map/radial/pallas_call | solution.py:352
  31.8 15.6 %all-to-all-start.1 = ((f32[64,8,128]{2,1,0:T(8,128)}), f32[64,8,128]{2,1,0:T(8,128)S(1)}, u32[]{:S(2)}, u32[]{:S(2)}) async-start(f32[64,8,128]{2,1,0:T(8,128)} %bitcast.4), calls=%async_computation.1 | async-start | bytes 524288 | tf_op jit(solution)/shard_map/all_to_all | solution.py:361
  47.4 0.0 copy-done.3
  47.4 4.6 %collective-permute-start.1 = (f32[4,3,4,8,128]{4,3,2,1,0:T(8,128)S(1)}, f32[4,3,4,8,128]{4,3,2,1,0:T(8,128)S(1)}, u32[]{:S(2)}, u32[]{:S(2)}) collective-permute-start(f32[4,3,4,8,128]{4,3,2,1,0:T(8,128)S(1)} %copy-done.3), channel_id=1, source_target_pairs={{0,7},{1,2},{2,1},{3,4},{4,3},{5,6},{6,5},{7,0},{8,15},{9,10},{10,... | collective-permute-start | bytes 589832 | tf_op jit(solution)/shard_map/ppermute | solution.py:328
  52.0 0.0 copy-done
  52.1 1.6 %theta.1 = (f32[3,4,8,512]{3,2,1,0:T(8,128)S(1)}, f32[3,4,8,512]{3,2,1,0:T(8,128)S(1)}) custom-call(f32[3,4,8,512]{3,2,1,0:T(8,128)S(1)} %copy-done, bf16[2,2,256,512]{3,2,1,0:T(8,128)(2,1)} %constant.5.clone.table_hbm), custom_call_target="tpu_custom_call" | custom-call | flops 301989888 | bytes 1179648 | tf_op jit(solution)/shard_map/theta/pallas_call | solution.py:332
  53.6 6.6 %collective-permute-done.1.far_ref = f32[4,3,4,8,128]{4,3,2,1,0:T(8,128)S(1)} collective-permute-done((f32[4,3,4,8,128]{4,3,2,1,0:T(8,128)S(1)}, f32[4,3,4,8,128]{4,3,2,1,0:T(8,128)S(1)}, u32[]{:S(2)}, u32[]{:S(2)}) %collective-permute-start.1) | collective-permute-done | bytes 196640 | tf_op jit(solution)/shard_map/ppermute | solution.py:328
  60.3 0.0 copy-done.4
  60.3 0.1 broadcast_in_dim.2.ratio_ref
  60.3 0.0 copy-done.2
  60.3 0.2 local.1.local_ref
  60.6 0.0 all-to-all-done.1.radial_ref
  60.6 0.9 %final.1 = (f32[3,4,8,512]{3,2,1,0:T(8,128)}, f32[3,4,8,512]{3,2,1,0:T(8,128)}) custom-call(f32[64,8,128]{2,1,0:T(8,128)S(1)} %all-to-all-done.1.radial_ref, f32[3,4,8,512]{3,2,1,0:T(8,128)S(1)} %local.1.local_ref, f32[3,4,8,512]{3,2,1,0:T(8,128)S(1)} %copy-done), custom_call_target="tpu_custom_call" | custom-call | flops 491520 | bytes 983040 | tf_op jit(solution)/shard_map/final/pallas_call | solution.py:366
Async XLA Ops:
  3.0 27.3 %all-to-all-start = ((f32[64,8,128]{2,1,0:T(8,128)}), f32[64,8,128]{2,1,0:T(8,128)S(1)}, u32[]{:S(2)}, u32[]{:S(2)}) async-start(f32[64,8,128]{2,1,0:T(8,128)} %bitcast.5), calls=%async_computation | async-start | bytes 524288 | tf_op jit(solution)/shard_map/all_to_all | solution.py:324
  24.5 5.3 %collective-permute-start = (f32[4,3,4,8,128]{4,3,2,1,0:T(8,128)}, f32[4,3,4,8,128]{4,3,2,1,0:T(8,128)S(1)}, u32[]{:S(2)}, u32[]{:S(2)}) collective-permute-start(f32[4,3,4,8,128]{4,3,2,1,0:T(8,128)} %get-tuple-element.9.smooth_ref), channel_id=1, source_target_pairs={{0,1},{1,0},{2,3},{3,2},{4,5},{5,4},{6,7},{7,6},{8,9},{9,8},{10,11... | collective-permute-start | bytes 589832 | tf_op jit(solution)/shard_map/ppermute | solution.py:327
  27.3 1.2 %copy-start.1 = (f32[512,512]{1,0:T(8,128)S(1)}, f32[512,512]{1,0:T(8,128)}, u32[]{:S(2)}) copy-start(f32[512,512]{1,0:T(8,128)} %matrix_ref.1) | copy-start | bytes 3145732
  29.7 17.7 %copy-start.3 = (f32[4,3,4,8,128]{4,3,2,1,0:T(8,128)S(1)}, f32[4,3,4,8,128]{4,3,2,1,0:T(8,128)}, u32[]{:S(2)}) copy-start(f32[4,3,4,8,128]{4,3,2,1,0:T(8,128)} %get-tuple-element.9.smooth_ref) | copy-start | bytes 589828
  29.7 22.3 %copy-start = (f32[3,4,8,512]{3,2,1,0:T(8,128)S(1)}, f32[3,4,8,512]{3,2,1,0:T(8,128)}, u32[]{:S(2)}) copy-start(f32[3,4,8,512]{3,2,1,0:T(8,128)} %velocity_ref.3) | copy-start | bytes 589828
  30.4 29.9 %copy-start.4 = (f32[8]{0:T(128)S(1)}, f32[8]{0:T(128)}, u32[]{:S(2)}) copy-start(f32[8]{0:T(128)} %param.9) | copy-start | bytes 100
  30.4 29.9 %copy-start.2 = (f32[3,4,8,512]{3,2,1,0:T(8,128)S(1)}, f32[3,4,8,512]{3,2,1,0:T(8,128)}, u32[]{:S(2)}) copy-start(f32[3,4,8,512]{3,2,1,0:T(8,128)} %previous_ref.1) | copy-start | bytes 589828
  31.8 28.8 %all-to-all-start.1 = ((f32[64,8,128]{2,1,0:T(8,128)}), f32[64,8,128]{2,1,0:T(8,128)S(1)}, u32[]{:S(2)}, u32[]{:S(2)}) async-start(f32[64,8,128]{2,1,0:T(8,128)} %bitcast.4), calls=%async_computation.1 | async-start | bytes 524288 | tf_op jit(solution)/shard_map/all_to_all | solution.py:361
  47.4 12.8 %collective-permute-start.1 = (f32[4,3,4,8,128]{4,3,2,1,0:T(8,128)S(1)}, f32[4,3,4,8,128]{4,3,2,1,0:T(8,128)S(1)}, u32[]{:S(2)}, u32[]{:S(2)}) collective-permute-start(f32[4,3,4,8,128]{4,3,2,1,0:T(8,128)S(1)} %copy-done.3), channel_id=1, source_target_pairs={{0,7},{1,2},{2,1},{3,4},{4,3},{5,6},{6,5},{7,0},{8,15},{9,10},{10,... | collective-permute-start | bytes 589832 | tf_op jit(solution)/shard_map/ppermute | solution.py:328

commit v7 on v6

--- a/solution.py
+++ b/solution.py
@@ -15,6 +15,7 @@
 GROUP = 32
 GROUPS = LANES // GROUP
 FIRST = 52
+HEAVY = 2000
 
 first_coefs = (4.0 / 5.0, -1.0 / 5.0, 4.0 / 105.0, -1.0 / 280.0)
 second_coefs = (8.0 / 5.0, -1.0 / 5.0, 8.0 / 315.0, -1.0 / 560.0)
@@ -334,7 +335,7 @@
         "theta",
         [VMEM, HBM],
         [(shape, f32, VMEM)] * 2,
-        12 * size * points,
+        HEAVY * size * points,
         24 * size,
         [pltpu.VMEM(theta.shape, bf16), dma(())],
     )(velocity, in_hbm(jnp.asarray(theta)))

time: 61.8 us -> 55.9 us (0.905)
  the two profiles are of different devices: /device:TPU:1 before, /device:TPU:2 now
where the time goes in v7:
time: 55.9 us; the launch traced here: 55.5 us
  starting transfers between devices  41.5 us (74%)
  Pallas kernels  7.69 us (14%)
  waiting for transfers between devices  4.22 us (8%)
  local copies, waits for them, and re-layouts  1.32 us (2%)
  between operations  0.78 us (1%)
    all_to_all x1, starting transfers between devices, shards(): pencil = exchange(message.reshape(peers, radial_rows, LANES))  19.4 us
    all_to_all x1, starting transfers between devices, shards(): radial = exchange(result.reshape(peers, radial_rows, LANES))  14.9 us
    ppermute x1, starting transfers between devices, shards(): lax.ppermute(smooth, 'axial', [(i, (i + (1 if i % 2 else ring - 1)) % rin...  5.3 us
    all_to_all x1, waiting for transfers between devices, shards(): radial = exchange(result.reshape(peers, radial_rows, LANES))  4.21 us
    pallas_call x1, Pallas kernels, shards(): call(filter_kernel, 'filter', [HBM] * 2, [(smooth_shape, f32, HBM), (mess...  2.41 us
    ppermute x1, starting transfers between devices, shards(): near = lax.ppermute(smooth, 'axial', [(i, i ^ 1) for i in range(ring)])  1.92 us
    pallas_call x1, Pallas kernels, shards(): call(theta_kernel, 'theta', [VMEM, HBM], [(shape, f32, VMEM)] * 2, HEAVY...  1.63 us
    pallas_call x1, Pallas kernels, shards(): call(functools.partial(radial_kernel, planes, first, peers), 'radial', [V...  1.37 us
  transfers between devices with their start and end apart: 4, of which 1 were waited for; matrix products, arithmetic and copies ran while one was open for 0% of the time, Pallas kernels for 8%

profile of v7, /device:TPU:2, one launch (start us, length us, event | category | flops | bytes accessed | tf_op | source)
XLA Modules:
  0.0 55.5 jit_solution(14407915409361519387)
XLA Ops:
  0.6 2.4 %filter.1 = (f32[4,3,4,8,128]{4,3,2,1,0:T(8,128)}, f32[4,4,4,8,128]{4,3,2,1,0:T(8,128)}) custom-call(f32[3,4,8,512]{3,2,1,0:T(8,128)} %velocity_ref.3, bf16[2,2,256,256]{3,2,1,0:T(8,128)(2,1)} %constant.4.clone.table_hbm), custom_call_target="tpu_custom_call" | custom-call | flops 150994944 | bytes 983040 | tf_op jit(solution)/shard_map/filter/pallas_call | solution.py:300
  3.0 19.4 %all-to-all-start = ((f32[64,8,128]{2,1,0:T(8,128)}), f32[64,8,128]{2,1,0:T(8,128)S(1)}, u32[]{:S(2)}, u32[]{:S(2)}) async-start(f32[64,8,128]{2,1,0:T(8,128)} %bitcast.5), calls=%async_computation | async-start | bytes 524288 | tf_op jit(solution)/shard_map/all_to_all | solution.py:325
  22.4 1.9 %collective-permute-start = (f32[4,3,4,8,128]{4,3,2,1,0:T(8,128)}, f32[4,3,4,8,128]{4,3,2,1,0:T(8,128)S(1)}, u32[]{:S(2)}, u32[]{:S(2)}) collective-permute-start(f32[4,3,4,8,128]{4,3,2,1,0:T(8,128)} %get-tuple-element.9.smooth_ref), channel_id=1, source_target_pairs={{0,1},{1,0},{2,3},{3,2},{4,5},{5,4},{6,7},{7,6},{8,9},{9,8},{10,11... | collective-permute-start | bytes 589832 | tf_op jit(solution)/shard_map/ppermute | solution.py:328
  24.4 5.3 %collective-permute-start.1 = (f32[4,3,4,8,128]{4,3,2,1,0:T(8,128)}, f32[4,3,4,8,128]{4,3,2,1,0:T(8,128)S(1)}, u32[]{:S(2)}, u32[]{:S(2)}) collective-permute-start(f32[4,3,4,8,128]{4,3,2,1,0:T(8,128)} %get-tuple-element.9.smooth_ref), channel_id=1, source_target_pairs={{0,7},{1,2},{2,1},{3,4},{4,3},{5,6},{6,5},{7,0},{8,15},{9,10},{10,... | collective-permute-start | bytes 589832 | tf_op jit(solution)/shard_map/ppermute | solution.py:329
  29.7 0.0 copy-start
  29.7 1.2 %copy-done = f32[512,512]{1,0:T(8,128)S(1)} copy-done((f32[512,512]{1,0:T(8,128)S(1)}, f32[512,512]{1,0:T(8,128)}, u32[]{:S(2)}) %copy-start) | copy-done | bytes 1048600
  30.9 1.2 %matrix.1.split_ref = bf16[2,4,256,512]{3,2,1,0:T(8,128)(2,1)S(1)} custom-call(f32[512,512]{1,0:T(8,128)S(1)} %copy-done), custom_call_target="tpu_custom_call" | custom-call | flops 805306368 | bytes 3145728 | tf_op jit(solution)/shard_map/matrix/pallas_call | solution.py:345
  32.1 0.0 copy-start.1
  32.1 0.0 collective-permute-done.near_ref
  32.1 0.0 all-to-all-done
  32.1 1.4 %radial.1 = f32[512,128]{1,0:T(8,128)} custom-call(f32[512,128]{1,0:T(8,128)S(1)} %bitcast.3, bf16[2,4,256,512]{3,2,1,0:T(8,128)(2,1)S(1)} %matrix.1.split_ref), custom_call_target="tpu_custom_call" | custom-call | flops 402653184 | bytes 1572864 | tf_op jit(solution)/shard_map/radial/pallas_call | solution.py:353
  33.5 14.9 %all-to-all-start.1 = ((f32[64,8,128]{2,1,0:T(8,128)}), f32[64,8,128]{2,1,0:T(8,128)S(1)}, u32[]{:S(2)}, u32[]{:S(2)}) async-start(f32[64,8,128]{2,1,0:T(8,128)} %bitcast.4), calls=%async_computation.1 | async-start | bytes 524288 | tf_op jit(solution)/shard_map/all_to_all | solution.py:362
  48.4 0.0 copy-done.1
  48.4 0.0 copy-start.4
  48.4 0.0 copy-start.2
  48.5 0.0 copy-start.3
  48.5 1.6 %theta.1 = (f32[3,4,8,512]{3,2,1,0:T(8,128)S(1)}, f32[3,4,8,512]{3,2,1,0:T(8,128)S(1)}) custom-call(f32[3,4,8,512]{3,2,1,0:T(8,128)S(1)} %copy-done.1, bf16[2,2,256,512]{3,2,1,0:T(8,128)(2,1)} %constant.5.clone.table_hbm), custom_call_target="tpu_custom_call" | custom-call | flops 50331648000 | bytes 1179648 | tf_op jit(solution)/shard_map/theta/pallas_call | solution.py:333
  50.1 0.0 collective-permute-done.1.far_ref
  50.1 0.0 copy-done.4
  50.1 0.1 broadcast_in_dim.2.ratio_ref
  50.2 0.0 copy-done.2
  50.2 0.0 copy-done.3
  50.2 0.2 local.1.local_ref
  50.4 4.2 %all-to-all-done.1.radial_ref = f32[64,8,128]{2,1,0:T(8,128)S(1)} async-done(((f32[64,8,128]{2,1,0:T(8,128)}), f32[64,8,128]{2,1,0:T(8,128)S(1)}, u32[]{:S(2)}, u32[]{:S(2)}) %all-to-all-start.1) | async-done | bytes 262176 | tf_op jit(solution)/shard_map/all_to_all | solution.py:362
  54.7 0.9 %final.1 = (f32[3,4,8,512]{3,2,1,0:T(8,128)}, f32[3,4,8,512]{3,2,1,0:T(8,128)}) custom-call(f32[64,8,128]{2,1,0:T(8,128)S(1)} %all-to-all-done.1.radial_ref, f32[3,4,8,512]{3,2,1,0:T(8,128)S(1)} %local.1.local_ref, f32[3,4,8,512]{3,2,1,0:T(8,128)S(1)} %copy-done.1), custom_call_target="tpu_custom_call" | custom-call | flops 491520 | bytes 983040 | tf_op jit(solution)/shard_map/final/pallas_call | solution.py:367
Async XLA Ops:
  3.0 29.0 %all-to-all-start = ((f32[64,8,128]{2,1,0:T(8,128)}), f32[64,8,128]{2,1,0:T(8,128)S(1)}, u32[]{:S(2)}, u32[]{:S(2)}) async-start(f32[64,8,128]{2,1,0:T(8,128)} %bitcast.5), calls=%async_computation | async-start | bytes 524288 | tf_op jit(solution)/shard_map/all_to_all | solution.py:325
  22.4 9.6 %collective-permute-start = (f32[4,3,4,8,128]{4,3,2,1,0:T(8,128)}, f32[4,3,4,8,128]{4,3,2,1,0:T(8,128)S(1)}, u32[]{:S(2)}, u32[]{:S(2)}) collective-permute-start(f32[4,3,4,8,128]{4,3,2,1,0:T(8,128)} %get-tuple-element.9.smooth_ref), channel_id=1, source_target_pairs={{0,1},{1,0},{2,3},{3,2},{4,5},{5,4},{6,7},{7,6},{8,9},{9,8},{10,11... | collective-permute-start | bytes 589832 | tf_op jit(solution)/shard_map/ppermute | solution.py:328
  24.4 25.8 %collective-permute-start.1 = (f32[4,3,4,8,128]{4,3,2,1,0:T(8,128)}, f32[4,3,4,8,128]{4,3,2,1,0:T(8,128)S(1)}, u32[]{:S(2)}, u32[]{:S(2)}) collective-permute-start(f32[4,3,4,8,128]{4,3,2,1,0:T(8,128)} %get-tuple-element.9.smooth_ref), channel_id=1, source_target_pairs={{0,7},{1,2},{2,1},{3,4},{4,3},{5,6},{6,5},{7,0},{8,15},{9,10},{10,... | collective-permute-start | bytes 589832 | tf_op jit(solution)/shard_map/ppermute | solution.py:329
  29.7 1.2 %copy-start = (f32[512,512]{1,0:T(8,128)S(1)}, f32[512,512]{1,0:T(8,128)}, u32[]{:S(2)}) copy-start(f32[512,512]{1,0:T(8,128)} %matrix_ref.1) | copy-start | bytes 3145732
  32.1 16.4 %copy-start.1 = (f32[3,4,8,512]{3,2,1,0:T(8,128)S(1)}, f32[3,4,8,512]{3,2,1,0:T(8,128)}, u32[]{:S(2)}) copy-start(f32[3,4,8,512]{3,2,1,0:T(8,128)} %velocity_ref.3) | copy-start | bytes 589828
  33.5 21.2 %all-to-all-start.1 = ((f32[64,8,128]{2,1,0:T(8,128)}), f32[64,8,128]{2,1,0:T(8,128)S(1)}, u32[]{:S(2)}, u32[]{:S(2)}) async-start(f32[64,8,128]{2,1,0:T(8,128)} %bitcast.4), calls=%async_computation.1 | async-start | bytes 524288 | tf_op jit(solution)/shard_map/all_to_all | solution.py:362
  48.4 1.7 %copy-start.4 = (f32[8]{0:T(128)S(1)}, f32[8]{0:T(128)}, u32[]{:S(2)}) copy-start(f32[8]{0:T(128)} %param.9) | copy-start | bytes 100
  48.4 1.8 %copy-start.2 = (f32[3,4,8,512]{3,2,1,0:T(8,128)S(1)}, f32[3,4,8,512]{3,2,1,0:T(8,128)}, u32[]{:S(2)}) copy-start(f32[3,4,8,512]{3,2,1,0:T(8,128)} %previous_ref.1) | copy-start | bytes 589828
  48.5 1.7 %copy-start.3 = (f32[4,3,4,8,128]{4,3,2,1,0:T(8,128)S(1)}, f32[4,3,4,8,128]{4,3,2,1,0:T(8,128)}, u32[]{:S(2)}) copy-start(f32[4,3,4,8,128]{4,3,2,1,0:T(8,128)} %get-tuple-element.9.smooth_ref) | copy-start | bytes 589828

commit v8 on v7

--- a/solution.py
+++ b/solution.py
@@ -77,8 +77,10 @@
 def filter_kernel(
     velocity_hbm,
     table_hbm,
+    matrix_hbm,
     smooth_hbm,
     message_hbm,
+    matrix_ref,
     velocity_ref,
     table_ref,
     smooth_ref,
@@ -92,6 +94,7 @@
         incoming.append(
             pltpu.make_async_copy(table_hbm.at[part], table_ref.at[part], in_sems.at[1 + part])
         )
+    incoming.append(pltpu.make_async_copy(matrix_hbm, matrix_ref, in_sems.at[3]))
     for copy in incoming:
         copy.start()
     incoming[0].wait()
@@ -124,6 +127,7 @@
             outgoing.append(copy)
     for copy in outgoing:
         copy.wait()
+    incoming[3].wait()
 
 
 def theta_kernel(velocity_ref, table_hbm, slope_ref, curve_ref, table_ref, sem):
@@ -141,43 +145,48 @@
         result_ref[..., half:] = (even[:, columns] - odd[:, columns]).reshape(shape)
 
 
-def matrix_kernel(turn, matrix_ref, split_ref):
-    matrix = pltpu.roll(pltpu.roll(matrix_ref[...], turn, 0), turn, 1)
-    once = halves(matrix)
-    twice = halves(product(once, once))
-    _, pieces, rows, _ = split_ref.shape
-    rows //= 2
-    for piece in range(pieces):
-        here = slice(piece * rows, (piece + 1) * rows)
-        for half in range(2):
-            split_ref[half, piece, :rows] = once[half][here]
-            split_ref[half, piece, rows:] = twice[half][here]
-
-
-def radial_kernel(planes, first, peers, pencil_ref, split_ref, result_hbm, result_ref, sems):
+def split_kernel(matrix_ref, split_ref):
+    split_ref[0], split_ref[1] = halves(matrix_ref[...])
+
+
+def wide_product(split_ref, rows, right):
+    high, low = halves(right)
+    both = jnp.concatenate([high, low], axis=1)
+    large = jnp.dot(split_ref[0, rows], both, preferred_element_type=jnp.float32)
+    small = jnp.dot(split_ref[1, rows], high, preferred_element_type=jnp.float32)
+    return large[:, :LANES] + (large[:, LANES:] + small)
+
+
+def radial_kernel(planes, first, peers, pieces, pencil_ref, split_ref, result_hbm, result_ref, sems):
     position = lax.rem(lax.axis_index("radial") + (peers - first), peers)
     part = lax.rem(lax.div(position, planes), GROUPS)
-    pencil = pencil_ref[...]
-    high, low = halves(pencil)
-    both = jnp.concatenate([high, low], axis=1)
+    full = pencil_ref.shape[0]
+    turn = (peers - first) % peers * (full // peers)
+    pencil = jnp.concatenate([pencil_ref[turn:], pencil_ref[:turn]], axis=0)
+    once = wide_product(split_ref, slice(None), pencil)
     groups = lane_groups(pencil.shape)
     place = lax.rem(groups - part + GROUPS, GROUPS)
     speed = jnp.where(place == 0, pencil, jnp.zeros_like(pencil))
     speed = jnp.where(place == 1, pltpu.roll(pencil, GROUP, 1), speed)
     speed = jnp.where(place == 2, pltpu.roll(pencil, 2 * GROUP, 1), speed)
-    _, pieces, rows, _ = split_ref.shape
-    rows //= 2
+    rows = full // pieces
     copies = []
     for piece in range(pieces):
-        large = jnp.dot(split_ref[0, piece], both, preferred_element_type=jnp.float32)
-        small = jnp.dot(split_ref[1, piece], high, preferred_element_type=jnp.float32)
-        derivs = large[:, :LANES] + (large[:, LANES:] + small)
         here = slice(piece * rows, (piece + 1) * rows)
-        result_ref[here] = viscosity * derivs[rows:] - speed[here] * derivs[:rows]
-        here = pl.ds(piece * rows, rows)
-        copy = pltpu.make_async_copy(result_ref.at[here], result_hbm.at[here], sems.at[piece])
-        copy.start()
-        copies.append(copy)
+        twice = wide_product(split_ref, here, once)
+        result = viscosity * twice - speed[here] * once[here]
+        place = (turn + piece * rows) % full
+        until = min(rows, full - place)
+        for start, target, count in ((0, place, until), (until, 0, rows - until)):
+            if count == 0:
+                continue
+            result_ref[target : target + count] = result[start : start + count]
+            there = pl.ds(target, count)
+            copy = pltpu.make_async_copy(
+                result_ref.at[there], result_hbm.at[there], sems.at[len(copies)]
+            )
+            copy.start()
+            copies.append(copy)
     for copy in copies:
         copy.wait()
 
@@ -260,6 +269,8 @@
 
 VMEM = pl.BlockSpec(memory_space=pltpu.VMEM)
 HBM = pl.BlockSpec(memory_space=pltpu.HBM)
+PINNED = pl.BlockSpec(memory_space=pltpu.VMEM)
+PINS = {id(HBM): pltpu.HBM, id(PINNED): pltpu.VMEM, id(VMEM): jax.ShapeDtypeStruct}
 
 
 in_hbm = functools.partial(pltpu.with_memory_space_constraint, memory_space=pltpu.HBM)
@@ -269,10 +280,7 @@
 def call(kernel, name, in_specs, outs, flops, moved, scratch=()):
     return pl.pallas_call(
         kernel,
-        out_shape=[
-            pltpu.HBM(shape, dtype) if spec is HBM else jax.ShapeDtypeStruct(shape, dtype)
-            for shape, dtype, spec in outs
-        ],
+        out_shape=[PINS[id(spec)](shape, dtype) for shape, dtype, spec in outs],
         in_specs=in_specs,
         out_specs=[spec for _, _, spec in outs],
         scratch_shapes=list(scratch),
@@ -297,11 +305,11 @@
 
     smooth_shape = (blocks, components, planes, radial_rows, LANES)
     message_shape = (blocks, GROUPS, planes, radial_rows, LANES)
-    smooth, message = call(
+    smooth, message, matrix = call(
         filter_kernel,
         "filter",
-        [HBM] * 2,
-        [(smooth_shape, f32, HBM), (message_shape, f32, HBM)],
+        [HBM] * 3,
+        [(smooth_shape, f32, HBM), (message_shape, f32, HBM), (radial_deriv.shape, f32, PINNED)],
         6 * size * points,
         20 * size,
         [
@@ -309,10 +317,10 @@
             pltpu.VMEM(keep.shape, bf16),
             pltpu.VMEM(smooth_shape, f32),
             pltpu.VMEM(message_shape, f32),
-            dma((3,)),
+            dma((4,)),
             dma((4,)),
         ],
-    )(in_hbm(velocity), in_hbm(jnp.asarray(keep)))
+    )(in_hbm(velocity), in_hbm(jnp.asarray(keep)), in_hbm(radial_deriv))
     first = FIRST % peers
     exchange = functools.partial(
         lax.all_to_all,
@@ -343,22 +351,22 @@
     full = peers * radial_rows
     pieces = 4
     (split,) = call(
-        functools.partial(matrix_kernel, (peers - first) * radial_rows % full),
-        "matrix",
+        split_kernel,
+        "split",
         [VMEM],
-        [((2, pieces, 2 * full // pieces, full), bf16, VMEM)],
-        6 * full * full * full,
-        12 * full * full,
-    )(radial_deriv)
+        [((2, full, full), bf16, PINNED)],
+        4 * full * full,
+        8 * full * full,
+    )(in_vmem(matrix))
     (result,) = call(
-        functools.partial(radial_kernel, planes, first, peers),
+        functools.partial(radial_kernel, planes, first, peers, pieces),
         "radial",
         [VMEM] * 2,
         [((full, LANES), f32, HBM)],
         12 * full * full * LANES,
         4 * full * (full + 2 * LANES),
-        [pltpu.VMEM((full, LANES), f32), dma((pieces,))],
-    )(in_vmem(pencil.reshape(full, LANES)), split)
+        [pltpu.VMEM((full, LANES), f32), dma((pieces + 1,))],
+    )(in_vmem(pencil.reshape(full, LANES)), in_vmem(split))
     radial = exchange(result.reshape(peers, radial_rows, LANES))
     ratio = jnp.broadcast_to(inv_radius[:, None], (radial_rows, LANES))
     (local,) = call(

time: 55.9 us -> 54.9 us (0.982)
  the two profiles are of different devices: /device:TPU:2 before, /device:TPU:1 now
where the time goes in v8:
time: 54.9 us; the launch traced here: 54 us
  starting transfers between devices  43 us (78%)
  Pallas kernels  6.81 us (12%)
  waiting for transfers between devices  3.3 us (6%)
  between operations  0.77 us (1%)
    all_to_all x1, starting transfers between devices, shards(): pencil = exchange(message.reshape(peers, radial_rows, LANES))  21.5 us
    all_to_all x1, starting transfers between devices, shards(): radial = exchange(result.reshape(peers, radial_rows, LANES))  15.6 us
    all_to_all x1, waiting for transfers between devices, shards(): radial = exchange(result.reshape(peers, radial_rows, LANES))  3.3 us
    ppermute x1, starting transfers between devices, shards(): lax.ppermute(smooth, 'axial', [(i, (i + (1 if i % 2 else ring - 1)) % rin...  3 us
    ppermute x1, starting transfers between devices, shards(): near = lax.ppermute(smooth, 'axial', [(i, i ^ 1) for i in range(ring)])  2.86 us
    pallas_call x1, Pallas kernels, shards(): call(filter_kernel, 'filter', [HBM] * 3, [(smooth_shape, f32, HBM), (mess...  2.42 us
    pallas_call x1, Pallas kernels, shards(): call(theta_kernel, 'theta', [VMEM, HBM], [(shape, f32, VMEM)] * 2, HEAVY...  1.62 us
    pallas_call x1, Pallas kernels, shards(): call(functools.partial(radial_kernel, planes, first, peers, pieces), 'rad...  1.51 us
  transfers between devices with their start and end apart: 4, of which 1 were waited for; matrix products, arithmetic and copies ran while one was open for 0% of the time, Pallas kernels for 6%

profile of v8, /device:TPU:1, one launch (start us, length us, event | category | flops | bytes accessed | tf_op | source)
XLA Modules:
  0.0 54.0 jit_solution(10019972441953198962)
XLA Ops:
  0.6 2.4 %filter.1 = (f32[4,3,4,8,128]{4,3,2,1,0:T(8,128)}, f32[4,4,4,8,128]{4,3,2,1,0:T(8,128)}, f32[512,512]{1,0:T(8,128)S(1)}) custom-call(f32[3,4,8,512]{3,2,1,0:T(8,128)} %velocity_ref.3, bf16[2,2,256,256]{3,2,1,0:T(8,128)(2,1)} %constant.4.clone.table_hbm, f32[512,512]{1,0:T(8,128)} %matrix_hbm.1), custom_call_target="tpu_custom_call" | custom-call | flops 150994944 | bytes 983040 | tf_op jit(solution)/shard_map/filter/pallas_call | solution.py:308
  3.1 0.0 copy-start.2
  3.1 21.5 %all-to-all-start = ((f32[64,8,128]{2,1,0:T(8,128)}), f32[64,8,128]{2,1,0:T(8,128)S(1)}, u32[]{:S(2)}, u32[]{:S(2)}) async-start(f32[64,8,128]{2,1,0:T(8,128)} %bitcast.5), calls=%async_computation | async-start | bytes 524288 | tf_op jit(solution)/shard_map/all_to_all | solution.py:333
  24.6 0.0 copy-done.2
  24.6 2.9 %collective-permute-start = (f32[4,3,4,8,128]{4,3,2,1,0:T(8,128)S(1)}, f32[4,3,4,8,128]{4,3,2,1,0:T(8,128)S(1)}, u32[]{:S(2)}, u32[]{:S(2)}) collective-permute-start(f32[4,3,4,8,128]{4,3,2,1,0:T(8,128)S(1)} %copy-done.2), channel_id=1, source_target_pairs={{0,1},{1,0},{2,3},{3,2},{4,5},{5,4},{6,7},{7,6},{8,9},{9,8},{10,11... | collective-permute-start | bytes 589832 | tf_op jit(solution)/shard_map/ppermute | solution.py:336
  27.5 3.0 %collective-permute-start.1 = (f32[4,3,4,8,128]{4,3,2,1,0:T(8,128)S(1)}, f32[4,3,4,8,128]{4,3,2,1,0:T(8,128)S(1)}, u32[]{:S(2)}, u32[]{:S(2)}) collective-permute-start(f32[4,3,4,8,128]{4,3,2,1,0:T(8,128)S(1)} %copy-done.2), channel_id=1, source_target_pairs={{0,7},{1,2},{2,1},{3,4},{4,3},{5,6},{6,5},{7,0},{8,15},{9,10},{10,... | collective-permute-start | bytes 589832 | tf_op jit(solution)/shard_map/ppermute | solution.py:337
  30.5 0.1 split.1.split_ref
  30.7 0.0 collective-permute-done.near_ref
  30.7 0.0 all-to-all-done
  30.7 1.5 %radial.1 = f32[512,128]{1,0:T(8,128)} custom-call(f32[512,128]{1,0:T(8,128)S(1)} %bitcast.3, bf16[2,512,512]{2,1,0:T(8,128)(2,1)S(1)} %split.1.split_ref), custom_call_target="tpu_custom_call" | custom-call | flops 402653184 | bytes 1572864 | tf_op jit(solution)/shard_map/radial/pallas_call | solution.py:361
  32.2 0.0 copy-start
  32.2 15.6 %all-to-all-start.1 = ((f32[64,8,128]{2,1,0:T(8,128)}), f32[64,8,128]{2,1,0:T(8,128)S(1)}, u32[]{:S(2)}, u32[]{:S(2)}) async-start(f32[64,8,128]{2,1,0:T(8,128)} %bitcast.4), calls=%async_computation.1 | async-start | bytes 524288 | tf_op jit(solution)/shard_map/all_to_all | solution.py:370
  47.8 0.0 copy-done
  47.8 0.0 copy-start.3
  47.9 0.0 copy-start.1
  47.9 1.6 %theta.1 = (f32[3,4,8,512]{3,2,1,0:T(8,128)S(1)}, f32[3,4,8,512]{3,2,1,0:T(8,128)S(1)}) custom-call(f32[3,4,8,512]{3,2,1,0:T(8,128)S(1)} %copy-done, bf16[2,2,256,512]{3,2,1,0:T(8,128)(2,1)} %constant.5.clone.table_hbm), custom_call_target="tpu_custom_call" | custom-call | flops 50331648000 | bytes 1179648 | tf_op jit(solution)/shard_map/theta/pallas_call | solution.py:341
  49.5 0.0 collective-permute-done.1.far_ref
  49.5 0.0 copy-done.3
  49.5 0.1 broadcast_in_dim.2.ratio_ref
  49.6 0.0 copy-done.1
  49.6 0.2 local.1.local_ref
  49.8 3.3 %all-to-all-done.1.radial_ref = f32[64,8,128]{2,1,0:T(8,128)S(1)} async-done(((f32[64,8,128]{2,1,0:T(8,128)}), f32[64,8,128]{2,1,0:T(8,128)S(1)}, u32[]{:S(2)}, u32[]{:S(2)}) %all-to-all-start.1) | async-done | bytes 262176 | tf_op jit(solution)/shard_map/all_to_all | solution.py:370
  53.1 0.9 %final.1 = (f32[3,4,8,512]{3,2,1,0:T(8,128)}, f32[3,4,8,512]{3,2,1,0:T(8,128)}) custom-call(f32[64,8,128]{2,1,0:T(8,128)S(1)} %all-to-all-done.1.radial_ref, f32[3,4,8,512]{3,2,1,0:T(8,128)S(1)} %local.1.local_ref, f32[3,4,8,512]{3,2,1,0:T(8,128)S(1)} %copy-done), custom_call_target="tpu_custom_call" | custom-call | flops 491520 | bytes 983040 | tf_op jit(solution)/shard_map/final/pallas_call | solution.py:375
Async XLA Ops:
  3.1 21.6 %copy-start.2 = (f32[4,3,4,8,128]{4,3,2,1,0:T(8,128)S(1)}, f32[4,3,4,8,128]{4,3,2,1,0:T(8,128)}, u32[]{:S(2)}) copy-start(f32[4,3,4,8,128]{4,3,2,1,0:T(8,128)} %get-tuple-element.10.smooth_ref) | copy-start | bytes 589828
  3.1 27.6 %all-to-all-start = ((f32[64,8,128]{2,1,0:T(8,128)}), f32[64,8,128]{2,1,0:T(8,128)S(1)}, u32[]{:S(2)}, u32[]{:S(2)}) async-start(f32[64,8,128]{2,1,0:T(8,128)} %bitcast.5), calls=%async_computation | async-start | bytes 524288 | tf_op jit(solution)/shard_map/all_to_all | solution.py:333
  24.6 6.0 %collective-permute-start = (f32[4,3,4,8,128]{4,3,2,1,0:T(8,128)S(1)}, f32[4,3,4,8,128]{4,3,2,1,0:T(8,128)S(1)}, u32[]{:S(2)}, u32[]{:S(2)}) collective-permute-start(f32[4,3,4,8,128]{4,3,2,1,0:T(8,128)S(1)} %copy-done.2), channel_id=1, source_target_pairs={{0,1},{1,0},{2,3},{3,2},{4,5},{5,4},{6,7},{7,6},{8,9},{9,8},{10,11... | collective-permute-start | bytes 589832 | tf_op jit(solution)/shard_map/ppermute | solution.py:336
  27.5 22.0 %collective-permute-start.1 = (f32[4,3,4,8,128]{4,3,2,1,0:T(8,128)S(1)}, f32[4,3,4,8,128]{4,3,2,1,0:T(8,128)S(1)}, u32[]{:S(2)}, u32[]{:S(2)}) collective-permute-start(f32[4,3,4,8,128]{4,3,2,1,0:T(8,128)S(1)} %copy-done.2), channel_id=1, source_target_pairs={{0,7},{1,2},{2,1},{3,4},{4,3},{5,6},{6,5},{7,0},{8,15},{9,10},{10,... | collective-permute-start | bytes 589832 | tf_op jit(solution)/shard_map/ppermute | solution.py:337
  32.2 15.6 %copy-start = (f32[3,4,8,512]{3,2,1,0:T(8,128)S(1)}, f32[3,4,8,512]{3,2,1,0:T(8,128)}, u32[]{:S(2)}) copy-start(f32[3,4,8,512]{3,2,1,0:T(8,128)} %velocity_ref.3) | copy-start | bytes 589828
  32.2 20.9 %all-to-all-start.1 = ((f32[64,8,128]{2,1,0:T(8,128)}), f32[64,8,128]{2,1,0:T(8,128)S(1)}, u32[]{:S(2)}, u32[]{:S(2)}) async-start(f32[64,8,128]{2,1,0:T(8,128)} %bitcast.4), calls=%async_computation.1 | async-start | bytes 524288 | tf_op jit(solution)/shard_map/all_to_all | solution.py:370
  47.8 1.7 %copy-start.3 = (f32[8]{0:T(128)S(1)}, f32[8]{0:T(128)}, u32[]{:S(2)}) copy-start(f32[8]{0:T(128)} %param.9) | copy-start | bytes 100
  47.9 1.7 %copy-start.1 = (f32[3,4,8,512]{3,2,1,0:T(8,128)S(1)}, f32[3,4,8,512]{3,2,1,0:T(8,128)}, u32[]{:S(2)}) copy-start(f32[3,4,8,512]{3,2,1,0:T(8,128)} %previous_ref.1) | copy-start | bytes 589828

commit v9 on v8

--- a/solution.py
+++ b/solution.py
@@ -14,6 +14,7 @@
 LANES = 128
 GROUP = 32
 GROUPS = LANES // GROUP
+PAIR = 2
 FIRST = 52
 HEAVY = 2000
 
@@ -70,8 +71,24 @@
     return halves(first + second), halves(first - second)
 
 
-def lane_groups(shape):
-    return lax.broadcasted_iota(jnp.int32, shape, len(shape) - 1) // GROUP
+def swapped(tiles):
+    rows = lax.broadcasted_iota(jnp.int32, tiles.shape, tiles.ndim - 2) // PAIR
+    groups = lax.broadcasted_iota(jnp.int32, tiles.shape, tiles.ndim - 1) // GROUP
+    apart = lax.rem(rows - groups + GROUPS, GROUPS)
+    result = tiles
+    for distance in range(1, GROUPS):
+        moved = pltpu.roll(tiles, PAIR * distance, tiles.ndim - 2)
+        moved = pltpu.roll(moved, LANES - GROUP * distance, tiles.ndim - 1)
+        result = jnp.where(apart == distance, moved, result)
+    return result
+
+
+def lanes_of(c):
+    return slice(c * LANES, (c + 1) * LANES)
+
+
+def pair_of(part):
+    return slice(part * PAIR, (part + 1) * PAIR)
 
 
 def filter_kernel(
@@ -103,7 +120,6 @@
     even = product(total, (table_ref[0, 0], table_ref[0, 1]))
     incoming[2].wait()
     odd = product(gap, (table_ref[1, 0], table_ref[1, 1]))
-    groups = lane_groups((planes, rows, LANES))
     outgoing = []
     blocks = points // LANES
     for section, smooth in enumerate((even + odd, even - odd)):
@@ -112,19 +128,20 @@
             block = section * (blocks // 2) + local
             tile = smooth[:, :, :, local * LANES : (local + 1) * LANES]
             smooth_ref[block] = tile
-            turned = [tile[0]] + [pltpu.roll(tile[c], c * GROUP, 2) for c in range(1, components)]
+            tile = swapped(tile.reshape(components * planes, rows, LANES))
             for part in range(GROUPS):
-                chosen = jnp.zeros_like(turned[0])
-                for c in range(components):
-                    chosen = jnp.where(groups == (part + c) % GROUPS, turned[c], chosen)
-                message_ref[block, part] = chosen
-        here = pl.ds(section * (blocks // 2), blocks // 2)
-        for source, target in ((message_ref, message_hbm), (smooth_ref, smooth_hbm)):
-            copy = pltpu.make_async_copy(
-                source.at[here], target.at[here], out_sems.at[len(outgoing)]
-            )
-            copy.start()
-            outgoing.append(copy)
+                for plane in range(planes):
+                    index = (block * GROUPS + part) * planes + plane
+                    for c in range(components):
+                        message_ref[index, :, lanes_of(c)] = tile[c * planes + plane, pair_of(part)]
+        count = message_ref.shape[0] // 2
+        here = pl.ds(section * count, count)
+        outgoing.append(
+            pltpu.make_async_copy(message_ref.at[here], message_hbm.at[here], out_sems.at[section])
+        )
+        outgoing[-1].start()
+    outgoing.append(pltpu.make_async_copy(smooth_ref, smooth_hbm, out_sems.at[2]))
+    outgoing[-1].start()
     for copy in outgoing:
         copy.wait()
     incoming[3].wait()
@@ -157,31 +174,40 @@
     return large[:, :LANES] + (large[:, LANES:] + small)
 
 
-def radial_kernel(planes, first, peers, pieces, pencil_ref, split_ref, result_hbm, result_ref, sems):
-    position = lax.rem(lax.axis_index("radial") + (peers - first), peers)
-    part = lax.rem(lax.div(position, planes), GROUPS)
-    full = pencil_ref.shape[0]
-    turn = (peers - first) % peers * (full // peers)
-    pencil = jnp.concatenate([pencil_ref[turn:], pencil_ref[:turn]], axis=0)
+def radial_kernel(
+    first, pieces, pencil_ref, split_ref, result_hbm, tiles_ref, result_ref, sems
+):
+    peers, rows, _ = tiles_ref.shape
+    components = pencil_ref.shape[2] // LANES
+    for c in range(components):
+        tiles_ref[:, pair_of(c)] = pencil_ref[:, :, lanes_of(c)]
+    for part in range(components, GROUPS):
+        tiles_ref[:, pair_of(part)] = jnp.zeros((peers, PAIR, LANES), jnp.float32)
+    turn = (peers - first) % peers
+    pencil = swapped(tiles_ref[...]).reshape(peers * rows, LANES)
+    pencil = jnp.concatenate([pencil[turn * rows :], pencil[: turn * rows]], axis=0)
     once = wide_product(split_ref, slice(None), pencil)
-    groups = lane_groups(pencil.shape)
-    place = lax.rem(groups - part + GROUPS, GROUPS)
-    speed = jnp.where(place == 0, pencil, jnp.zeros_like(pencil))
-    speed = jnp.where(place == 1, pltpu.roll(pencil, GROUP, 1), speed)
-    speed = jnp.where(place == 2, pltpu.roll(pencil, 2 * GROUP, 1), speed)
-    rows = full // pieces
+    groups = lax.broadcasted_iota(jnp.int32, pencil.shape, 1) // GROUP
+    speed = jnp.where(groups == 0, pencil, jnp.zeros_like(pencil))
+    speed = jnp.where(groups == 1, pltpu.roll(pencil, GROUP, 1), speed)
+    speed = jnp.where(groups == 2, pltpu.roll(pencil, 2 * GROUP, 1), speed)
+    count = peers // pieces
     copies = []
     for piece in range(pieces):
-        here = slice(piece * rows, (piece + 1) * rows)
+        here = slice(piece * count * rows, (piece + 1) * count * rows)
         twice = wide_product(split_ref, here, once)
         result = viscosity * twice - speed[here] * once[here]
-        place = (turn + piece * rows) % full
-        until = min(rows, full - place)
-        for start, target, count in ((0, place, until), (until, 0, rows - until)):
-            if count == 0:
+        result = swapped(result.reshape(count, rows, LANES))
+        place = (turn + piece * count) % peers
+        until = min(count, peers - place)
+        for start, target, some in ((0, place, until), (until, 0, count - until)):
+            if some == 0:
                 continue
-            result_ref[target : target + count] = result[start : start + count]
-            there = pl.ds(target, count)
+            for c in range(components):
+                result_ref[target : target + some, :, lanes_of(c)] = result[
+                    start : start + some, pair_of(c)
+                ]
+            there = pl.ds(target, some)
             copy = pltpu.make_async_copy(
                 result_ref.at[there], result_hbm.at[there], sems.at[len(copies)]
             )
@@ -231,27 +257,24 @@
     velocity_ref,
     velocity_hbm,
     rhs_hbm,
+    tiles_ref,
     velocity_out_ref,
     rhs_out_ref,
     sems,
 ):
     components, planes, rows, points = velocity_ref.shape
     blocks = points // LANES
-    groups = lane_groups((rows, LANES))
     copies = []
     for plane in range(planes):
         for block in range(blocks):
-            tiles = [
-                radial_ref[(block * GROUPS + part) * planes + plane] for part in range(GROUPS)
-            ]
+            for part in range(GROUPS):
+                index = (block * GROUPS + part) * planes + plane
+                for c in range(components):
+                    tiles_ref[block, c, pair_of(part)] = radial_ref[index, :, lanes_of(c)]
+            radial = swapped(tiles_ref[block])
             for c in range(components):
-                chosen = tiles[0]
-                for part in range(1, GROUPS):
-                    chosen = jnp.where(groups == (part + c) % GROUPS, tiles[part], chosen)
-                if c > 0:
-                    chosen = pltpu.roll(chosen, LANES - c * GROUP, 1)
-                lanes = slice(block * LANES, (block + 1) * LANES)
-                rhs = local_ref[c, plane, :, lanes] + chosen
+                lanes = lanes_of(block)
+                rhs = local_ref[c, plane, :, lanes] + radial[c]
                 rhs_out_ref[c, plane, :, lanes] = rhs
                 velocity_out_ref[c, plane, :, lanes] = (
                     velocity_ref[c, plane, :, lanes] + (section_weight * timestep) * rhs
@@ -304,7 +327,7 @@
     )
 
     smooth_shape = (blocks, components, planes, radial_rows, LANES)
-    message_shape = (blocks, GROUPS, planes, radial_rows, LANES)
+    message_shape = (peers, PAIR, components * LANES)
     smooth, message, matrix = call(
         filter_kernel,
         "filter",
@@ -318,7 +341,7 @@
             pltpu.VMEM(smooth_shape, f32),
             pltpu.VMEM(message_shape, f32),
             dma((4,)),
-            dma((4,)),
+            dma((3,)),
         ],
     )(in_hbm(velocity), in_hbm(jnp.asarray(keep)), in_hbm(radial_deriv))
     first = FIRST % peers
@@ -330,7 +353,7 @@
         tiled=True,
         axis_index_groups=[[(first + i) % peers for i in range(peers)]],
     )
-    pencil = exchange(message.reshape(peers, radial_rows, LANES))
+    pencil = exchange(message)
 
     ring = lax.axis_size("axial")
     near = lax.ppermute(smooth, "axial", [(i, i ^ 1) for i in range(ring)])
@@ -359,15 +382,19 @@
         8 * full * full,
     )(in_vmem(matrix))
     (result,) = call(
-        functools.partial(radial_kernel, planes, first, peers, pieces),
+        functools.partial(radial_kernel, first, pieces),
         "radial",
         [VMEM] * 2,
-        [((full, LANES), f32, HBM)],
+        [(message_shape, f32, HBM)],
         12 * full * full * LANES,
         4 * full * (full + 2 * LANES),
-        [pltpu.VMEM((full, LANES), f32), dma((pieces + 1,))],
-    )(in_vmem(pencil.reshape(full, LANES)), in_vmem(split))
-    radial = exchange(result.reshape(peers, radial_rows, LANES))
+        [
+            pltpu.VMEM((peers, radial_rows, LANES), f32),
+            pltpu.VMEM(message_shape, f32),
+            dma((pieces + 1,)),
+        ],
+    )(in_vmem(pencil), in_vmem(split))
+    radial = exchange(result)
     ratio = jnp.broadcast_to(inv_radius[:, None], (radial_rows, LANES))
     (local,) = call(
         local_kernel, "local", [VMEM] * 7, [(shape, f32, VMEM)], 40 * size, 32 * size
@@ -379,7 +406,12 @@
         [(shape, f32, HBM)] * 2,
         10 * size,
         20 * size,
-        [pltpu.VMEM(shape, f32), pltpu.VMEM(shape, f32), dma((2 * planes,))],
+        [
+            pltpu.VMEM((blocks, components, radial_rows, LANES), f32),
+            pltpu.VMEM(shape, f32),
+            pltpu.VMEM(shape, f32),
+            dma((2 * planes,)),
+        ],
     )(radial, local, velocity)
 
 

time: 54.9 us -> 53.8 us (0.980)
  the two profiles are of different devices: /device:TPU:1 before, /device:TPU:4 now
where the time goes in v9:
time: 53.8 us; the launch traced here: 53.5 us
  starting transfers between devices  41 us (76%)
  Pallas kernels  7.22 us (13%)
  waiting for transfers between devices  4.45 us (8%)
  between operations  0.77 us (1%)
    all_to_all x1, starting transfers between devices, shards(): pencil = exchange(message)  18.7 us
    all_to_all x1, starting transfers between devices, shards(): radial = exchange(result)  15.1 us
    ppermute x1, starting transfers between devices, shards(): lax.ppermute(smooth, 'axial', [(i, (i + (1 if i % 2 else ring - 1)) % rin...  5.3 us
    all_to_all x1, waiting for transfers between devices, shards(): radial = exchange(result)  4.44 us
    pallas_call x1, Pallas kernels, shards(): call(filter_kernel, 'filter', [HBM] * 3, [(smooth_shape, f32, HBM), (mess...  2.5 us
    ppermute x1, starting transfers between devices, shards(): near = lax.ppermute(smooth, 'axial', [(i, i ^ 1) for i in range(ring)])  1.92 us
    pallas_call x1, Pallas kernels, shards(): call(functools.partial(radial_kernel, first, pieces), 'radial', [VMEM] *...  1.76 us
    pallas_call x1, Pallas kernels, shards(): call(theta_kernel, 'theta', [VMEM, HBM], [(shape, f32, VMEM)] * 2, HEAVY...  1.62 us
  transfers between devices with their start and end apart: 4, of which 1 were waited for; matrix products, arithmetic and copies ran while one was open for 0% of the time, Pallas kernels for 7%

profile of v9, /device:TPU:4, one launch (start us, length us, event | category | flops | bytes accessed | tf_op | source)
XLA Modules:
  0.0 53.5 jit_solution(3441321722019770052)
XLA Ops:
  0.6 2.5 %filter.1 = (f32[4,3,4,8,128]{4,3,2,1,0:T(8,128)}, f32[64,2,384]{2,1,0:T(2,128)}, f32[512,512]{1,0:T(8,128)S(1)}) custom-call(f32[3,4,8,512]{3,2,1,0:T(8,128)} %velocity_ref.3, bf16[2,2,256,256]{3,2,1,0:T(8,128)(2,1)} %constant.4.clone.table_hbm, f32[512,512]{1,0:T(8,128)} %matrix_hbm.1), custom_call_target="tpu_custom_call" | custom-call | flops 150994944 | bytes 983040 | tf_op jit(solution)/shard_map/filter/pallas_call | solution.py:331
  3.1 0.0 copy-start.2
  3.2 18.7 %all-to-all-start = ((f32[64,2,384]{2,1,0:T(2,128)}), f32[64,2,384]{2,1,0:T(2,128)S(1)}, u32[]{:S(2)}, u32[]{:S(2)}) async-start(f32[64,2,384]{2,1,0:T(2,128)} %get-tuple-element.9), calls=%async_computation | async-start | bytes 393216 | tf_op jit(solution)/shard_map/all_to_all | solution.py:356
  21.8 0.0 copy-done.2
  21.8 1.9 %collective-permute-start = (f32[4,3,4,8,128]{4,3,2,1,0:T(8,128)S(1)}, f32[4,3,4,8,128]{4,3,2,1,0:T(8,128)S(1)}, u32[]{:S(2)}, u32[]{:S(2)}) collective-permute-start(f32[4,3,4,8,128]{4,3,2,1,0:T(8,128)S(1)} %copy-done.2), channel_id=1, source_target_pairs={{0,1},{1,0},{2,3},{3,2},{4,5},{5,4},{6,7},{7,6},{8,9},{9,8},{10,11... | collective-permute-start | bytes 589832 | tf_op jit(solution)/shard_map/ppermute | solution.py:359
  23.8 5.3 %collective-permute-start.1 = (f32[4,3,4,8,128]{4,3,2,1,0:T(8,128)S(1)}, f32[4,3,4,8,128]{4,3,2,1,0:T(8,128)S(1)}, u32[]{:S(2)}, u32[]{:S(2)}) collective-permute-start(f32[4,3,4,8,128]{4,3,2,1,0:T(8,128)S(1)} %copy-done.2), channel_id=1, source_target_pairs={{0,7},{1,2},{2,1},{3,4},{4,3},{5,6},{6,5},{7,0},{8,15},{9,10},{10,... | collective-permute-start | bytes 589832 | tf_op jit(solution)/shard_map/ppermute | solution.py:360
  29.1 0.1 split.1.split_ref
  29.2 0.0 collective-permute-done.near_ref
  29.2 0.0 all-to-all-done.pencil_ref
  29.2 1.8 %radial.1 = f32[64,2,384]{2,1,0:T(2,128)} custom-call(f32[64,2,384]{2,1,0:T(2,128)S(1)} %all-to-all-done.pencil_ref, bf16[2,512,512]{2,1,0:T(8,128)(2,1)S(1)} %split.1.split_ref), custom_call_target="tpu_custom_call" | custom-call | flops 402653184 | bytes 1572864 | tf_op jit(solution)/shard_map/radial/pallas_call | solution.py:384
  31.0 0.0 copy-start
  31.0 15.1 %all-to-all-start.1 = ((f32[64,2,384]{2,1,0:T(2,128)}), f32[64,2,384]{2,1,0:T(2,128)S(1)}, u32[]{:S(2)}, u32[]{:S(2)}) async-start(f32[64,2,384]{2,1,0:T(2,128)} %radial.1), calls=%async_computation.1 | async-start | bytes 393216 | tf_op jit(solution)/shard_map/all_to_all | solution.py:397
  46.1 0.0 copy-done
  46.1 0.0 copy-start.3
  46.1 0.0 copy-start.1
  46.1 1.6 %theta.1 = (f32[3,4,8,512]{3,2,1,0:T(8,128)S(1)}, f32[3,4,8,512]{3,2,1,0:T(8,128)S(1)}) custom-call(f32[3,4,8,512]{3,2,1,0:T(8,128)S(1)} %copy-done, bf16[2,2,256,512]{3,2,1,0:T(8,128)(2,1)} %constant.5.clone.table_hbm), custom_call_target="tpu_custom_call" | custom-call | flops 50331648000 | bytes 1179648 | tf_op jit(solution)/shard_map/theta/pallas_call | solution.py:364
  47.8 0.0 collective-permute-done.1.far_ref
  47.8 0.0 copy-done.3
  47.8 0.1 broadcast_in_dim.2.ratio_ref
  47.9 0.0 copy-done.1
  47.9 0.2 local.1.local_ref
  48.1 4.4 %all-to-all-done.1.radial_ref = f32[64,2,384]{2,1,0:T(2,128)S(1)} async-done(((f32[64,2,384]{2,1,0:T(2,128)}), f32[64,2,384]{2,1,0:T(2,128)S(1)}, u32[]{:S(2)}, u32[]{:S(2)}) %all-to-all-start.1) | async-done | bytes 196640 | tf_op jit(solution)/shard_map/all_to_all | solution.py:397
  52.5 1.0 %final.1 = (f32[3,4,8,512]{3,2,1,0:T(8,128)}, f32[3,4,8,512]{3,2,1,0:T(8,128)}) custom-call(f32[64,2,384]{2,1,0:T(2,128)S(1)} %all-to-all-done.1.radial_ref, f32[3,4,8,512]{3,2,1,0:T(8,128)S(1)} %local.1.local_ref, f32[3,4,8,512]{3,2,1,0:T(8,128)S(1)} %copy-done), custom_call_target="tpu_custom_call" | custom-call | flops 491520 | bytes 983040 | tf_op jit(solution)/shard_map/final/pallas_call | solution.py:402
Async XLA Ops:
  3.1 18.7 %copy-start.2 = (f32[4,3,4,8,128]{4,3,2,1,0:T(8,128)S(1)}, f32[4,3,4,8,128]{4,3,2,1,0:T(8,128)}, u32[]{:S(2)}) copy-start(f32[4,3,4,8,128]{4,3,2,1,0:T(8,128)} %get-tuple-element.10.smooth_ref) | copy-start | bytes 589828
  3.2 26.1 %all-to-all-start = ((f32[64,2,384]{2,1,0:T(2,128)}), f32[64,2,384]{2,1,0:T(2,128)S(1)}, u32[]{:S(2)}, u32[]{:S(2)}) async-start(f32[64,2,384]{2,1,0:T(2,128)} %get-tuple-element.9), calls=%async_computation | async-start | bytes 393216 | tf_op jit(solution)/shard_map/all_to_all | solution.py:356
  21.8 7.4 %collective-permute-start = (f32[4,3,4,8,128]{4,3,2,1,0:T(8,128)S(1)}, f32[4,3,4,8,128]{4,3,2,1,0:T(8,128)S(1)}, u32[]{:S(2)}, u32[]{:S(2)}) collective-permute-start(f32[4,3,4,8,128]{4,3,2,1,0:T(8,128)S(1)} %copy-done.2), channel_id=1, source_target_pairs={{0,1},{1,0},{2,3},{3,2},{4,5},{5,4},{6,7},{7,6},{8,9},{9,8},{10,11... | collective-permute-start | bytes 589832 | tf_op jit(solution)/shard_map/ppermute | solution.py:359
  23.8 24.0 %collective-permute-start.1 = (f32[4,3,4,8,128]{4,3,2,1,0:T(8,128)S(1)}, f32[4,3,4,8,128]{4,3,2,1,0:T(8,128)S(1)}, u32[]{:S(2)}, u32[]{:S(2)}) collective-permute-start(f32[4,3,4,8,128]{4,3,2,1,0:T(8,128)S(1)} %copy-done.2), channel_id=1, source_target_pairs={{0,7},{1,2},{2,1},{3,4},{4,3},{5,6},{6,5},{7,0},{8,15},{9,10},{10,... | collective-permute-start | bytes 589832 | tf_op jit(solution)/shard_map/ppermute | solution.py:360
  31.0 15.1 %copy-start = (f32[3,4,8,512]{3,2,1,0:T(8,128)S(1)}, f32[3,4,8,512]{3,2,1,0:T(8,128)}, u32[]{:S(2)}) copy-start(f32[3,4,8,512]{3,2,1,0:T(8,128)} %velocity_ref.3) | copy-start | bytes 589828
  31.0 21.5 %all-to-all-start.1 = ((f32[64,2,384]{2,1,0:T(2,128)}), f32[64,2,384]{2,1,0:T(2,128)S(1)}, u32[]{:S(2)}, u32[]{:S(2)}) async-start(f32[64,2,384]{2,1,0:T(2,128)} %radial.1), calls=%async_computation.1 | async-start | bytes 393216 | tf_op jit(solution)/shard_map/all_to_all | solution.py:397
  46.1 1.7 %copy-start.3 = (f32[8]{0:T(128)S(1)}, f32[8]{0:T(128)}, u32[]{:S(2)}) copy-start(f32[8]{0:T(128)} %param.9) | copy-start | bytes 100
  46.1 1.7 %copy-start.1 = (f32[3,4,8,512]{3,2,1,0:T(8,128)S(1)}, f32[3,4,8,512]{3,2,1,0:T(8,128)}, u32[]{:S(2)}) copy-start(f32[3,4,8,512]{3,2,1,0:T(8,128)} %previous_ref.1) | copy-start | bytes 589828

commit v10 on v9

--- a/solution.py
+++ b/solution.py
@@ -16,7 +16,7 @@
 GROUPS = LANES // GROUP
 PAIR = 2
 FIRST = 52
-HEAVY = 2000
+HEAVY = 100
 
 first_coefs = (4.0 / 5.0, -1.0 / 5.0, 4.0 / 105.0, -1.0 / 280.0)
 second_coefs = (8.0 / 5.0, -1.0 / 5.0, 8.0 / 315.0, -1.0 / 560.0)
@@ -95,12 +95,11 @@
     velocity_hbm,
     table_hbm,
     matrix_hbm,
-    smooth_hbm,
+    smooth_ref,
     message_hbm,
     matrix_ref,
     velocity_ref,
     table_ref,
-    smooth_ref,
     message_ref,
     in_sems,
     out_sems,
@@ -111,7 +110,6 @@
         incoming.append(
             pltpu.make_async_copy(table_hbm.at[part], table_ref.at[part], in_sems.at[1 + part])
         )
-    incoming.append(pltpu.make_async_copy(matrix_hbm, matrix_ref, in_sems.at[3]))
     for copy in incoming:
         copy.start()
     incoming[0].wait()
@@ -119,6 +117,8 @@
     incoming[1].wait()
     even = product(total, (table_ref[0, 0], table_ref[0, 1]))
     incoming[2].wait()
+    matrix = pltpu.make_async_copy(matrix_hbm, matrix_ref, in_sems.at[3])
+    matrix.start()
     odd = product(gap, (table_ref[1, 0], table_ref[1, 1]))
     outgoing = []
     blocks = points // LANES
@@ -134,17 +134,16 @@
                     index = (block * GROUPS + part) * planes + plane
                     for c in range(components):
                         message_ref[index, :, lanes_of(c)] = tile[c * planes + plane, pair_of(part)]
-        count = message_ref.shape[0] // 2
-        here = pl.ds(section * count, count)
-        outgoing.append(
-            pltpu.make_async_copy(message_ref.at[here], message_hbm.at[here], out_sems.at[section])
-        )
-        outgoing[-1].start()
-    outgoing.append(pltpu.make_async_copy(smooth_ref, smooth_hbm, out_sems.at[2]))
-    outgoing[-1].start()
+            count = GROUPS * planes
+            here = pl.ds(block * count, count)
+            copy = pltpu.make_async_copy(
+                message_ref.at[here], message_hbm.at[here], out_sems.at[block]
+            )
+            copy.start()
+            outgoing.append(copy)
     for copy in outgoing:
         copy.wait()
-    incoming[3].wait()
+    matrix.wait()
 
 
 def theta_kernel(velocity_ref, table_hbm, slope_ref, curve_ref, table_ref, sem):
@@ -332,16 +331,19 @@
         filter_kernel,
         "filter",
         [HBM] * 3,
-        [(smooth_shape, f32, HBM), (message_shape, f32, HBM), (radial_deriv.shape, f32, PINNED)],
+        [
+            (smooth_shape, f32, PINNED),
+            (message_shape, f32, HBM),
+            (radial_deriv.shape, f32, PINNED),
+        ],
         6 * size * points,
         20 * size,
         [
             pltpu.VMEM(shape, f32),
             pltpu.VMEM(keep.shape, bf16),
-            pltpu.VMEM(smooth_shape, f32),
             pltpu.VMEM(message_shape, f32),
             dma((4,)),
-            dma((3,)),
+            dma((blocks,)),
         ],
     )(in_hbm(velocity), in_hbm(jnp.asarray(keep)), in_hbm(radial_deriv))
     first = FIRST % peers
@@ -356,11 +358,10 @@
     pencil = exchange(message)
 
     ring = lax.axis_size("axial")
-    near = lax.ppermute(smooth, "axial", [(i, i ^ 1) for i in range(ring)])
     far = lax.ppermute(
         smooth, "axial", [(i, (i + (1 if i % 2 else ring - 1)) % ring) for i in range(ring)]
     )
-    pencil, near = lax.optimization_barrier((pencil, near))
+    steady, far = lax.optimization_barrier((velocity, far))
     theta_slope, theta_curve = call(
         theta_kernel,
         "theta",
@@ -369,7 +370,7 @@
         HEAVY * size * points,
         24 * size,
         [pltpu.VMEM(theta.shape, bf16), dma(())],
-    )(velocity, in_hbm(jnp.asarray(theta)))
+    )(steady, in_hbm(jnp.asarray(theta)))
 
     full = peers * radial_rows
     pieces = 4
@@ -394,6 +395,8 @@
             dma((pieces + 1,)),
         ],
     )(in_vmem(pencil), in_vmem(split))
+    result, late = lax.optimization_barrier((result, smooth))
+    near = lax.ppermute(late, "axial", [(i, i ^ 1) for i in range(ring)])
     radial = exchange(result)
     ratio = jnp.broadcast_to(inv_radius[:, None], (radial_rows, LANES))
     (local,) = call(

time: 53.8 us -> 54.4 us (1.011)
  the two profiles are of different devices: /device:TPU:4 before, /device:TPU:1 now
where the time goes in v10:
time: 54.4 us; the launch traced here: 54 us
  starting transfers between devices  44.6 us (82%)
  Pallas kernels  7.26 us (13%)
  between operations  0.75 us (1%)
  local copies, waits for them, and re-layouts  0.73 us (1%)
  waiting for transfers between devices  0.71 us (1%)
    all_to_all x1, starting transfers between devices, shards(): pencil = exchange(message)  21.4 us
    all_to_all x1, starting transfers between devices, shards(): radial = exchange(result)  15.5 us
    ppermute x1, starting transfers between devices, shards(): lax.ppermute(smooth, 'axial', [(i, (i + (1 if i % 2 else ring - 1)) % rin...  3.94 us
    ppermute x1, starting transfers between devices, shards(): near = lax.ppermute(late, 'axial', [(i, i ^ 1) for i in range(ring)])  3.69 us
    pallas_call x1, Pallas kernels, shards(): call(filter_kernel, 'filter', [HBM] * 3, [(smooth_shape, f32, PINNED), (m...  2.58 us
    pallas_call x1, Pallas kernels, shards(): call(functools.partial(radial_kernel, first, pieces), 'radial', [VMEM] *...  1.76 us
    pallas_call x1, Pallas kernels, shards(): call(theta_kernel, 'theta', [VMEM, HBM], [(shape, f32, VMEM)] * 2, HEAVY...  1.58 us
  transfers between devices with their start and end apart: 4, of which 1 were waited for; matrix products, arithmetic and copies ran while one was open for 0% of the time, Pallas kernels for 7%

profile of v10, /device:TPU:1, one launch (start us, length us, event | category | flops | bytes accessed | tf_op | source)
XLA Modules:
  0.0 54.0 jit_solution(2736167599625547160)
XLA Ops:
  0.6 2.6 %filter.1 = (f32[4,3,4,8,128]{4,3,2,1,0:T(8,128)S(1)}, f32[64,2,384]{2,1,0:T(2,128)}, f32[512,512]{1,0:T(8,128)S(1)}) custom-call(f32[3,4,8,512]{3,2,1,0:T(8,128)} %velocity_ref.2, bf16[2,2,256,256]{3,2,1,0:T(8,128)(2,1)} %constant.4.clone.table_hbm, f32[512,512]{1,0:T(8,128)} %matrix_hbm.1), custom_call_target="tpu_custom_call" | custom-call | flops 150994944 | bytes 983040 | tf_op jit(solution)/shard_map/filter/pallas_call | solution.py:330
  3.2 21.4 %all-to-all-start = ((f32[64,2,384]{2,1,0:T(2,128)}), f32[64,2,384]{2,1,0:T(2,128)S(1)}, u32[]{:S(2)}, u32[]{:S(2)}) async-start(f32[64,2,384]{2,1,0:T(2,128)} %get-tuple-element.11), calls=%async_computation | async-start | bytes 393216 | tf_op jit(solution)/shard_map/all_to_all | solution.py:358
  24.6 3.9 %collective-permute-start.1 = (f32[4,3,4,8,128]{4,3,2,1,0:T(8,128)S(1)}, f32[4,3,4,8,128]{4,3,2,1,0:T(8,128)S(1)}, u32[]{:S(2)}, u32[]{:S(2)}) collective-permute-start(f32[4,3,4,8,128]{4,3,2,1,0:T(8,128)S(1)} %get-tuple-element.15.smooth_ref), channel_id=1, source_target_pairs={{0,7},{1,2},{2,1},{3,4},{4,3},{5,6},{6,5},{7,0},{8,15},{9,10},{10,... | collective-permute-start | bytes 589832 | tf_op jit(solution)/shard_map/ppermute | solution.py:361
  28.6 0.1 split.1.split_ref
  28.7 0.7 %all-to-all-done.pencil_ref = f32[64,2,384]{2,1,0:T(2,128)S(1)} async-done(((f32[64,2,384]{2,1,0:T(2,128)}), f32[64,2,384]{2,1,0:T(2,128)S(1)}, u32[]{:S(2)}, u32[]{:S(2)}) %all-to-all-start) | async-done | bytes 196640 | tf_op jit(solution)/shard_map/all_to_all | solution.py:358
  29.4 1.8 %radial.1 = f32[64,2,384]{2,1,0:T(2,128)} custom-call(f32[64,2,384]{2,1,0:T(2,128)S(1)} %all-to-all-done.pencil_ref, bf16[2,512,512]{2,1,0:T(8,128)(2,1)S(1)} %split.1.split_ref), custom_call_target="tpu_custom_call" | custom-call | flops 402653184 | bytes 1572864 | tf_op jit(solution)/shard_map/radial/pallas_call | solution.py:385
  31.2 0.0 copy-start
  31.2 15.5 %all-to-all-start.1 = ((f32[64,2,384]{2,1,0:T(2,128)}), f32[64,2,384]{2,1,0:T(2,128)S(1)}, u32[]{:S(2)}, u32[]{:S(2)}) async-start(f32[64,2,384]{2,1,0:T(2,128)} %radial.1), calls=%async_computation.1 | async-start | bytes 393216 | tf_op jit(solution)/shard_map/all_to_all | solution.py:400
  46.8 0.0 copy-start.1
  46.8 0.0 collective-permute-done.1.far_ref
  46.8 3.7 %collective-permute-start = (f32[4,3,4,8,128]{4,3,2,1,0:T(8,128)S(1)}, f32[4,3,4,8,128]{4,3,2,1,0:T(8,128)S(1)}, u32[]{:S(2)}, u32[]{:S(2)}) collective-permute-start(f32[4,3,4,8,128]{4,3,2,1,0:T(8,128)S(1)} %get-tuple-element.15.smooth_ref), channel_id=1, source_target_pairs={{0,1},{1,0},{2,3},{3,2},{4,5},{5,4},{6,7},{7,6},{8,9},{9,8},{10,11... | collective-permute-start | bytes 589832 | tf_op jit(solution)/shard_map/ppermute | solution.py:399
  50.5 0.0 copy-done
  50.5 1.6 %theta.1 = (f32[3,4,8,512]{3,2,1,0:T(8,128)S(1)}, f32[3,4,8,512]{3,2,1,0:T(8,128)S(1)}) custom-call(f32[3,4,8,512]{3,2,1,0:T(8,128)S(1)} %copy-done, bf16[2,2,256,512]{3,2,1,0:T(8,128)(2,1)} %constant.5.clone.table_hbm), custom_call_target="tpu_custom_call" | custom-call | flops 2516582400 | bytes 1179648 | tf_op jit(solution)/shard_map/theta/pallas_call | solution.py:365
  52.1 0.0 collective-permute-done.near_ref
  52.1 0.0 copy-start.2
  52.1 0.6 %copy-done.2 = f32[8]{0:T(128)S(1)} copy-done((f32[8]{0:T(128)S(1)}, f32[8]{0:T(128)}, u32[]{:S(2)}) %copy-start.2) | copy-done | bytes 56
  52.8 0.1 broadcast_in_dim.2.ratio_ref
  52.8 0.0 copy-done.1
  52.8 0.2 local.1.local_ref
  53.1 0.0 all-to-all-done.1.radial_ref
  53.1 1.0 %final.1 = (f32[3,4,8,512]{3,2,1,0:T(8,128)}, f32[3,4,8,512]{3,2,1,0:T(8,128)}) custom-call(f32[64,2,384]{2,1,0:T(2,128)S(1)} %all-to-all-done.1.radial_ref, f32[3,4,8,512]{3,2,1,0:T(8,128)S(1)} %local.1.local_ref, f32[3,4,8,512]{3,2,1,0:T(8,128)S(1)} %copy-done), custom_call_target="tpu_custom_call" | custom-call | flops 491520 | bytes 983040 | tf_op jit(solution)/shard_map/final/pallas_call | solution.py:405
Async XLA Ops:
  3.2 26.2 %all-to-all-start = ((f32[64,2,384]{2,1,0:T(2,128)}), f32[64,2,384]{2,1,0:T(2,128)S(1)}, u32[]{:S(2)}, u32[]{:S(2)}) async-start(f32[64,2,384]{2,1,0:T(2,128)} %get-tuple-element.11), calls=%async_computation | async-start | bytes 393216 | tf_op jit(solution)/shard_map/all_to_all | solution.py:358
  24.6 22.1 %collective-permute-start.1 = (f32[4,3,4,8,128]{4,3,2,1,0:T(8,128)S(1)}, f32[4,3,4,8,128]{4,3,2,1,0:T(8,128)S(1)}, u32[]{:S(2)}, u32[]{:S(2)}) collective-permute-start(f32[4,3,4,8,128]{4,3,2,1,0:T(8,128)S(1)} %get-tuple-element.15.smooth_ref), channel_id=1, source_target_pairs={{0,7},{1,2},{2,1},{3,4},{4,3},{5,6},{6,5},{7,0},{8,15},{9,10},{10,... | collective-permute-start | bytes 589832 | tf_op jit(solution)/shard_map/ppermute | solution.py:361
  31.2 19.3 %copy-start = (f32[3,4,8,512]{3,2,1,0:T(8,128)S(1)}, f32[3,4,8,512]{3,2,1,0:T(8,128)}, u32[]{:S(2)}) copy-start(f32[3,4,8,512]{3,2,1,0:T(8,128)} %velocity_ref.2) | copy-start | bytes 589828
  31.2 21.8 %all-to-all-start.1 = ((f32[64,2,384]{2,1,0:T(2,128)}), f32[64,2,384]{2,1,0:T(2,128)S(1)}, u32[]{:S(2)}, u32[]{:S(2)}) async-start(f32[64,2,384]{2,1,0:T(2,128)} %radial.1), calls=%async_computation.1 | async-start | bytes 393216 | tf_op jit(solution)/shard_map/all_to_all | solution.py:400
  46.8 6.1 %copy-start.1 = (f32[3,4,8,512]{3,2,1,0:T(8,128)S(1)}, f32[3,4,8,512]{3,2,1,0:T(8,128)}, u32[]{:S(2)}) copy-start(f32[3,4,8,512]{3,2,1,0:T(8,128)} %previous_ref.1) | copy-start | bytes 589828
  46.8 5.3 %collective-permute-start = (f32[4,3,4,8,128]{4,3,2,1,0:T(8,128)S(1)}, f32[4,3,4,8,128]{4,3,2,1,0:T(8,128)S(1)}, u32[]{:S(2)}, u32[]{:S(2)}) collective-permute-start(f32[4,3,4,8,128]{4,3,2,1,0:T(8,128)S(1)} %get-tuple-element.15.smooth_ref), channel_id=1, source_target_pairs={{0,1},{1,0},{2,3},{3,2},{4,5},{5,4},{6,7},{7,6},{8,9},{9,8},{10,11... | collective-permute-start | bytes 589832 | tf_op jit(solution)/shard_map/ppermute | solution.py:399
  52.1 0.7 %copy-start.2 = (f32[8]{0:T(128)S(1)}, f32[8]{0:T(128)}, u32[]{:S(2)}) copy-start(f32[8]{0:T(128)} %param.9) | copy-start | bytes 100

commit v11 on v10

--- a/solution.py
+++ b/solution.py
@@ -110,15 +110,14 @@
         incoming.append(
             pltpu.make_async_copy(table_hbm.at[part], table_ref.at[part], in_sems.at[1 + part])
         )
-    for copy in incoming:
+    matrix = pltpu.make_async_copy(matrix_hbm, matrix_ref, in_sems.at[3])
+    for copy in incoming + [matrix]:
         copy.start()
     incoming[0].wait()
     total, gap = sum_and_difference(velocity_ref[...])
     incoming[1].wait()
     even = product(total, (table_ref[0, 0], table_ref[0, 1]))
     incoming[2].wait()
-    matrix = pltpu.make_async_copy(matrix_hbm, matrix_ref, in_sems.at[3])
-    matrix.start()
     odd = product(gap, (table_ref[1, 0], table_ref[1, 1]))
     outgoing = []
     blocks = points // LANES
@@ -146,12 +145,17 @@
     matrix.wait()
 
 
-def theta_kernel(velocity_ref, table_hbm, slope_ref, curve_ref, table_ref, sem):
-    copy = pltpu.make_async_copy(table_hbm, table_ref, sem)
-    copy.start()
+def theta_kernel(velocity_ref, table_hbm, slope_ref, curve_ref, table_ref, sems):
+    copies = [
+        pltpu.make_async_copy(table_hbm.at[part], table_ref.at[part], sems.at[part])
+        for part in range(2)
+    ]
+    for copy in copies:
+        copy.start()
     total, gap = sum_and_difference(velocity_ref[...])
-    copy.wait()
+    copies[0].wait()
     even = product(total, (table_ref[0, 0], table_ref[0, 1]))
+    copies[1].wait()
     odd = product(gap, (table_ref[1, 0], table_ref[1, 1]))
     half = even.shape[1] // 2
     shape = velocity_ref.shape[:3] + (half,)
@@ -369,9 +373,11 @@
         [(shape, f32, VMEM)] * 2,
         HEAVY * size * points,
         24 * size,
-        [pltpu.VMEM(theta.shape, bf16), dma(())],
+        [pltpu.VMEM(theta.shape, bf16), dma((2,))],
     )(steady, in_hbm(jnp.asarray(theta)))
 
+    ratio = jnp.broadcast_to(inv_radius[:, None], (radial_rows, LANES))
+    pencil, ratio = lax.optimization_barrier((pencil, ratio))
     full = peers * radial_rows
     pieces = 4
     (split,) = call(
@@ -398,7 +404,6 @@
     result, late = lax.optimization_barrier((result, smooth))
     near = lax.ppermute(late, "axial", [(i, i ^ 1) for i in range(ring)])
     radial = exchange(result)
-    ratio = jnp.broadcast_to(inv_radius[:, None], (radial_rows, LANES))
     (local,) = call(
         local_kernel, "local", [VMEM] * 7, [(shape, f32, VMEM)], 40 * size, 32 * size
     )(smooth, near, far, theta_slope, theta_curve, previous_rhs, ratio)

time: 54.4 us -> 53.5 us (0.983)
  local copies, waits for them, and re-layouts: 0.73 us -> 0.09 us
    unnamed x6, local copies, waits for them, and re-layouts: 0.66 us -> 0.02 us
where the time goes in v11:
time: 53.5 us; the launch traced here: 53.2 us
  starting transfers between devices  44.6 us (83%)
  Pallas kernels  7.09 us (13%)
  between operations  0.76 us (1%)
  waiting for transfers between devices  0.7 us (1%)
    all_to_all x1, starting transfers between devices, shards(): pencil = exchange(message)  21.4 us
    all_to_all x1, starting transfers between devices, shards(): radial = exchange(result)  15.5 us
    ppermute x1, starting transfers between devices, shards(): lax.ppermute(smooth, 'axial', [(i, (i + (1 if i % 2 else ring - 1)) % rin...  3.94 us
    ppermute x1, starting transfers between devices, shards(): near = lax.ppermute(late, 'axial', [(i, i ^ 1) for i in range(ring)])  3.69 us
    pallas_call x1, Pallas kernels, shards(): call(filter_kernel, 'filter', [HBM] * 3, [(smooth_shape, f32, PINNED), (m...  2.43 us
    pallas_call x1, Pallas kernels, shards(): call(functools.partial(radial_kernel, first, pieces), 'radial', [VMEM] *...  1.76 us
    pallas_call x1, Pallas kernels, shards(): call(theta_kernel, 'theta', [VMEM, HBM], [(shape, f32, VMEM)] * 2, HEAVY...  1.55 us
  transfers between devices with their start and end apart: 4, of which 1 were waited for; matrix products, arithmetic and copies ran while one was open for 0% of the time, Pallas kernels for 7%

profile of v11, /device:TPU:1, one launch (start us, length us, event | category | flops | bytes accessed | tf_op | source)
XLA Modules:
  0.0 53.2 jit_solution(11443037062213471283)
XLA Ops:
  0.6 2.4 %filter.1 = (f32[4,3,4,8,128]{4,3,2,1,0:T(8,128)S(1)}, f32[64,2,384]{2,1,0:T(2,128)}, f32[512,512]{1,0:T(8,128)S(1)}) custom-call(f32[3,4,8,512]{3,2,1,0:T(8,128)} %velocity_ref.2, bf16[2,2,256,256]{3,2,1,0:T(8,128)(2,1)} %constant.4.clone.table_hbm, f32[512,512]{1,0:T(8,128)} %matrix_hbm.1), custom_call_target="tpu_custom_call" | custom-call | flops 150994944 | bytes 983040 | tf_op jit(solution)/shard_map/filter/pallas_call | solution.py:334
  3.1 21.4 %all-to-all-start = ((f32[64,2,384]{2,1,0:T(2,128)}), f32[64,2,384]{2,1,0:T(2,128)S(1)}, u32[]{:S(2)}, u32[]{:S(2)}) async-start(f32[64,2,384]{2,1,0:T(2,128)} %get-tuple-element.13), calls=%async_computation | async-start | bytes 393216 | tf_op jit(solution)/shard_map/all_to_all | solution.py:362
  24.5 3.9 %collective-permute-start.1 = (f32[4,3,4,8,128]{4,3,2,1,0:T(8,128)S(1)}, f32[4,3,4,8,128]{4,3,2,1,0:T(8,128)S(1)}, u32[]{:S(2)}, u32[]{:S(2)}) collective-permute-start(f32[4,3,4,8,128]{4,3,2,1,0:T(8,128)S(1)} %get-tuple-element.18.smooth_ref), channel_id=1, source_target_pairs={{0,7},{1,2},{2,1},{3,4},{4,3},{5,6},{6,5},{7,0},{8,15},{9,10},{10,... | collective-permute-start | bytes 589832 | tf_op jit(solution)/shard_map/ppermute | solution.py:365
  28.4 0.0 copy-start.2
  28.5 0.1 split.1.split_ref
  28.6 0.7 %all-to-all-done.pencil_ref = f32[64,2,384]{2,1,0:T(2,128)S(1)} async-done(((f32[64,2,384]{2,1,0:T(2,128)}), f32[64,2,384]{2,1,0:T(2,128)S(1)}, u32[]{:S(2)}, u32[]{:S(2)}) %all-to-all-start) | async-done | bytes 196640 | tf_op jit(solution)/shard_map/all_to_all | solution.py:362
  29.3 0.0 copy-done.2
  29.3 0.1 broadcast_in_dim.2.ratio_ref
  29.4 1.8 %radial.1 = f32[64,2,384]{2,1,0:T(2,128)} custom-call(f32[64,2,384]{2,1,0:T(2,128)S(1)} %all-to-all-done.pencil_ref, bf16[2,512,512]{2,1,0:T(8,128)(2,1)S(1)} %split.1.split_ref), custom_call_target="tpu_custom_call" | custom-call | flops 402653184 | bytes 1572864 | tf_op jit(solution)/shard_map/radial/pallas_call | solution.py:391
  31.1 0.0 copy-start
  31.2 15.5 %all-to-all-start.1 = ((f32[64,2,384]{2,1,0:T(2,128)}), f32[64,2,384]{2,1,0:T(2,128)S(1)}, u32[]{:S(2)}, u32[]{:S(2)}) async-start(f32[64,2,384]{2,1,0:T(2,128)} %radial.1), calls=%async_computation.1 | async-start | bytes 393216 | tf_op jit(solution)/shard_map/all_to_all | solution.py:406
  46.7 0.0 copy-start.1
  46.7 0.0 collective-permute-done.1.far_ref
  46.7 3.7 %collective-permute-start = (f32[4,3,4,8,128]{4,3,2,1,0:T(8,128)S(1)}, f32[4,3,4,8,128]{4,3,2,1,0:T(8,128)S(1)}, u32[]{:S(2)}, u32[]{:S(2)}) collective-permute-start(f32[4,3,4,8,128]{4,3,2,1,0:T(8,128)S(1)} %get-tuple-element.18.smooth_ref), channel_id=1, source_target_pairs={{0,1},{1,0},{2,3},{3,2},{4,5},{5,4},{6,7},{7,6},{8,9},{9,8},{10,11... | collective-permute-start | bytes 589832 | tf_op jit(solution)/shard_map/ppermute | solution.py:405
  50.4 0.0 copy-done
  50.4 1.6 %theta.1 = (f32[3,4,8,512]{3,2,1,0:T(8,128)S(1)}, f32[3,4,8,512]{3,2,1,0:T(8,128)S(1)}) custom-call(f32[3,4,8,512]{3,2,1,0:T(8,128)S(1)} %copy-done, bf16[2,2,256,512]{3,2,1,0:T(8,128)(2,1)} %constant.5.clone.table_hbm), custom_call_target="tpu_custom_call" | custom-call | flops 2516582400 | bytes 1179648 | tf_op jit(solution)/shard_map/theta/pallas_call | solution.py:369
  52.0 0.0 collective-permute-done.near_ref
  52.0 0.0 copy-done.1
  52.0 0.2 local.1.local_ref
  52.2 0.0 all-to-all-done.1.radial_ref
  52.3 1.0 %final.1 = (f32[3,4,8,512]{3,2,1,0:T(8,128)}, f32[3,4,8,512]{3,2,1,0:T(8,128)}) custom-call(f32[64,2,384]{2,1,0:T(2,128)S(1)} %all-to-all-done.1.radial_ref, f32[3,4,8,512]{3,2,1,0:T(8,128)S(1)} %local.1.local_ref, f32[3,4,8,512]{3,2,1,0:T(8,128)S(1)} %copy-done), custom_call_target="tpu_custom_call" | custom-call | flops 491520 | bytes 983040 | tf_op jit(solution)/shard_map/final/pallas_call | solution.py:410
Async XLA Ops:
  3.1 26.2 %all-to-all-start = ((f32[64,2,384]{2,1,0:T(2,128)}), f32[64,2,384]{2,1,0:T(2,128)S(1)}, u32[]{:S(2)}, u32[]{:S(2)}) async-start(f32[64,2,384]{2,1,0:T(2,128)} %get-tuple-element.13), calls=%async_computation | async-start | bytes 393216 | tf_op jit(solution)/shard_map/all_to_all | solution.py:362
  24.5 22.2 %collective-permute-start.1 = (f32[4,3,4,8,128]{4,3,2,1,0:T(8,128)S(1)}, f32[4,3,4,8,128]{4,3,2,1,0:T(8,128)S(1)}, u32[]{:S(2)}, u32[]{:S(2)}) collective-permute-start(f32[4,3,4,8,128]{4,3,2,1,0:T(8,128)S(1)} %get-tuple-element.18.smooth_ref), channel_id=1, source_target_pairs={{0,7},{1,2},{2,1},{3,4},{4,3},{5,6},{6,5},{7,0},{8,15},{9,10},{10,... | collective-permute-start | bytes 589832 | tf_op jit(solution)/shard_map/ppermute | solution.py:365
  28.4 0.9 %copy-start.2 = (f32[8]{0:T(128)S(1)}, f32[8]{0:T(128)}, u32[]{:S(2)}) copy-start(f32[8]{0:T(128)} %param.9) | copy-start | bytes 100
  31.1 19.3 %copy-start = (f32[3,4,8,512]{3,2,1,0:T(8,128)S(1)}, f32[3,4,8,512]{3,2,1,0:T(8,128)}, u32[]{:S(2)}) copy-start(f32[3,4,8,512]{3,2,1,0:T(8,128)} %velocity_ref.2) | copy-start | bytes 589828
  31.2 21.1 %all-to-all-start.1 = ((f32[64,2,384]{2,1,0:T(2,128)}), f32[64,2,384]{2,1,0:T(2,128)S(1)}, u32[]{:S(2)}, u32[]{:S(2)}) async-start(f32[64,2,384]{2,1,0:T(2,128)} %radial.1), calls=%async_computation.1 | async-start | bytes 393216 | tf_op jit(solution)/shard_map/all_to_all | solution.py:406
  46.7 5.3 %copy-start.1 = (f32[3,4,8,512]{3,2,1,0:T(8,128)S(1)}, f32[3,4,8,512]{3,2,1,0:T(8,128)}, u32[]{:S(2)}) copy-start(f32[3,4,8,512]{3,2,1,0:T(8,128)} %previous_ref.1) | copy-start | bytes 589828
  46.7 5.3 %collective-permute-start = (f32[4,3,4,8,128]{4,3,2,1,0:T(8,128)S(1)}, f32[4,3,4,8,128]{4,3,2,1,0:T(8,128)S(1)}, u32[]{:S(2)}, u32[]{:S(2)}) collective-permute-start(f32[4,3,4,8,128]{4,3,2,1,0:T(8,128)S(1)} %get-tuple-element.18.smooth_ref), channel_id=1, source_target_pairs={{0,1},{1,0},{2,3},{3,2},{4,5},{5,4},{6,7},{7,6},{8,9},{9,8},{10,11... | collective-permute-start | bytes 589832 | tf_op jit(solution)/shard_map/ppermute | solution.py:405

commit v12 on v11

--- a/solution.py
+++ b/solution.py
@@ -379,7 +379,7 @@
     ratio = jnp.broadcast_to(inv_radius[:, None], (radial_rows, LANES))
     pencil, ratio = lax.optimization_barrier((pencil, ratio))
     full = peers * radial_rows
-    pieces = 4
+    pieces = 2
     (split,) = call(
         split_kernel,
         "split",

time: 53.5 us -> 53.5 us (level)
  no operation moved by 1% of the time
where the time goes in v12:
time: 53.5 us; the launch traced here: 53.2 us
  starting transfers between devices  44.6 us (83%)
  Pallas kernels  7.04 us (13%)
  between operations  0.76 us (1%)
  waiting for transfers between devices  0.7 us (1%)
    all_to_all x1, starting transfers between devices, shards(): pencil = exchange(message)  21.4 us
    all_to_all x1, starting transfers between devices, shards(): radial = exchange(result)  15.5 us
    ppermute x1, starting transfers between devices, shards(): lax.ppermute(smooth, 'axial', [(i, (i + (1 if i % 2 else ring - 1)) % rin...  3.94 us
    ppermute x1, starting transfers between devices, shards(): near = lax.ppermute(late, 'axial', [(i, i ^ 1) for i in range(ring)])  3.69 us
    pallas_call x1, Pallas kernels, shards(): call(filter_kernel, 'filter', [HBM] * 3, [(smooth_shape, f32, PINNED), (m...  2.43 us
    pallas_call x1, Pallas kernels, shards(): call(functools.partial(radial_kernel, first, pieces), 'radial', [VMEM] *...  1.71 us
    pallas_call x1, Pallas kernels, shards(): call(theta_kernel, 'theta', [VMEM, HBM], [(shape, f32, VMEM)] * 2, HEAVY...  1.55 us
  transfers between devices with their start and end apart: 4, of which 1 were waited for; matrix products, arithmetic and copies ran while one was open for 0% of the time, Pallas kernels for 7%

profile of v12, /device:TPU:1, one launch (start us, length us, event | category | flops | bytes accessed | tf_op | source)
XLA Modules:
  0.0 53.2 jit_solution(17467948326991368312)
XLA Ops:
  0.6 2.4 %filter.1 = (f32[4,3,4,8,128]{4,3,2,1,0:T(8,128)S(1)}, f32[64,2,384]{2,1,0:T(2,128)}, f32[512,512]{1,0:T(8,128)S(1)}) custom-call(f32[3,4,8,512]{3,2,1,0:T(8,128)} %velocity_ref.2, bf16[2,2,256,256]{3,2,1,0:T(8,128)(2,1)} %constant.4.clone.table_hbm, f32[512,512]{1,0:T(8,128)} %matrix_hbm.1), custom_call_target="tpu_custom_call" | custom-call | flops 150994944 | bytes 983040 | tf_op jit(solution)/shard_map/filter/pallas_call | solution.py:334
  3.1 21.4 %all-to-all-start = ((f32[64,2,384]{2,1,0:T(2,128)}), f32[64,2,384]{2,1,0:T(2,128)S(1)}, u32[]{:S(2)}, u32[]{:S(2)}) async-start(f32[64,2,384]{2,1,0:T(2,128)} %get-tuple-element.13), calls=%async_computation | async-start | bytes 393216 | tf_op jit(solution)/shard_map/all_to_all | solution.py:362
  24.5 3.9 %collective-permute-start.1 = (f32[4,3,4,8,128]{4,3,2,1,0:T(8,128)S(1)}, f32[4,3,4,8,128]{4,3,2,1,0:T(8,128)S(1)}, u32[]{:S(2)}, u32[]{:S(2)}) collective-permute-start(f32[4,3,4,8,128]{4,3,2,1,0:T(8,128)S(1)} %get-tuple-element.18.smooth_ref), channel_id=1, source_target_pairs={{0,7},{1,2},{2,1},{3,4},{4,3},{5,6},{6,5},{7,0},{8,15},{9,10},{10,... | collective-permute-start | bytes 589832 | tf_op jit(solution)/shard_map/ppermute | solution.py:365
  28.4 0.0 copy-start.2
  28.5 0.1 split.1.split_ref
  28.6 0.7 %all-to-all-done.pencil_ref = f32[64,2,384]{2,1,0:T(2,128)S(1)} async-done(((f32[64,2,384]{2,1,0:T(2,128)}), f32[64,2,384]{2,1,0:T(2,128)S(1)}, u32[]{:S(2)}, u32[]{:S(2)}) %all-to-all-start) | async-done | bytes 196640 | tf_op jit(solution)/shard_map/all_to_all | solution.py:362
  29.3 0.0 copy-done.2
  29.3 0.1 broadcast_in_dim.2.ratio_ref
  29.4 1.7 %radial.1 = f32[64,2,384]{2,1,0:T(2,128)} custom-call(f32[64,2,384]{2,1,0:T(2,128)S(1)} %all-to-all-done.pencil_ref, bf16[2,512,512]{2,1,0:T(8,128)(2,1)S(1)} %split.1.split_ref), custom_call_target="tpu_custom_call" | custom-call | flops 402653184 | bytes 1572864 | tf_op jit(solution)/shard_map/radial/pallas_call | solution.py:391
  31.1 0.0 copy-start
  31.1 15.5 %all-to-all-start.1 = ((f32[64,2,384]{2,1,0:T(2,128)}), f32[64,2,384]{2,1,0:T(2,128)S(1)}, u32[]{:S(2)}, u32[]{:S(2)}) async-start(f32[64,2,384]{2,1,0:T(2,128)} %radial.1), calls=%async_computation.1 | async-start | bytes 393216 | tf_op jit(solution)/shard_map/all_to_all | solution.py:406
  46.6 0.0 copy-start.1
  46.6 0.0 collective-permute-done.1.far_ref
  46.7 3.7 %collective-permute-start = (f32[4,3,4,8,128]{4,3,2,1,0:T(8,128)S(1)}, f32[4,3,4,8,128]{4,3,2,1,0:T(8,128)S(1)}, u32[]{:S(2)}, u32[]{:S(2)}) collective-permute-start(f32[4,3,4,8,128]{4,3,2,1,0:T(8,128)S(1)} %get-tuple-element.18.smooth_ref), channel_id=1, source_target_pairs={{0,1},{1,0},{2,3},{3,2},{4,5},{5,4},{6,7},{7,6},{8,9},{9,8},{10,11... | collective-permute-start | bytes 589832 | tf_op jit(solution)/shard_map/ppermute | solution.py:405
  50.4 0.0 copy-done
  50.4 1.6 %theta.1 = (f32[3,4,8,512]{3,2,1,0:T(8,128)S(1)}, f32[3,4,8,512]{3,2,1,0:T(8,128)S(1)}) custom-call(f32[3,4,8,512]{3,2,1,0:T(8,128)S(1)} %copy-done, bf16[2,2,256,512]{3,2,1,0:T(8,128)(2,1)} %constant.5.clone.table_hbm), custom_call_target="tpu_custom_call" | custom-call | flops 2516582400 | bytes 1179648 | tf_op jit(solution)/shard_map/theta/pallas_call | solution.py:369
  51.9 0.0 collective-permute-done.near_ref
  51.9 0.0 copy-done.1
  51.9 0.2 local.1.local_ref
  52.2 0.0 all-to-all-done.1.radial_ref
  52.2 1.0 %final.1 = (f32[3,4,8,512]{3,2,1,0:T(8,128)}, f32[3,4,8,512]{3,2,1,0:T(8,128)}) custom-call(f32[64,2,384]{2,1,0:T(2,128)S(1)} %all-to-all-done.1.radial_ref, f32[3,4,8,512]{3,2,1,0:T(8,128)S(1)} %local.1.local_ref, f32[3,4,8,512]{3,2,1,0:T(8,128)S(1)} %copy-done), custom_call_target="tpu_custom_call" | custom-call | flops 491520 | bytes 983040 | tf_op jit(solution)/shard_map/final/pallas_call | solution.py:410
Async XLA Ops:
  3.1 26.2 %all-to-all-start = ((f32[64,2,384]{2,1,0:T(2,128)}), f32[64,2,384]{2,1,0:T(2,128)S(1)}, u32[]{:S(2)}, u32[]{:S(2)}) async-start(f32[64,2,384]{2,1,0:T(2,128)} %get-tuple-element.13), calls=%async_computation | async-start | bytes 393216 | tf_op jit(solution)/shard_map/all_to_all | solution.py:362
  24.5 22.1 %collective-permute-start.1 = (f32[4,3,4,8,128]{4,3,2,1,0:T(8,128)S(1)}, f32[4,3,4,8,128]{4,3,2,1,0:T(8,128)S(1)}, u32[]{:S(2)}, u32[]{:S(2)}) collective-permute-start(f32[4,3,4,8,128]{4,3,2,1,0:T(8,128)S(1)} %get-tuple-element.18.smooth_ref), channel_id=1, source_target_pairs={{0,7},{1,2},{2,1},{3,4},{4,3},{5,6},{6,5},{7,0},{8,15},{9,10},{10,... | collective-permute-start | bytes 589832 | tf_op jit(solution)/shard_map/ppermute | solution.py:365
  28.4 0.9 %copy-start.2 = (f32[8]{0:T(128)S(1)}, f32[8]{0:T(128)}, u32[]{:S(2)}) copy-start(f32[8]{0:T(128)} %param.9) | copy-start | bytes 100
  31.1 19.3 %copy-start = (f32[3,4,8,512]{3,2,1,0:T(8,128)S(1)}, f32[3,4,8,512]{3,2,1,0:T(8,128)}, u32[]{:S(2)}) copy-start(f32[3,4,8,512]{3,2,1,0:T(8,128)} %velocity_ref.2) | copy-start | bytes 589828
  31.1 21.1 %all-to-all-start.1 = ((f32[64,2,384]{2,1,0:T(2,128)}), f32[64,2,384]{2,1,0:T(2,128)S(1)}, u32[]{:S(2)}, u32[]{:S(2)}) async-start(f32[64,2,384]{2,1,0:T(2,128)} %radial.1), calls=%async_computation.1 | async-start | bytes 393216 | tf_op jit(solution)/shard_map/all_to_all | solution.py:406
  46.6 5.3 %copy-start.1 = (f32[3,4,8,512]{3,2,1,0:T(8,128)S(1)}, f32[3,4,8,512]{3,2,1,0:T(8,128)}, u32[]{:S(2)}) copy-start(f32[3,4,8,512]{3,2,1,0:T(8,128)} %previous_ref.1) | copy-start | bytes 589828
  46.7 5.3 %collective-permute-start = (f32[4,3,4,8,128]{4,3,2,1,0:T(8,128)S(1)}, f32[4,3,4,8,128]{4,3,2,1,0:T(8,128)S(1)}, u32[]{:S(2)}, u32[]{:S(2)}) collective-permute-start(f32[4,3,4,8,128]{4,3,2,1,0:T(8,128)S(1)} %get-tuple-element.18.smooth_ref), channel_id=1, source_target_pairs={{0,1},{1,0},{2,3},{3,2},{4,5},{5,4},{6,7},{7,6},{8,9},{9,8},{10,11... | collective-permute-start | bytes 589832 | tf_op jit(solution)/shard_map/ppermute | solution.py:405

commit v13 on v11

--- a/solution.py
+++ b/solution.py
@@ -15,7 +15,7 @@
 GROUP = 32
 GROUPS = LANES // GROUP
 PAIR = 2
-FIRST = 52
+FIRST = 44
 HEAVY = 100
 
 first_coefs = (4.0 / 5.0, -1.0 / 5.0, 4.0 / 105.0, -1.0 / 280.0)

time: 53.5 us -> 52.4 us (0.979)
  starting transfers between devices: 44.6 us -> 41.7 us
  waiting for transfers between devices: 0.7 us -> 2.03 us
    all_to_all x1, starting transfers between devices: 15.5 us -> 13.7 us  [shards(): radial = exchange(result)]
    all_to_all x1, starting transfers between devices: 21.4 us -> 19.9 us  [shards(): pencil = exchange(message)]
    all_to_all x1, waiting for transfers between devices: 0.69 us -> 2.03 us  [shards(): pencil = exchange(message)]
where the time goes in v13:
time: 52.4 us; the launch traced here: 51.7 us
  starting transfers between devices  41.7 us (80%)
  Pallas kernels  7.1 us (14%)
  waiting for transfers between devices  2.03 us (4%)
  between operations  0.76 us (1%)
    all_to_all x1, starting transfers between devices, shards(): pencil = exchange(message)  19.9 us
    all_to_all x1, starting transfers between devices, shards(): radial = exchange(result)  13.7 us
    ppermute x1, starting transfers between devices, shards(): lax.ppermute(smooth, 'axial', [(i, (i + (1 if i % 2 else ring - 1)) % rin...  4.07 us
    ppermute x1, starting transfers between devices, shards(): near = lax.ppermute(late, 'axial', [(i, i ^ 1) for i in range(ring)])  4.04 us
    pallas_call x1, Pallas kernels, shards(): call(filter_kernel, 'filter', [HBM] * 3, [(smooth_shape, f32, PINNED), (m...  2.43 us
    all_to_all x1, waiting for transfers between devices, shards(): pencil = exchange(message)  2.03 us
    pallas_call x1, Pallas kernels, shards(): call(functools.partial(radial_kernel, first, pieces), 'radial', [VMEM] *...  1.77 us
    pallas_call x1, Pallas kernels, shards(): call(theta_kernel, 'theta', [VMEM, HBM], [(shape, f32, VMEM)] * 2, HEAVY...  1.55 us
  transfers between devices with their start and end apart: 4, of which 1 were waited for; matrix products, arithmetic and copies ran while one was open for 0% of the time, Pallas kernels for 7%

profile of v13, /device:TPU:1, one launch (start us, length us, event | category | flops | bytes accessed | tf_op | source)
XLA Modules:
  0.0 51.7 jit_solution(1550282780268084417)
XLA Ops:
  0.6 2.4 %filter.1 = (f32[4,3,4,8,128]{4,3,2,1,0:T(8,128)S(1)}, f32[64,2,384]{2,1,0:T(2,128)}, f32[512,512]{1,0:T(8,128)S(1)}) custom-call(f32[3,4,8,512]{3,2,1,0:T(8,128)} %velocity_ref.2, bf16[2,2,256,256]{3,2,1,0:T(8,128)(2,1)} %constant.4.clone.table_hbm, f32[512,512]{1,0:T(8,128)} %matrix_hbm.1), custom_call_target="tpu_custom_call" | custom-call | flops 150994944 | bytes 983040 | tf_op jit(solution)/shard_map/filter/pallas_call | solution.py:334
  3.1 19.9 %all-to-all-start = ((f32[64,2,384]{2,1,0:T(2,128)}), f32[64,2,384]{2,1,0:T(2,128)S(1)}, u32[]{:S(2)}, u32[]{:S(2)}) async-start(f32[64,2,384]{2,1,0:T(2,128)} %get-tuple-element.13), calls=%async_computation | async-start | bytes 393216 | tf_op jit(solution)/shard_map/all_to_all | solution.py:362
  23.0 4.1 %collective-permute-start.1 = (f32[4,3,4,8,128]{4,3,2,1,0:T(8,128)S(1)}, f32[4,3,4,8,128]{4,3,2,1,0:T(8,128)S(1)}, u32[]{:S(2)}, u32[]{:S(2)}) collective-permute-start(f32[4,3,4,8,128]{4,3,2,1,0:T(8,128)S(1)} %get-tuple-element.18.smooth_ref), channel_id=1, source_target_pairs={{0,7},{1,2},{2,1},{3,4},{4,3},{5,6},{6,5},{7,0},{8,15},{9,10},{10,... | collective-permute-start | bytes 589832 | tf_op jit(solution)/shard_map/ppermute | solution.py:365
  27.1 0.0 copy-start.2
  27.1 0.1 split.1.split_ref
  27.3 2.0 %all-to-all-done.pencil_ref = f32[64,2,384]{2,1,0:T(2,128)S(1)} async-done(((f32[64,2,384]{2,1,0:T(2,128)}), f32[64,2,384]{2,1,0:T(2,128)S(1)}, u32[]{:S(2)}, u32[]{:S(2)}) %all-to-all-start) | async-done | bytes 196640 | tf_op jit(solution)/shard_map/all_to_all | solution.py:362
  29.3 0.0 copy-done.2
  29.3 0.1 broadcast_in_dim.2.ratio_ref
  29.4 1.8 %radial.1 = f32[64,2,384]{2,1,0:T(2,128)} custom-call(f32[64,2,384]{2,1,0:T(2,128)S(1)} %all-to-all-done.pencil_ref, bf16[2,512,512]{2,1,0:T(8,128)(2,1)S(1)} %split.1.split_ref), custom_call_target="tpu_custom_call" | custom-call | flops 402653184 | bytes 1572864 | tf_op jit(solution)/shard_map/radial/pallas_call | solution.py:391
  31.1 0.0 copy-start
  31.2 13.7 %all-to-all-start.1 = ((f32[64,2,384]{2,1,0:T(2,128)}), f32[64,2,384]{2,1,0:T(2,128)S(1)}, u32[]{:S(2)}, u32[]{:S(2)}) async-start(f32[64,2,384]{2,1,0:T(2,128)} %radial.1), calls=%async_computation.1 | async-start | bytes 393216 | tf_op jit(solution)/shard_map/all_to_all | solution.py:406
  44.8 0.0 copy-start.1
  44.9 0.0 collective-permute-done.1.far_ref
  44.9 4.0 %collective-permute-start = (f32[4,3,4,8,128]{4,3,2,1,0:T(8,128)S(1)}, f32[4,3,4,8,128]{4,3,2,1,0:T(8,128)S(1)}, u32[]{:S(2)}, u32[]{:S(2)}) collective-permute-start(f32[4,3,4,8,128]{4,3,2,1,0:T(8,128)S(1)} %get-tuple-element.18.smooth_ref), channel_id=1, source_target_pairs={{0,1},{1,0},{2,3},{3,2},{4,5},{5,4},{6,7},{7,6},{8,9},{9,8},{10,11... | collective-permute-start | bytes 589832 | tf_op jit(solution)/shard_map/ppermute | solution.py:405
  48.9 0.0 copy-done
  48.9 1.6 %theta.1 = (f32[3,4,8,512]{3,2,1,0:T(8,128)S(1)}, f32[3,4,8,512]{3,2,1,0:T(8,128)S(1)}) custom-call(f32[3,4,8,512]{3,2,1,0:T(8,128)S(1)} %copy-done, bf16[2,2,256,512]{3,2,1,0:T(8,128)(2,1)} %constant.5.clone.table_hbm), custom_call_target="tpu_custom_call" | custom-call | flops 2516582400 | bytes 1179648 | tf_op jit(solution)/shard_map/theta/pallas_call | solution.py:369
  50.5 0.0 collective-permute-done.near_ref
  50.5 0.0 copy-done.1
  50.5 0.2 local.1.local_ref
  50.8 0.0 all-to-all-done.1.radial_ref
  50.8 1.0 %final.1 = (f32[3,4,8,512]{3,2,1,0:T(8,128)}, f32[3,4,8,512]{3,2,1,0:T(8,128)}) custom-call(f32[64,2,384]{2,1,0:T(2,128)S(1)} %all-to-all-done.1.radial_ref, f32[3,4,8,512]{3,2,1,0:T(8,128)S(1)} %local.1.local_ref, f32[3,4,8,512]{3,2,1,0:T(8,128)S(1)} %copy-done), custom_call_target="tpu_custom_call" | custom-call | flops 491520 | bytes 983040 | tf_op jit(solution)/shard_map/final/pallas_call | solution.py:410
Async XLA Ops:
  3.1 26.2 %all-to-all-start = ((f32[64,2,384]{2,1,0:T(2,128)}), f32[64,2,384]{2,1,0:T(2,128)S(1)}, u32[]{:S(2)}, u32[]{:S(2)}) async-start(f32[64,2,384]{2,1,0:T(2,128)} %get-tuple-element.13), calls=%async_computation | async-start | bytes 393216 | tf_op jit(solution)/shard_map/all_to_all | solution.py:362
  23.0 21.8 %collective-permute-start.1 = (f32[4,3,4,8,128]{4,3,2,1,0:T(8,128)S(1)}, f32[4,3,4,8,128]{4,3,2,1,0:T(8,128)S(1)}, u32[]{:S(2)}, u32[]{:S(2)}) collective-permute-start(f32[4,3,4,8,128]{4,3,2,1,0:T(8,128)S(1)} %get-tuple-element.18.smooth_ref), channel_id=1, source_target_pairs={{0,7},{1,2},{2,1},{3,4},{4,3},{5,6},{6,5},{7,0},{8,15},{9,10},{10,... | collective-permute-start | bytes 589832 | tf_op jit(solution)/shard_map/ppermute | solution.py:365
  27.1 2.2 %copy-start.2 = (f32[8]{0:T(128)S(1)}, f32[8]{0:T(128)}, u32[]{:S(2)}) copy-start(f32[8]{0:T(128)} %param.9) | copy-start | bytes 100
  31.1 17.8 %copy-start = (f32[3,4,8,512]{3,2,1,0:T(8,128)S(1)}, f32[3,4,8,512]{3,2,1,0:T(8,128)}, u32[]{:S(2)}) copy-start(f32[3,4,8,512]{3,2,1,0:T(8,128)} %velocity_ref.2) | copy-start | bytes 589828
  31.2 19.6 %all-to-all-start.1 = ((f32[64,2,384]{2,1,0:T(2,128)}), f32[64,2,384]{2,1,0:T(2,128)S(1)}, u32[]{:S(2)}, u32[]{:S(2)}) async-start(f32[64,2,384]{2,1,0:T(2,128)} %radial.1), calls=%async_computation.1 | async-start | bytes 393216 | tf_op jit(solution)/shard_map/all_to_all | solution.py:406
  44.8 5.7 %copy-start.1 = (f32[3,4,8,512]{3,2,1,0:T(8,128)S(1)}, f32[3,4,8,512]{3,2,1,0:T(8,128)}, u32[]{:S(2)}) copy-start(f32[3,4,8,512]{3,2,1,0:T(8,128)} %previous_ref.1) | copy-start | bytes 589828
  44.9 5.6 %collective-permute-start = (f32[4,3,4,8,128]{4,3,2,1,0:T(8,128)S(1)}, f32[4,3,4,8,128]{4,3,2,1,0:T(8,128)S(1)}, u32[]{:S(2)}, u32[]{:S(2)}) collective-permute-start(f32[4,3,4,8,128]{4,3,2,1,0:T(8,128)S(1)} %get-tuple-element.18.smooth_ref), channel_id=1, source_target_pairs={{0,1},{1,0},{2,3},{3,2},{4,5},{5,4},{6,7},{7,6},{8,9},{9,8},{10,11... | collective-permute-start | bytes 589832 | tf_op jit(solution)/shard_map/ppermute | solution.py:405

commit v14 on v13

--- a/solution.py
+++ b/solution.py
@@ -15,7 +15,7 @@
 GROUP = 32
 GROUPS = LANES // GROUP
 PAIR = 2
-FIRST = 44
+FIRST = 43
 HEAVY = 100
 
 first_coefs = (4.0 / 5.0, -1.0 / 5.0, 4.0 / 105.0, -1.0 / 280.0)

time: 52.4 us -> 54.5 us (1.040)
  waiting for transfers between devices: 2.03 us -> 5.65 us
  starting transfers between devices: 41.7 us -> 40.1 us
    all_to_all x1, waiting for transfers between devices: 0.01 us -> 2.21 us  [shards(): radial = exchange(result)]
    all_to_all x1, waiting for transfers between devices: 2.03 us -> 3.44 us  [shards(): pencil = exchange(message)]
    all_to_all x1, starting transfers between devices: 13.7 us -> 12.6 us  [shards(): radial = exchange(result)]
  transfers between devices with their start and end apart: 4 -> 4, of which waited for: 1 -> 2; matrix products, arithmetic and copies ran while one was open for 0% -> 0% of each run, Pallas kernels for 7% -> 7%
where the time goes in v14:
time: 54.5 us; the launch traced here: 53.7 us
  starting transfers between devices  40.1 us (74%)
  Pallas kernels  7.09 us (13%)
  waiting for transfers between devices  5.65 us (10%)
  between operations  0.76 us (1%)
    all_to_all x1, starting transfers between devices, shards(): pencil = exchange(message)  19.8 us
    all_to_all x1, starting transfers between devices, shards(): radial = exchange(result)  12.6 us
    ppermute x1, starting transfers between devices, shards(): lax.ppermute(smooth, 'axial', [(i, (i + (1 if i % 2 else ring - 1)) % rin...  4.22 us
    ppermute x1, starting transfers between devices, shards(): near = lax.ppermute(late, 'axial', [(i, i ^ 1) for i in range(ring)])  3.52 us
    all_to_all x1, waiting for transfers between devices, shards(): pencil = exchange(message)  3.44 us
    pallas_call x1, Pallas kernels, shards(): call(filter_kernel, 'filter', [HBM] * 3, [(smooth_shape, f32, PINNED), (m...  2.43 us
    all_to_all x1, waiting for transfers between devices, shards(): radial = exchange(result)  2.21 us
    pallas_call x1, Pallas kernels, shards(): call(functools.partial(radial_kernel, first, pieces), 'radial', [VMEM] *...  1.77 us
  transfers between devices with their start and end apart: 4, of which 2 were waited for; matrix products, arithmetic and copies ran while one was open for 0% of the time, Pallas kernels for 7%

profile of v14, /device:TPU:1, one launch (start us, length us, event | category | flops | bytes accessed | tf_op | source)
XLA Modules:
  0.0 53.7 jit_solution(4264631907938634092)
XLA Ops:
  0.6 2.4 %filter.1 = (f32[4,3,4,8,128]{4,3,2,1,0:T(8,128)S(1)}, f32[64,2,384]{2,1,0:T(2,128)}, f32[512,512]{1,0:T(8,128)S(1)}) custom-call(f32[3,4,8,512]{3,2,1,0:T(8,128)} %velocity_ref.2, bf16[2,2,256,256]{3,2,1,0:T(8,128)(2,1)} %constant.4.clone.table_hbm, f32[512,512]{1,0:T(8,128)} %matrix_hbm.1), custom_call_target="tpu_custom_call" | custom-call | flops 150994944 | bytes 983040 | tf_op jit(solution)/shard_map/filter/pallas_call | solution.py:334
  3.1 19.8 %all-to-all-start = ((f32[64,2,384]{2,1,0:T(2,128)}), f32[64,2,384]{2,1,0:T(2,128)S(1)}, u32[]{:S(2)}, u32[]{:S(2)}) async-start(f32[64,2,384]{2,1,0:T(2,128)} %get-tuple-element.13), calls=%async_computation | async-start | bytes 393216 | tf_op jit(solution)/shard_map/all_to_all | solution.py:362
  22.9 4.2 %collective-permute-start.1 = (f32[4,3,4,8,128]{4,3,2,1,0:T(8,128)S(1)}, f32[4,3,4,8,128]{4,3,2,1,0:T(8,128)S(1)}, u32[]{:S(2)}, u32[]{:S(2)}) collective-permute-start(f32[4,3,4,8,128]{4,3,2,1,0:T(8,128)S(1)} %get-tuple-element.18.smooth_ref), channel_id=1, source_target_pairs={{0,7},{1,2},{2,1},{3,4},{4,3},{5,6},{6,5},{7,0},{8,15},{9,10},{10,... | collective-permute-start | bytes 589832 | tf_op jit(solution)/shard_map/ppermute | solution.py:365
  27.1 0.0 copy-start.2
  27.1 0.1 split.1.split_ref
  27.3 3.4 %all-to-all-done.pencil_ref = f32[64,2,384]{2,1,0:T(2,128)S(1)} async-done(((f32[64,2,384]{2,1,0:T(2,128)}), f32[64,2,384]{2,1,0:T(2,128)S(1)}, u32[]{:S(2)}, u32[]{:S(2)}) %all-to-all-start) | async-done | bytes 196640 | tf_op jit(solution)/shard_map/all_to_all | solution.py:362
  30.7 0.0 copy-done.2
  30.7 0.1 broadcast_in_dim.2.ratio_ref
  30.8 1.8 %radial.1 = f32[64,2,384]{2,1,0:T(2,128)} custom-call(f32[64,2,384]{2,1,0:T(2,128)S(1)} %all-to-all-done.pencil_ref, bf16[2,512,512]{2,1,0:T(8,128)(2,1)S(1)} %split.1.split_ref), custom_call_target="tpu_custom_call" | custom-call | flops 402653184 | bytes 1572864 | tf_op jit(solution)/shard_map/radial/pallas_call | solution.py:391
  32.6 0.0 copy-start
  32.6 12.6 %all-to-all-start.1 = ((f32[64,2,384]{2,1,0:T(2,128)}), f32[64,2,384]{2,1,0:T(2,128)S(1)}, u32[]{:S(2)}, u32[]{:S(2)}) async-start(f32[64,2,384]{2,1,0:T(2,128)} %radial.1), calls=%async_computation.1 | async-start | bytes 393216 | tf_op jit(solution)/shard_map/all_to_all | solution.py:406
  45.2 0.0 copy-start.1
  45.2 0.0 collective-permute-done.1.far_ref
  45.2 3.5 %collective-permute-start = (f32[4,3,4,8,128]{4,3,2,1,0:T(8,128)S(1)}, f32[4,3,4,8,128]{4,3,2,1,0:T(8,128)S(1)}, u32[]{:S(2)}, u32[]{:S(2)}) collective-permute-start(f32[4,3,4,8,128]{4,3,2,1,0:T(8,128)S(1)} %get-tuple-element.18.smooth_ref), channel_id=1, source_target_pairs={{0,1},{1,0},{2,3},{3,2},{4,5},{5,4},{6,7},{7,6},{8,9},{9,8},{10,11... | collective-permute-start | bytes 589832 | tf_op jit(solution)/shard_map/ppermute | solution.py:405
  48.7 0.0 copy-done
  48.7 1.6 %theta.1 = (f32[3,4,8,512]{3,2,1,0:T(8,128)S(1)}, f32[3,4,8,512]{3,2,1,0:T(8,128)S(1)}) custom-call(f32[3,4,8,512]{3,2,1,0:T(8,128)S(1)} %copy-done, bf16[2,2,256,512]{3,2,1,0:T(8,128)(2,1)} %constant.5.clone.table_hbm), custom_call_target="tpu_custom_call" | custom-call | flops 2516582400 | bytes 1179648 | tf_op jit(solution)/shard_map/theta/pallas_call | solution.py:369
  50.3 0.0 collective-permute-done.near_ref
  50.3 0.0 copy-done.1
  50.3 0.2 local.1.local_ref
  50.6 2.2 %all-to-all-done.1.radial_ref = f32[64,2,384]{2,1,0:T(2,128)S(1)} async-done(((f32[64,2,384]{2,1,0:T(2,128)}), f32[64,2,384]{2,1,0:T(2,128)S(1)}, u32[]{:S(2)}, u32[]{:S(2)}) %all-to-all-start.1) | async-done | bytes 196640 | tf_op jit(solution)/shard_map/all_to_all | solution.py:406
  52.8 1.0 %final.1 = (f32[3,4,8,512]{3,2,1,0:T(8,128)}, f32[3,4,8,512]{3,2,1,0:T(8,128)}) custom-call(f32[64,2,384]{2,1,0:T(2,128)S(1)} %all-to-all-done.1.radial_ref, f32[3,4,8,512]{3,2,1,0:T(8,128)S(1)} %local.1.local_ref, f32[3,4,8,512]{3,2,1,0:T(8,128)S(1)} %copy-done), custom_call_target="tpu_custom_call" | custom-call | flops 491520 | bytes 983040 | tf_op jit(solution)/shard_map/final/pallas_call | solution.py:410
Async XLA Ops:
  3.1 27.6 %all-to-all-start = ((f32[64,2,384]{2,1,0:T(2,128)}), f32[64,2,384]{2,1,0:T(2,128)S(1)}, u32[]{:S(2)}, u32[]{:S(2)}) async-start(f32[64,2,384]{2,1,0:T(2,128)} %get-tuple-element.13), calls=%async_computation | async-start | bytes 393216 | tf_op jit(solution)/shard_map/all_to_all | solution.py:362
  22.9 22.3 %collective-permute-start.1 = (f32[4,3,4,8,128]{4,3,2,1,0:T(8,128)S(1)}, f32[4,3,4,8,128]{4,3,2,1,0:T(8,128)S(1)}, u32[]{:S(2)}, u32[]{:S(2)}) collective-permute-start(f32[4,3,4,8,128]{4,3,2,1,0:T(8,128)S(1)} %get-tuple-element.18.smooth_ref), channel_id=1, source_target_pairs={{0,7},{1,2},{2,1},{3,4},{4,3},{5,6},{6,5},{7,0},{8,15},{9,10},{10,... | collective-permute-start | bytes 589832 | tf_op jit(solution)/shard_map/ppermute | solution.py:365
  27.1 3.6 %copy-start.2 = (f32[8]{0:T(128)S(1)}, f32[8]{0:T(128)}, u32[]{:S(2)}) copy-start(f32[8]{0:T(128)} %param.9) | copy-start | bytes 100
  32.6 16.2 %copy-start = (f32[3,4,8,512]{3,2,1,0:T(8,128)S(1)}, f32[3,4,8,512]{3,2,1,0:T(8,128)}, u32[]{:S(2)}) copy-start(f32[3,4,8,512]{3,2,1,0:T(8,128)} %velocity_ref.2) | copy-start | bytes 589828
  32.6 20.2 %all-to-all-start.1 = ((f32[64,2,384]{2,1,0:T(2,128)}), f32[64,2,384]{2,1,0:T(2,128)S(1)}, u32[]{:S(2)}, u32[]{:S(2)}) async-start(f32[64,2,384]{2,1,0:T(2,128)} %radial.1), calls=%async_computation.1 | async-start | bytes 393216 | tf_op jit(solution)/shard_map/all_to_all | solution.py:406
  45.2 5.1 %copy-start.1 = (f32[3,4,8,512]{3,2,1,0:T(8,128)S(1)}, f32[3,4,8,512]{3,2,1,0:T(8,128)}, u32[]{:S(2)}) copy-start(f32[3,4,8,512]{3,2,1,0:T(8,128)} %previous_ref.1) | copy-start | bytes 589828
  45.2 5.1 %collective-permute-start = (f32[4,3,4,8,128]{4,3,2,1,0:T(8,128)S(1)}, f32[4,3,4,8,128]{4,3,2,1,0:T(8,128)S(1)}, u32[]{:S(2)}, u32[]{:S(2)}) collective-permute-start(f32[4,3,4,8,128]{4,3,2,1,0:T(8,128)S(1)} %get-tuple-element.18.smooth_ref), channel_id=1, source_target_pairs={{0,1},{1,0},{2,3},{3,2},{4,5},{5,4},{6,7},{7,6},{8,9},{9,8},{10,11... | collective-permute-start | bytes 589832 | tf_op jit(solution)/shard_map/ppermute | solution.py:405
